TPU v7x, 32 devices: a whole 2x2x4 slice. The times are simulated.
32 devices in a mesh: dp: 8 (over y, x, core), mp: 4 (over z).
Axes of the slice: x: 2, y: 2, z: 4, core: 2. Of those that a mesh axis runs over, the one named last changes fastest.
Arguments:
- task_codes: bfloat16 [16, 128], replicated, may hold values from -6 to 6
- hyper_weight: bfloat16 [128, 196608], P(None, ('dp', 'mp')), may hold values from -0.5 to 0.5
- frozen_weight: bfloat16 [5120, 1024], P('mp'), may hold values from -0.125 to 0.125
- tokens: bfloat16 [8192, 5120], P(('dp', 'mp')), may hold values from -6 to 6
- teacher: bfloat16 [8192, 1024], P(('dp', 'mp')), may hold values from -6 to 6
- seq_slot: int32 [64], P(('dp', 'mp')), may hold values from 0 to 3, as said below
- task_share: int32 [8], replicated, may hold values from 1 to 4, as said below
- token_counts: int32 [16], replicated, may hold values from 1024 to 3071
Outputs:
- hyper_grad: float32 [128, 196608], P(None, ('dp', 'mp'))
Inputs may be any that keep to these rules, and one draw needn't show every extreme that they name: Group g owns task_share[g] tasks, numbered after those of groups 0 to g - 1; the entries sum to 16; in every draw some group owns exactly 4 tasks. For sequence s of group g = s // 8, seq_slot[s] < task_share[g]; in every group some sequence names the group's last task.
All inputs are finite; a program needn't handle non-finite values.
Results may differ from a plain program's by a relative error of at most 0.012.
Values may be sent and summed in bfloat16 or wider, within the bound.
No kernel may reach another device: no remote copies, remote signals or barrier semaphores. Data moves between devices by JAX's collectives and lax.ppermute only.
A program may use at most 64 MiB of HBM per device.

v0:
```python
import math

import jax
import jax.numpy as jnp
from jax import lax
from jax.sharding import PartitionSpec as P

D = 5120
KV = 1024
R = 32
TPG = 4
SEQ_LEN = 128


def swapped(array, axis, bit):
    return lax.ppermute(array, axis, [(i, i ^ 1 << bit) for i in range(lax.axis_size(axis))])


def shards(
    task_codes, hyper_weight, frozen_weight, tokens, teacher, seq_slot, task_share, token_counts
):
    groups = lax.axis_size("dp")
    members = lax.axis_size("mp")
    tok_dev = tokens.shape[0]
    shard_cols = hyper_weight.shape[1]
    shrink_factor = 1.0 / math.sqrt(D)
    rank_scale = 1.0 / math.sqrt(R)
    loss_scale = 1.0 / math.sqrt(tok_dev * members)
    slot_iota = jnp.arange(TPG, dtype=jnp.int32)
    offsets = jnp.cumsum(task_share) - task_share
    slot_live = slot_iota[:, None] < task_share[None, :]
    slot_task = jnp.where(slot_live, offsets[None, :] + slot_iota[:, None], 0).reshape(-1)
    live_rows = slot_live.reshape(-1, 1)
    adapters = jnp.dot(task_codes, hyper_weight, preferred_element_type=jnp.float32).astype(
        jnp.bfloat16
    )
    picked = jnp.where(
        live_rows, jnp.take(adapters, slot_task, axis=0), jnp.zeros((), jnp.bfloat16)
    )
    blocks = lax.all_to_all(
        picked.reshape(TPG, groups, 1, shard_cols), "dp", split_axis=1, concat_axis=1, tiled=True
    )
    own_adapters = lax.all_gather(blocks, "mp", axis=2, tiled=True).reshape(TPG, -1)
    adapter_input = own_adapters[:, : D * R].reshape(TPG, D, R)
    adapter_out = own_adapters[:, D * R :].reshape(TPG * R, KV)
    tok_slot = jnp.repeat(seq_slot, SEQ_LEN)
    onehot = (tok_slot[:, None] == slot_iota[None, :]).astype(jnp.float32)
    half_rows = frozen_weight.shape[0] // 2
    parity = lax.axis_index("dp") % 2
    own_half = lax.dynamic_slice_in_dim(frozen_weight, parity * half_rows, half_rows, 0)
    gathered = lax.all_gather(own_half, "mp", axis=0, tiled=True)
    other_half = swapped(gathered, "dp", 0)
    split_tokens = tokens.reshape(tok_dev, members, 2, half_rows)
    own_part = lax.dynamic_index_in_dim(split_tokens, parity, 2, keepdims=False).reshape(
        tok_dev, -1
    )
    other_part = lax.dynamic_index_in_dim(split_tokens, 1 - parity, 2, keepdims=False).reshape(
        tok_dev, -1
    )
    frozen_out = jnp.dot(own_part, gathered, preferred_element_type=jnp.float32) + jnp.dot(
        other_part, other_half, preferred_element_type=jnp.float32
    )
    low_all = jnp.einsum("td,sdr->tsr", tokens, adapter_input, preferred_element_type=jnp.float32)
    compact_factor_carry = (
        (low_all * (onehot[:, :, None] * shrink_factor))
        .astype(jnp.bfloat16)
        .reshape(tok_dev, TPG * R)
    )
    adapter_term = (
        jnp.dot(compact_factor_carry, adapter_out, preferred_element_type=jnp.float32) * rank_scale
    )
    counts = token_counts.astype(jnp.float32)
    task_weight = jnp.mean(counts) / counts
    own_offset = jnp.take(offsets, lax.axis_index("dp"))
    slot_weight = jnp.take(task_weight, jnp.minimum(own_offset + slot_iota, counts.shape[0] - 1))
    token_weight = jnp.sum(onehot * slot_weight[None, :], axis=1) * loss_scale
    value_grad = (
        (frozen_out + adapter_term - teacher.astype(jnp.float32)) * token_weight[:, None]
    ).astype(jnp.bfloat16)
    low_grad_all = (
        jnp.einsum("tk,ck->tc", value_grad, adapter_out, preferred_element_type=jnp.float32)
        * rank_scale
    )
    narrow_derivative = (low_grad_all.reshape(tok_dev, TPG, R) * onehot[:, :, None]).astype(
        jnp.bfloat16
    )
    primary_derivative = (
        jnp.einsum("td,tsr->sdr", tokens, narrow_derivative, preferred_element_type=jnp.float32)
        * shrink_factor
    )
    second_grad = (
        jnp.einsum(
            "tc,tk->ck", compact_factor_carry, value_grad, preferred_element_type=jnp.float32
        )
        * rank_scale
    )
    device_grad = jnp.concatenate(
        [primary_derivative.reshape(TPG, D * R), second_grad.reshape(TPG, R * KV)], axis=1
    )
    rounded = lax.optimization_barrier(device_grad.astype(jnp.bfloat16)).reshape(
        TPG, groups, members, shard_cols
    )
    routed = lax.all_to_all(rounded, "dp", split_axis=1, concat_axis=1, tiled=True)
    summed = lax.psum_scatter(
        routed.astype(jnp.float32).astype(jnp.bfloat16), "mp", scatter_dimension=2, tiled=True
    ).astype(jnp.float32)
    task_iota = jnp.arange(counts.shape[0], dtype=jnp.int32)
    select = ((slot_task[None, :] == task_iota[:, None]) & slot_live.reshape(1, -1)).astype(
        jnp.float32
    )
    adapter_grad = jnp.dot(select, summed.reshape(-1, shard_cols), precision=lax.Precision.HIGHEST)
    return jnp.dot(task_codes.astype(jnp.float32).T, adapter_grad, precision=lax.Precision.HIGHEST)


def solution(mesh):
    placed = (
        P(),
        P(None, ("dp", "mp")),
        P("mp", None),
        P(("dp", "mp"), None),
        P(("dp", "mp"), None),
        P(("dp", "mp")),
        P(),
        P(),
    )
    return jax.shard_map(
        shards, mesh=mesh, in_specs=placed, out_specs=P(None, ("dp", "mp")), check_vma=False
    )
```

profile of v0, /device:TPU:1, one launch (start us, length us, event | category | flops | bytes accessed | tf_op | source)
XLA Modules:
  0.0 291.3 jit_solution(15062447338065339702)
XLA Ops:
  6.6 1.7 copy-done
  9.8 1.7 convolution_convert_fusion
  11.5 98.4 %all-gather.3.cloned.1.call-done = bf16[2560,1024]{1,0:T(8,128)(2,1)} async-done(((bf16[640,1024]{1,0:T(8,128)(2,1)}), bf16[2560,1024]{1,0:T(8,128)(2,1)}) %all-gather.3.cloned.1.call-update) | async-done | bytes 5242896 | tf_op jit(solution)/shard_map/all_gather | solution.py:51
  112.0 11.0 %all_to_all.10 = bf16[4,8,1,6144]{3,0,2,1:T(4,128)(2,1)S(1)} all-to-all(bf16[4,8,1,6144]{3,0,2,1:T(4,128)(2,1)S(1)} %fusion.21), channel_id=1, replica_groups=mesh['dp'=8,'mp'=4] {'dp'}, dimensions={1} | all-to-all | bytes 786432 | tf_op jit(solution)/shard_map/all_to_all | solution.py:40
  124.8 4.4 %copy.21 = bf16[256,5120]{0,1:T(8,128)(2,1)} copy(bf16[256,5120]{1,0:T(8,128)(2,1)} %param.11) | data formatting | bytes 5242880 | tf_op args[3]
  131.8 3.4 %constant_dynamic-slice_fusion = (bf16[256,4,1,640]{0,3,2,1:T(8,128)(2,1)}, bf16[256,4,1,640]{0,3,2,1:T(8,128)(2,1)}) fusion(bf16[256,4,2,640]{0,3,2,1:T(8,128)(2,1)} %bitcast.58, s32[]{:T(128)S(6)} %select_n.120, s32[]{:T(128)S(6)} %select_n.118), kind=kLoop, calls=%fused_computation.48 | loop fusion | bytes 5242888 | tf_op jit(solution)/shard_map/jit(dynamic_index_in_dim)/dynamic_slice | solution.py:57
  135.4 21.8 %all-gather.5.cloned.1.call-done = bf16[4,8,4,6144]{3,1,0,2:T(8,128)(2,1)} async-done(((bf16[4,8,1,6144]{3,1,0,2:T(8,128)(2,1)}), bf16[4,8,4,6144]{3,1,0,2:T(8,128)(2,1)}) %all-gather.5.cloned.1.call-update) | async-done | bytes 1572880 | tf_op jit(solution)/shard_map/all_gather | solution.py:43
  157.2 3.8 %copy.26 = bf16[4,8,4,6144]{3,2,1,0:T(4,128)(2,1)} copy(bf16[4,8,4,6144]{3,1,0,2:T(8,128)(2,1)} %all-gather.5.cloned.1.call-done) | data formatting | bytes 3145728 | tf_op jit(solution)/shard_map/all_gather | solution.py:43
  161.0 3.7 %reshape.306 = bf16[4,196608]{1,0:T(4,128)(2,1)} reshape(bf16[4,8,4,6144]{3,2,1,0:T(4,128)(2,1)} %copy.26) | data formatting | bytes 3145728 | tf_op jit(solution)/shard_map/reshape | solution.py:43
  164.7 2.4 slice.17
  167.1 3.7 %reshape.361 = bf16[655360]{0:T(1024)(128)(2,1)} reshape(bf16[4,163840]{1,0:T(4,128)(2,1)} %slice.17) | data formatting | bytes 2621440
  170.8 6.6 %reshape.307 = bf16[4,5120,32]{2,1,0:T(8,128)(2,1)} reshape(bf16[655360]{0:T(1024)(128)(2,1)} %reshape.361) | data formatting | bytes 2621440 | tf_op jit(solution)/shard_map/reshape | solution.py:44
  177.6 5.0 %fusion.16 = bf16[256,4,32]{0,2,1:T(8,128)(2,1)S(1)} fusion(bf16[4,5120,32]{2,1,0:T(8,128)(2,1)} %reshape.307, bf16[256,5120]{1,0:T(8,128)(2,1)} %param.11, f32[256,4]{0,1:T(4,128)S(1)} %get-tuple-element.19), kind=kOutput, calls=%fused_computation.22 | convolution fusion | flops 335609856 | bytes 4001792 | tf_op jit(solution)/shard_map/td,sdr->tsr/dot_general | solution.py:63
  182.6 4.2 %fusion.31 = f32[256,1024]{1,0:T(8,128)S(1)} fusion(bf16[256,2560]{0,1:T(8,128)(2,1)S(1)} %bitcast.57, bf16[2560,1024]{1,0:T(8,128)(2,1)} %all-gather.3.cloned.1.call-done), kind=kOutput, calls=%fused_computation.59 | convolution fusion | flops 1342177280 | bytes 7602176 | tf_op jit(solution)/shard_map/dot_general | solution.py:60
  186.8 4.1 %convolution_add_fusion = f32[256,1024]{1,0:T(8,128)S(1)} fusion(f32[256,1024]{1,0:T(8,128)S(1)} %fusion.31, bf16[256,2560]{0,1:T(8,128)(2,1)S(1)} %bitcast.61, bf16[2560,1024]{1,0:T(8,128)(2,1)} %collective-permute-done), kind=kOutput, calls=%fused_computation.15 | convolution fusion | flops 1342439424 | bytes 8650752 | tf_op jit(solution)/shard_map/dot_general | solution.py:60
  194.3 5.2 %copy.28 = bf16[4,5120,32]{2,1,0:T(8,128)(2,1)} copy(bf16[4,5120,32]{1,2,0:T(8,128)(2,1)} %fusion.1) | data formatting | bytes 2621440 | tf_op jit(solution)/shard_map/mul | solution.py:88
  199.5 7.2 %reshape.363 = bf16[655360]{0:T(1024)(128)(2,1)} reshape(bf16[4,5120,32]{2,1,0:T(8,128)(2,1)} %copy.28) | data formatting | bytes 2621440
  206.7 2.9 reshape.311
  209.8 6.4 %pad_maximum_fusion = bf16[4,196608]{1,0:T(4,128)(2,1)S(1)} fusion(bf16[4,32768]{1,0:T(4,128)(2,1)S(1)} %reshape.312, bf16[4,163840]{1,0:T(4,128)(2,1)} %reshape.311), kind=kLoop, calls=%fused_computation.10 | loop fusion | flops 3145728 | bytes 3145728 | tf_op jit(solution)/shard_map/concatenate | solution.py:97
  216.1 24.6 %all_to_all.11 = bf16[4,8,4,6144]{3,0,2,1:T(4,128)(2,1)S(1)} all-to-all(bf16[4,8,4,6144]{3,0,2,1:T(4,128)(2,1)S(1)} %bitcast.59), channel_id=1, replica_groups=mesh['dp'=8,'mp'=4] {'dp'}, dimensions={1} | all-to-all | bytes 3145728 | tf_op jit(solution)/shard_map/all_to_all | solution.py:103
  240.8 2.0 copy.30
  243.0 32.8 %reduce-scatter.2.cloned.1.call-done = bf16[4,8,1,6144]{3,1,0,2:T(8,128)(2,1)} async-done(((bf16[4,8,4,6144]{3,1,0,2:T(8,128)(2,1)}), bf16[4,8,1,6144]{3,1,0,2:T(8,128)(2,1)}) %reduce-scatter.2.cloned.1.call-update) | async-done | bytes 393232 | tf_op jit(solution)/shard_map/reduce_scatter | solution.py:104
  277.0 4.3 %convolution_bitcast_fusion = f32[128,6144]{0,1:T(8,128)} fusion(f32[16,6144]{1,0:T(8,128)S(1)} %fusion.19, bf16[16,128]{1,0:T(8,128)(2,1)S(1)} %copy-done.5), kind=kOutput, calls=%fused_computation.2 | convolution fusion | flops 150994944 | bytes 3543040 | tf_op jit(solution)/shard_map/dot_general | solution.py:112
  281.2 3.5 %copy.31 = f32[128,6144]{1,0:T(8,128)} copy(f32[128,6144]{0,1:T(8,128)} %convolution_bitcast_fusion) | data formatting | bytes 6291456 | tf_op jit(solution)/shard_map/dot_general | solution.py:112
  (61 shorter events, 11.9 us)
Async XLA Ops:
  6.5 1.7 copy-start
  6.5 3.0 %copy-start.6 = (s32[8]{0:T(128)S(1)}, s32[8]{0:T(128)}, u32[]{:S(2)}) copy-start(s32[8]{0:T(128)} %param.14) | copy-start | bytes 100
  6.5 3.3 %copy-start.5 = (bf16[16,128]{1,0:T(8,128)(2,1)S(1)}, bf16[16,128]{1,0:T(8,128)(2,1)}, u32[]{:S(2)}) copy-start(bf16[16,128]{1,0:T(8,128)(2,1)} %param.8) | copy-start | bytes 12292
  6.5 103.4 %all-gather.3.cloned.1.call-start = ((), (), s32[]{:S(2)}) async-start(), calls=%async_computation.3 | async-start | bytes 6553600 | tf_op jit(solution)/shard_map/all_gather | solution.py:51
  9.4 147.8 %all-gather.5.cloned.1.call-start = ((), (), s32[]{:S(2)}) async-start(), calls=%async_computation.4 | async-start | bytes 1966080 | tf_op jit(solution)/shard_map/all_gather | solution.py:43
  109.9 76.9 %collective-permute-start = (bf16[2560,1024]{1,0:T(8,128)(2,1)}, bf16[2560,1024]{1,0:T(8,128)(2,1)}, u32[]{:S(2)}, u32[]{:S(2)}) collective-permute-start(bf16[2560,1024]{1,0:T(8,128)(2,1)} %all-gather.3.cloned.1.call-done), channel_id=1, source_target_pairs={{0,4},{4,0},{8,12},{12,8},{16,20},{20,16},{24,28},{28,24},{1,5},{5... | collective-permute-start | bytes 15728648 | tf_op jit(solution)/shard_map/ppermute | solution.py:16
  124.0 151.7 %reduce-scatter.2.cloned.1.call-start = ((), (), s32[]{:S(2)}) async-start(), calls=%async_computation.5 | async-start | bytes 1966080 | tf_op jit(solution)/shard_map/reduce_scatter | solution.py:104
  124.8 4.4 %copy-start.7 = (s32[16]{0:T(128)S(1)}, s32[16]{0:T(128)}, u32[]{:S(2)}) copy-start(s32[16]{0:T(128)} %param.15) | copy-start | bytes 196
  131.8 3.4 %copy-start.8 = (s32[2]{0:T(128)S(1)}, s32[2]{0:T(128)}, u32[]{:S(2)}) copy-start(s32[2]{0:T(128)} %param.13) | copy-start | bytes 28
  170.8 6.6 %slice-start = ((bf16[4,196608]{1,0:T(4,128)(2,1)}), bf16[4,32768]{1,0:T(4,128)(2,1)S(1)}, s32[]{:S(2)}) async-start(bf16[4,196608]{1,0:T(4,128)(2,1)} %reshape.306), calls=%async_computation.6 | async-start | bytes 524288 | tf_op jit(solution)/shard_map/slice | solution.py:45
  177.6 5.0 %copy-start.2 = (bf16[256,4,1,640]{0,3,2,1:T(8,128)(2,1)S(1)}, bf16[256,4,1,640]{0,3,2,1:T(8,128)(2,1)}, u32[]{:S(2)}) copy-start(bf16[256,4,1,640]{0,3,2,1:T(8,128)(2,1)} %get-tuple-element.17) | copy-start | bytes 3932164
  182.6 4.2 %copy-start.3 = (bf16[256,4,1,640]{0,3,2,1:T(8,128)(2,1)S(1)}, bf16[256,4,1,640]{0,3,2,1:T(8,128)(2,1)}, u32[]{:S(2)}) copy-start(bf16[256,4,1,640]{0,3,2,1:T(8,128)(2,1)} %get-tuple-element.16) | copy-start | bytes 3932164
  186.8 4.1 %copy-start.4 = (bf16[256,1024]{1,0:T(8,128)(2,1)S(1)}, bf16[256,1024]{1,0:T(8,128)(2,1)}, u32[]{:S(2)}) copy-start(bf16[256,1024]{1,0:T(8,128)(2,1)} %param.12) | copy-start | bytes 1572868
  190.9 1.7 copy-start.1
Sparse Core Ops, SparseCore 0:
  9.6 100.2 all-gather.2
  124.2 33.0 all-gather.4
  242.9 32.8 reduce-scatter.1
where the time goes:
time: 293 us; the launch traced here: 291 us
  waiting for transfers between devices  153 us (52%)
  local copies, waits for them, and re-layouts  56.5 us (19%)
  blocking collectives  35.7 us (12%)
  matrix products  22.9 us (8%)
  between operations  14.7 us (5%)
  other arithmetic  7.91 us (3%)
    all_gather x1, waiting for transfers between devices, shards(): gathered = lax.all_gather(own_half, 'mp', axis=0, tiled=True)  98.4 us
    reduce_scatter x1, waiting for transfers between devices, shards(): lax.psum_scatter(routed.astype(jnp.float32).astype(jnp.bfloat16), 'mp', s...  32.8 us
    all_to_all x1, blocking collectives, shards(): lax.all_to_all(rounded, 'dp', split_axis=1, concat_axis=1, tiled=True)  24.6 us
    all_gather x1, waiting for transfers between devices, shards(): lax.all_gather(blocks, 'mp', axis=2, tiled=True).reshape(TPG, -1)  21.8 us
    unnamed x21, local copies, waits for them, and re-layouts  17.8 us
    all_to_all x1, blocking collectives, shards(): lax.all_to_all(picked.reshape(TPG, groups, 1, shard_cols), 'dp', split_ax...  11 us
    reshape x1, local copies, waits for them, and re-layouts, shards(): adapter_input = own_adapters[:, :D * R].reshape(TPG, D, R)  6.64 us
    concatenate x1, other arithmetic, shards(): jnp.concatenate([primary_derivative.reshape(TPG, D * R), second_grad.resh...  6.36 us
  transfers between devices with their start and end apart: 4, of which 3 were waited for; matrix products, arithmetic and copies ran while one was open for 15% of the time, Pallas kernels for 0%

commit v1 on v0

v1 whole, which is shorter than its diff:
```python
import functools
import math

import jax
import jax.numpy as jnp
from jax import lax
from jax.experimental import pallas as pl
from jax.experimental.pallas import tpu as pltpu
from jax.sharding import PartitionSpec as P

D = 5120
KV = 1024
R = 32
SEQ_LEN = 128
LANES = 128
PACK = LANES // R
A_ROWS = D * R // LANES
B_ROWS = R * KV // LANES
COL_TILES = KV // LANES
BLOCK_D = 512
BLOCK_Q = BLOCK_D // PACK
SHRINK = 1.0 / math.sqrt(D)
RANK_SCALE = 1.0 / math.sqrt(R)
F32 = jnp.float32
BF16 = jnp.bfloat16
VMEM_LIMIT = 48 * 1024 * 1024


def dot(a, b):
    return jnp.dot(a, b, preferred_element_type=F32)


def dot_nt(a, b):
    return lax.dot_general(a, b, (((1,), (1,)), ((), ())), preferred_element_type=F32)


def call(body, outs, scratch=(), n_smem=0, n_in=0, flops=0, nbytes=0, **kw):
    specs = [pl.BlockSpec(memory_space=pltpu.SMEM)] * n_smem
    specs += [pl.BlockSpec(memory_space=pltpu.VMEM)] * n_in
    out_specs = [pl.BlockSpec(memory_space=pltpu.VMEM)] * len(outs)
    return pl.pallas_call(
        body,
        out_shape=list(outs),
        in_specs=specs,
        out_specs=out_specs,
        scratch_shapes=list(scratch),
        compiler_params=pltpu.CompilerParams(vmem_limit_bytes=VMEM_LIMIT),
        cost_estimate=pl.CostEstimate(flops=flops, bytes_accessed=nbytes, transcendentals=0),
        **kw,
    )


def sds(shape, dtype):
    return jax.ShapeDtypeStruct(shape, dtype)


def xor_permute(array, axis, mask):
    return lax.ppermute(array, axis, [(i, i ^ mask) for i in range(lax.axis_size(axis))])


def adapters_kernel(tiles, task_ref, codes_ref, weight_ref, out_ref, scr):
    rows = task_ref.shape[0]
    tasks = codes_ref.shape[0]
    pick = (task_ref[...] == lax.broadcasted_iota(jnp.int32, (rows, tasks), 1)).astype(BF16)
    chosen = dot(pick, codes_ref[...]).astype(BF16)
    for k in range(tiles):
        part = dot(chosen, weight_ref[:, k * LANES : (k + 1) * LANES])
        scr[pl.ds(k, rows, stride=tiles), :] = part
    for i in range(rows):
        out_ref[i] = scr[i * tiles : (i + 1) * tiles, :].astype(BF16)


def low_rank_kernel(adapt_ref, tokens_ref, low_ref, b4_ref, tok_t_ref, scr, held):
    seqs = b4_ref.shape[0]
    if len(adapt_ref.shape) == 4:
        tiles = adapt_ref.shape[2]
        for i in range(adapt_ref.shape[0]):
            for s in range(seqs):
                held[s, i * tiles : (i + 1) * tiles, :] = adapt_ref[i, s]
        adapt_ref = held
    lane = lax.broadcasted_iota(jnp.int32, (BLOCK_D, LANES * seqs), 1)
    row = lax.broadcasted_iota(jnp.int32, (BLOCK_D, LANES * seqs), 0)
    keep = (lane % LANES) // R == row % PACK
    spread = (
        lax.broadcasted_iota(jnp.int32, (BLOCK_D, BLOCK_Q), 0) // PACK
        == lax.broadcasted_iota(jnp.int32, (BLOCK_D, BLOCK_Q), 1)
    ).astype(BF16)
    acc = jnp.zeros((tokens_ref.shape[0], LANES * seqs), F32)
    for b in range(D // BLOCK_D):
        cols = slice(b * BLOCK_D, (b + 1) * BLOCK_D)
        part = jnp.concatenate(
            [adapt_ref[s, b * BLOCK_Q : (b + 1) * BLOCK_Q, :] for s in range(seqs)], axis=1
        )
        wide = jnp.where(keep, dot(spread, part), 0.0).astype(BF16)
        block = tokens_ref[:, cols]
        acc = acc + dot(block, wide)
        tok_t_ref[cols, :] = block.T
    first = lax.broadcasted_iota(jnp.int32, (SEQ_LEN, LANES), 1) < R
    for s in range(seqs):
        z = acc[s * SEQ_LEN : (s + 1) * SEQ_LEN, s * LANES : (s + 1) * LANES]
        total = z
        for j in range(1, PACK):
            total = total + pltpu.roll(z, j * R, 1)
        low_ref[s * SEQ_LEN : (s + 1) * SEQ_LEN, :] = jnp.where(first, total * SHRINK, 0.0).astype(
            BF16
        )
        scr[...] = adapt_ref[s, A_ROWS:, :].astype(F32)
        for c in range(COL_TILES):
            piece = scr[pl.ds(c, R, stride=COL_TILES), :].astype(BF16)
            for j in range(PACK):
                b4_ref[s, j * R : (j + 1) * R, c * LANES : (c + 1) * LANES] = piece


def frozen_kernel(members, place_ref, weight_ref, own_ref, other_ref, *refs):
    pieces, (out_own, out_other) = refs[:-2], refs[-2:]
    half = out_own.shape[1]
    depth = weight_ref.shape[0]
    width = pieces[0].shape[1]
    me, core, chip = place_ref[0], place_ref[1], place_ref[2]
    rows = own_ref.shape[0]

    def both(block):
        cols = pl.ds(pl.multiple_of(block * depth, LANES), depth)
        return jnp.concatenate([own_ref[:, cols], other_ref[:, cols]], axis=0)

    first = dot(both(me), weight_ref[:, pl.ds(pl.multiple_of(core * half, LANES), half)])
    out_own[...] = first[:rows]
    out_other[...] = first[rows:]
    for k in range(1, members):
        left = both(me ^ k)
        span = slice((k - 1) * depth, k * depth)
        for m in range(0, len(pieces), 2):
            pair = range(m, min(m + 2, len(pieces)))
            right = jnp.concatenate([pieces[i][span, :] for i in pair], axis=1)
            part = dot(left, right)
            for at, i in enumerate(pair):
                cols = pl.ds(pl.multiple_of((chip ^ i) * width, LANES), width)
                out_own[:, cols] += part[:rows, at * width : (at + 1) * width]
                out_other[:, cols] += part[rows:, at * width : (at + 1) * width]


def backward_kernel(
    place_ref, scale_ref, mine_ref, theirs_ref, teacher_ref, low_ref, b4_ref, tok_t_ref, out_ref,
    values, spaced, grads,
):
    seqs = b4_ref.shape[0]
    half = mine_ref.shape[1]
    core = place_ref[1]
    values[:, pl.ds(pl.multiple_of(core * half, LANES), half)] = mine_ref[...]
    values[:, pl.ds(pl.multiple_of((1 - core) * half, LANES), half)] = theirs_ref[...]
    blocks = []
    for s in range(seqs):
        rows = slice(s * SEQ_LEN, (s + 1) * SEQ_LEN)
        low = low_ref[rows, :]
        b4 = b4_ref[s]
        error = values[rows, :] + dot(low, b4) * RANK_SCALE - teacher_ref[rows, :].astype(F32)
        value_grad = (error * scale_ref[s]).astype(BF16)
        blocks.append((dot_nt(value_grad, b4) * RANK_SCALE).astype(BF16))
        second = dot(low.T, value_grad)[:R] * RANK_SCALE
        for c in range(COL_TILES):
            spaced[pl.ds(c, R, stride=COL_TILES), :] = second[:, c * LANES : (c + 1) * LANES]
        grads[s, A_ROWS:, :] = spaced[...].astype(BF16)
    zero = jnp.zeros_like(blocks[0])
    low_grad = jnp.concatenate(
        [
            jnp.concatenate([blocks[s] if s == i else zero for i in range(seqs)], axis=1)
            for s in range(seqs)
        ],
        axis=0,
    )
    lane = lax.broadcasted_iota(jnp.int32, (BLOCK_D, LANES * seqs), 1)
    row = lax.broadcasted_iota(jnp.int32, (BLOCK_D, LANES * seqs), 0)
    keep = (lane % LANES) // R == row % PACK
    merge = (
        lax.broadcasted_iota(jnp.int32, (BLOCK_Q, BLOCK_D), 1) // PACK
        == lax.broadcasted_iota(jnp.int32, (BLOCK_Q, BLOCK_D), 0)
    ).astype(BF16)
    for b in range(D // BLOCK_D):
        full = dot(tok_t_ref[b * BLOCK_D : (b + 1) * BLOCK_D, :], low_grad)
        kept = jnp.where(keep, full * SHRINK, 0.0).astype(BF16)
        merged = dot(merge, kept).astype(BF16)
        for s in range(seqs):
            grads[s, b * BLOCK_Q : (b + 1) * BLOCK_Q, :] = merged[:, s * LANES : (s + 1) * LANES]
    store_grads(grads, out_ref)


def store_grads(grads, out_ref):
    if len(out_ref.shape) == 3:
        out_ref[...] = grads[...]
        return
    tiles = out_ref.shape[2]
    for i in range(out_ref.shape[0]):
        for s in range(out_ref.shape[1]):
            out_ref[i, s] = grads[s, i * tiles : (i + 1) * tiles, :]


def hyper_kernel(codes_t_ref, grads_ref, out_ref, scr):
    devices, seqs, tiles, _ = grads_ref.shape
    rows = devices * seqs
    for i in range(devices):
        for s in range(seqs):
            at = (i * seqs + s) * tiles
            scr[at : at + tiles, :] = grads_ref[i, s].astype(F32)
    codes_t = codes_t_ref[...]
    for k in range(tiles):
        part = scr[pl.ds(k, rows, stride=tiles), :].astype(BF16)
        out_ref[:, k * LANES : (k + 1) * LANES] = dot(codes_t, part)


def shards(
    task_codes, hyper_weight, frozen_weight, tokens, teacher, seq_slot, task_share, token_counts
):
    groups = lax.axis_size("dp")
    members = lax.axis_size("mp")
    devices = groups * members
    chips = groups // 2
    tok_dev = tokens.shape[0]
    seqs = seq_slot.shape[0]
    depth = frozen_weight.shape[0]
    tiles = hyper_weight.shape[1] // LANES
    rows = A_ROWS + B_ROWS
    n_tasks, width_h = task_codes.shape
    loss_scale = 1.0 / math.sqrt(tok_dev * members)
    me_dp, me_mp = lax.axis_index("dp"), lax.axis_index("mp")
    core, chip = me_dp % 2, me_dp // 2
    place = jnp.stack([me_mp, core, chip]).astype(jnp.int32)
    half = KV // 2
    width = half // chips
    whole_tiles = tiles % 16 == 0

    chunk = lax.dynamic_slice_in_dim(frozen_weight, core * half + chip * width, width, 1)
    arrived = jnp.concatenate(
        [xor_permute(chunk, "mp", k) for k in range(1, members)], axis=0
    )
    other_tokens = xor_permute(tokens, "dp", 1)

    slots = lax.all_to_all(
        jnp.broadcast_to(seq_slot[None], (devices, seqs)), ("dp", "mp"), 0, 0, tiled=True
    ).reshape(-1)
    offsets = jnp.cumsum(task_share) - task_share
    task_of = jnp.repeat(offsets, members * seqs) + slots
    codes_t = jnp.dot(
        task_codes.T, (jnp.arange(n_tasks)[:, None] == task_of[None, :]).astype(BF16),
        preferred_element_type=F32,
    ).astype(BF16)
    counts = token_counts.astype(F32)
    task_weight = jnp.mean(counts) / counts
    own_task = jnp.take(offsets, me_dp) + seq_slot
    scale = jnp.take(task_weight, own_task) * loss_scale

    held = {0: arrived}
    middle = arrived.shape[0] // 2
    for m in range(1, chips):
        low_bit, high_bit = m & -m, 1 << (m.bit_length() - 1)
        if low_bit == high_bit:
            held[m] = xor_permute(arrived, "dp", m << 1)
        else:
            held[m] = jnp.concatenate(
                [
                    xor_permute(held[m ^ high_bit][:middle], "dp", high_bit << 1),
                    xor_permute(held[m ^ low_bit][middle:], "dp", low_bit << 1),
                ],
                axis=0,
            )

    sent = call(
        functools.partial(adapters_kernel, tiles),
        [sds((devices * seqs, tiles, LANES), BF16)],
        scratch=[pltpu.VMEM((devices * seqs * tiles, LANES), F32)],
        n_in=3,
        flops=2 * devices * seqs * hyper_weight.size,
        nbytes=4 * hyper_weight.size,
    )(task_of[:, None], task_codes, hyper_weight)[0]
    adapt = lax.all_to_all(
        sent.reshape(devices, seqs, tiles, LANES), ("dp", "mp"), 0, 0, tiled=True
    )
    if not whole_tiles:
        adapt = adapt.transpose(1, 0, 2, 3).reshape(seqs, rows, LANES)
    low, b4, tok_t = call(
        low_rank_kernel,
        [
            sds((tok_dev, LANES), BF16),
            sds((seqs, LANES, KV), BF16),
            sds((D, tok_dev), BF16),
        ],
        scratch=[pltpu.VMEM((B_ROWS, LANES), F32), pltpu.VMEM((seqs, rows, LANES), BF16)],
        n_in=2,
        flops=4 * tokens.size * LANES * seqs,
        nbytes=4 * tokens.size + 4 * seqs * rows * LANES,
    )(adapt, tokens)

    if width % LANES == 0 and depth % LANES == 0:
        mine, theirs = call(
            functools.partial(frozen_kernel, members),
            [sds((tok_dev, half), F32)] * 2,
            n_smem=1,
            n_in=3 + chips,
            flops=4 * tokens.size * half,
            nbytes=4 * tokens.size + 2 * D * half,
        )(place, frozen_weight, tokens, other_tokens, *[held[m] for m in range(chips)])
    else:
        own_half = lax.dynamic_slice_in_dim(frozen_weight, core * half, half, 1)
        moved = jnp.stack([held[m].reshape(members - 1, depth, width) for m in range(chips)], 1)
        moved = jnp.take(moved, jnp.arange(chips) ^ chip, axis=1)
        moved = moved.transpose(0, 2, 1, 3).reshape(members - 1, depth, half)
        blocks = jnp.concatenate([own_half[None], moved], axis=0)
        weight = jnp.take(blocks, jnp.arange(members) ^ me_mp, axis=0).reshape(D, half)
        mine = jnp.dot(tokens, weight, preferred_element_type=F32)
        theirs = jnp.dot(other_tokens, weight, preferred_element_type=F32)
    received = xor_permute(theirs, "dp", 1)

    split = (devices, seqs, tiles, LANES)
    grads = call(
        backward_kernel,
        [sds(split if whole_tiles else (seqs, rows, LANES), BF16)],
        scratch=[
            pltpu.VMEM((tok_dev, KV), F32),
            pltpu.VMEM((B_ROWS, LANES), F32),
            pltpu.VMEM((seqs, rows, LANES), BF16),
        ],
        n_smem=2,
        n_in=6,
        flops=4 * tokens.size * LANES * seqs,
        nbytes=4 * tokens.size,
    )(place, scale, mine, received, teacher, low, b4, tok_t)[0]
    if not whole_tiles:
        grads = grads.reshape(seqs, devices, tiles, LANES).transpose(1, 0, 2, 3)
    routed = lax.all_to_all(grads, ("dp", "mp"), 0, 0, tiled=True)
    step = 16 if whole_tiles else tiles
    return pl.pallas_call(
        hyper_kernel,
        grid=(tiles // step,),
        out_shape=sds((width_h, tiles * LANES), F32),
        in_specs=[
            pl.BlockSpec((width_h, devices * seqs), lambda i: (0, 0)),
            pl.BlockSpec((devices, seqs, step, LANES), lambda i: (0, 0, i, 0)),
        ],
        out_specs=pl.BlockSpec((width_h, step * LANES), lambda i: (0, i)),
        scratch_shapes=[pltpu.VMEM((devices * seqs * step, LANES), F32)],
        compiler_params=pltpu.CompilerParams(vmem_limit_bytes=VMEM_LIMIT),
    )(codes_t, routed)


def solution(mesh):
    placed = (
        P(),
        P(None, ("dp", "mp")),
        P("mp", None),
        P(("dp", "mp"), None),
        P(("dp", "mp"), None),
        P(("dp", "mp")),
        P(),
        P(),
    )
    return jax.shard_map(
        shards, mesh=mesh, in_specs=placed, out_specs=P(None, ("dp", "mp")), check_vma=False
    )
```

time: 293 us -> 127 us (0.43)
  waiting for transfers between devices: 153 us -> 56.9 us
  local copies, waits for them, and re-layouts: 56.5 us -> 6.49 us
  starting transfers between devices: 0.6 us -> 36.9 us
  blocking collectives: 35.7 us -> 0 us
  matrix products: 22.9 us -> 0.2 us
  Pallas kernels: 0 us -> 21.6 us
  between operations: 14.7 us -> 1.51 us
  other arithmetic: 7.91 us -> 2.85 us
    all_gather x2 -> x0, waiting for transfers between devices: 120 us -> none  [the longest x1 98.4 us: shards(): gathered = lax.all_gather(own_half, 'mp', axis=0, tiled=True)]
    all_to_all x2 -> x0, blocking collectives: 35.7 us -> none  [the longest x1 24.6 us: shards(): lax.all_to_all(rounded, 'dp', split_axis=1, concat_axis=1, tiled=True)]
    reduce_scatter x1 -> x0, waiting for transfers between devices: 32.8 us -> none  [shards(): lax.psum_scatter(routed.astype(jnp.float32).astype(jnp.bfloat16), 'mp', s...]
    all_to_all x0 -> x3, waiting for transfers between devices: none -> 31.2 us  [the longest x1 19.1 us: shards(): routed = lax.all_to_all(grads, ('dp', 'mp'), 0, 0, tiled=True)]
    all_to_all x0 -> x3, starting transfers between devices: none -> 25.8 us  [the longest x1 11.7 us: shards(): lax.all_to_all(sent.reshape(devices, seqs, tiles, LANES), ('dp', 'mp'), 0...]
    ppermute x1 -> x9, waiting for transfers between devices: 0.01 us -> 25.7 us  [xor_permute(): lax.ppermute(array, axis, [(i, i ^ mask) for i in range(lax.axis_size(axi...]
    dot_general x10 -> x1, matrix products: 22.9 us -> 0.2 us  [shards(): jnp.dot(task_codes.T, (jnp.arange(n_tasks)[:, None] == task_of[None, :])....]
    pallas_call x0 -> x5, Pallas kernels: none -> 21.6 us  [the longest x1 7.38 us: shards(): call(functools.partial(frozen_kernel, members), [sds((tok_dev, half), F32...]
  transfers between devices with their start and end apart: 4 -> 12, of which waited for: 3 -> 6; matrix products, arithmetic and copies ran while one was open for 15% -> 6% of each run, Pallas kernels for 0% -> 11%
where the time goes in v1:
time: 127 us; the launch traced here: 126 us
  waiting for transfers between devices  56.9 us (45%)
  starting transfers between devices  36.9 us (29%)
  Pallas kernels  21.6 us (17%)
  local copies, waits for them, and re-layouts  6.49 us (5%)
  other arithmetic  2.85 us (2%)
  between operations  1.51 us (1%)
    ppermute x9, waiting for transfers between devices, xor_permute(): lax.ppermute(array, axis, [(i, i ^ mask) for i in range(lax.axis_size(axi...  25.7 us
    all_to_all x1, waiting for transfers between devices, shards(): routed = lax.all_to_all(grads, ('dp', 'mp'), 0, 0, tiled=True)  19.1 us
    all_to_all x1, starting transfers between devices, shards(): lax.all_to_all(sent.reshape(devices, seqs, tiles, LANES), ('dp', 'mp'), 0...  11.7 us
    ppermute x9, starting transfers between devices, xor_permute(): lax.ppermute(array, axis, [(i, i ^ mask) for i in range(lax.axis_size(axi...  11.1 us
    all_to_all x1, starting transfers between devices, shards(): lax.all_to_all(jnp.broadcast_to(seq_slot[None], (devices, seqs)), ('dp',...  11 us
    all_to_all x1, waiting for transfers between devices, shards(): lax.all_to_all(sent.reshape(devices, seqs, tiles, LANES), ('dp', 'mp'), 0...  9.2 us
    pallas_call x1, Pallas kernels, shards(): call(functools.partial(frozen_kernel, members), [sds((tok_dev, half), F32...  7.38 us
    pallas_call x1, Pallas kernels, shards(): call(backward_kernel, [sds(split if whole_tiles else (seqs, rows, LANES),...  5.32 us
  transfers between devices with their start and end apart: 12, of which 6 were waited for; matrix products, arithmetic and copies ran while one was open for 6% of the time, Pallas kernels for 11%

profile of v1, /device:TPU:1, one launch (start us, length us, event | category | flops | bytes accessed | tf_op | source)
XLA Modules:
  0.0 126.4 jit_solution(9068249081430304208)
XLA Ops:
  0.0 1.0 constant_dynamic-slice_fusion
  1.1 2.2 %collective-permute-start.1 = (bf16[1280,128]{1,0:T(8,128)(2,1)S(1)}, bf16[1280,128]{1,0:T(8,128)(2,1)S(1)}, u32[]{:S(2)}, u32[]{:S(2)}) collective-permute-start(bf16[1280,128]{1,0:T(8,128)(2,1)S(1)} %constant_dynamic-slice_fusion), channel_id=1, source_target_pairs={{0,1},{1,0},{2,3},{3,2},{4,5},{5,4},{6,7},{7,6},{8,9},{9,8},{10,11... | collective-permute-start | bytes 983048 | tf_op jit(solution)/shard_map/ppermute | solution.py:58
  3.3 2.3 %collective-permute-start.2 = (bf16[1280,128]{1,0:T(8,128)(2,1)S(1)}, bf16[1280,128]{1,0:T(8,128)(2,1)S(1)}, u32[]{:S(2)}, u32[]{:S(2)}) collective-permute-start(bf16[1280,128]{1,0:T(8,128)(2,1)S(1)} %constant_dynamic-slice_fusion), channel_id=1, source_target_pairs={{0,2},{1,3},{2,0},{3,1},{4,6},{5,7},{6,4},{7,5},{8,10},{9,11},{10,... | collective-permute-start | bytes 983048 | tf_op jit(solution)/shard_map/ppermute | solution.py:58
  5.6 1.2 collective-permute-start
  6.8 10.1 %collective-permute-done.1 = bf16[1280,128]{1,0:T(8,128)(2,1)S(1)} collective-permute-done((bf16[1280,128]{1,0:T(8,128)(2,1)S(1)}, bf16[1280,128]{1,0:T(8,128)(2,1)S(1)}, u32[]{:S(2)}, u32[]{:S(2)}) %collective-permute-start.1) | collective-permute-done | bytes 327712 | tf_op jit(solution)/shard_map/ppermute | solution.py:58
  17.0 9.6 %collective-permute-done.3 = bf16[1280,128]{1,0:T(8,128)(2,1)S(1)} collective-permute-done((bf16[1280,128]{1,0:T(8,128)(2,1)S(1)}, bf16[1280,128]{1,0:T(8,128)(2,1)S(1)}, u32[]{:S(2)}, u32[]{:S(2)}) %collective-permute-start.3) | collective-permute-done | bytes 327712 | tf_op jit(solution)/shard_map/ppermute | solution.py:58
  26.7 1.3 %collective-permute-start.4 = (bf16[3840,128]{1,0:T(8,128)(2,1)S(1)}, bf16[3840,128]{1,0:T(8,128)(2,1)S(1)}, u32[]{:S(2)}, u32[]{:S(2)}) collective-permute-start(bf16[3840,128]{1,0:T(8,128)(2,1)S(1)} %constant_dynamic-update-slice_fusion.refs_0_), channel_id=1, source_target_pairs={{0,8},{4,12},{8,0},{12,4},{16,24},{20,28},{24,16},{28,20},{1,9},{5... | collective-permute-start | bytes 2949128 | tf_op jit(solution)/shard_map/ppermute | solution.py:58
  28.0 1.2 collective-permute-start.5
  29.8 11.0 %all-to-all-start = ((s32[32,1,2]{2,1,0:T(1,128)}), s32[32,1,2]{2,1,0:T(1,128)S(1)}, u32[]{:S(2)}, u32[]{:S(2)}) async-start(s32[32,1,2]{2,1,0:T(1,128)} %broadcast_in_dim.21), calls=%async_computation | async-start | bytes 32768 | tf_op jit(solution)/shard_map/all_to_all | solution.py:237
  41.0 5.9 %collective-permute-done.4.refs_1_ = bf16[3840,128]{1,0:T(8,128)(2,1)S(1)} collective-permute-done((bf16[3840,128]{1,0:T(8,128)(2,1)S(1)}, bf16[3840,128]{1,0:T(8,128)(2,1)S(1)}, u32[]{:S(2)}, u32[]{:S(2)}) %collective-permute-start.4) | collective-permute-done | bytes 983072 | tf_op jit(solution)/shard_map/ppermute | solution.py:58
  47.0 1.3 %collective-permute-start.6 = (bf16[1920,128]{1,0:T(8,128)(2,1)S(1)}, bf16[1920,128]{1,0:T(8,128)(2,1)}, u32[]{:S(2)}, u32[]{:S(2)}) collective-permute-start(bf16[1920,128]{1,0:T(8,128)(2,1)S(1)} %slice.15), channel_id=1, source_target_pairs={{0,16},{4,20},{8,24},{12,28},{16,0},{20,4},{24,8},{28,12},{1,17},{... | collective-permute-start | bytes 1474568 | tf_op jit(solution)/shard_map/ppermute | solution.py:58
  49.1 1.2 collective-permute-start.7
  51.1 2.9 %all-to-all-done = s32[32,1,2]{2,1,0:T(1,128)S(1)} async-done(((s32[32,1,2]{2,1,0:T(1,128)}), s32[32,1,2]{2,1,0:T(1,128)S(1)}, u32[]{:S(2)}, u32[]{:S(2)}) %all-to-all-start) | async-done | bytes 288 | tf_op jit(solution)/shard_map/all_to_all | solution.py:237
  54.2 1.4 %copy-done = bf16[128,6144]{1,0:T(8,128)(2,1)S(1)} copy-done((bf16[128,6144]{1,0:T(8,128)(2,1)S(1)}, bf16[128,6144]{1,0:T(8,128)(2,1)}, u32[]{:S(2)}) %copy-start) | copy-done | bytes 1572888
  55.6 2.0 %shard_map.83 = bf16[64,48,128]{2,1,0:T(8,128)(2,1)} custom-call(s32[64,1]{1,0:T(8,128)S(1)} %copy.19.task_ref, bf16[16,128]{1,0:T(8,128)(2,1)S(1)} %copy-done.2, bf16[128,6144]{1,0:T(8,128)(2,1)S(1)} %copy-done), custom_call_target="tpu_custom_call" | custom-call | flops 100663296 | bytes 3145728 | tf_op jit(solution)/shard_map/pallas_call | solution.py:266
  57.6 11.7 %all-to-all-start.1 = ((bf16[32,2,48,128]{3,2,1,0:T(8,128)(2,1)}), bf16[32,2,48,128]{3,2,1,0:T(8,128)(2,1)}, u32[]{:S(2)}, u32[]{:S(2)}) async-start(bf16[32,2,48,128]{3,2,1,0:T(8,128)(2,1)} %bitcast.8), calls=%async_computation.1 | async-start | bytes 1572864 | tf_op jit(solution)/shard_map/all_to_all | solution.py:274
  71.4 1.2 pad_maximum_fusion.refs_3_
  72.7 7.4 %shard_map.82 = (f32[256,512]{1,0:T(8,128)S(1)}, f32[256,512]{1,0:T(8,128)}) custom-call(s32[3]{0:T(128)S(1)} %pad_add_fusion.place_ref, bf16[1280,1024]{1,0:T(8,128)(2,1)} %weight_ref.2, bf16[256,5120]{1,0:T(8,128)(2,1)} %tokens_ref.1, bf16[256,5120]{1,0:T(8,128)(2,1)} %collective-permute-done.other_ref, ...), custom_call_target="tpu_custom_call" | custom-call | flops 2684354560 | bytes 10485760 | tf_op jit(solution)/shard_map/pallas_call | solution.py:293
  81.0 9.2 %all-to-all-done.1.adapt_ref = bf16[32,2,48,128]{3,2,1,0:T(8,128)(2,1)} async-done(((bf16[32,2,48,128]{3,2,1,0:T(8,128)(2,1)}), bf16[32,2,48,128]{3,2,1,0:T(8,128)(2,1)}, u32[]{:S(2)}, u32[]{:S(2)}) %all-to-all-start.1) | async-done | bytes 786464 | tf_op jit(solution)/shard_map/all_to_all | solution.py:274
  90.2 4.2 %shard_map.84 = (bf16[256,128]{1,0:T(8,128)(2,1)S(1)}, bf16[2,128,1024]{2,1,0:T(8,128)(2,1)S(1)}, bf16[5120,256]{1,0:T(8,128)(2,1)S(1)}) custom-call(bf16[32,2,48,128]{3,2,1,0:T(8,128)(2,1)} %all-to-all-done.1.adapt_ref, bf16[256,5120]{1,0:T(8,128)(2,1)} %tokens_ref.1), custom_call_target="tpu_custom_call" | custom-call | flops 1342177280 | bytes 6815744 | tf_op jit(solution)/shard_map/pallas_call | solution.py:279
  94.4 5.3 %shard_map.85 = bf16[32,2,48,128]{3,2,1,0:T(8,128)(2,1)} custom-call(s32[3]{0:T(128)S(1)} %pad_add_fusion.place_ref, f32[2]{0:T(128)S(1)} %fusion.1.scale_ref, f32[256,512]{1,0:T(8,128)S(1)} %get-tuple-element.10.mine_ref, f32[256,512]{1,0:T(8,128)S(1)} %collective-permute-done.8.theirs_ref, bf16[256,1024]{1,0:T(8,128)(2,1)S(1)} %copy-done.1, ...), custom_call_target="tpu_custom_call" | custom-call | flops 1342177280 | bytes 5242880 | tf_op jit(solution)/shard_map/pallas_call | solution.py:313
  99.7 3.2 %all-to-all-start.2 = ((bf16[32,2,48,128]{3,2,1,0:T(8,128)(2,1)}), bf16[32,2,48,128]{3,2,1,0:T(8,128)(2,1)S(1)}, u32[]{:S(2)}, u32[]{:S(2)}) async-start(bf16[32,2,48,128]{3,2,1,0:T(8,128)(2,1)} %shard_map.85), calls=%async_computation.2 | async-start | bytes 1572864 | tf_op jit(solution)/shard_map/all_to_all | solution.py:328
  104.7 19.1 %all-to-all-done.2.grads_ref = bf16[32,2,48,128]{3,2,1,0:T(8,128)(2,1)S(1)} async-done(((bf16[32,2,48,128]{3,2,1,0:T(8,128)(2,1)}), bf16[32,2,48,128]{3,2,1,0:T(8,128)(2,1)S(1)}, u32[]{:S(2)}, u32[]{:S(2)}) %all-to-all-start.2) | async-done | bytes 786464 | tf_op jit(solution)/shard_map/all_to_all | solution.py:328
  123.7 2.7 %shard_map.86 = f32[128,6144]{1,0:T(8,128)} custom-call(bf16[128,64]{1,0:T(8,128)(2,1)S(1)} %bitcast.12, bf16[32,2,48,128]{3,2,1,0:T(8,128)(2,1)S(1)} %all-to-all-done.2.grads_ref), custom_call_target="tpu_custom_call" | custom-call | tf_op jit(solution)/shard_map/pallas_call | solution.py:330
  (47 shorter events, 6.2 us)
Async XLA Ops:
  0.0 29.2 %copy-start.3 = (s32[2]{0:T(128)S(1)}, s32[2]{0:T(128)}, u32[]{:S(2)}) copy-start(s32[2]{0:T(128)} %param.13) | copy-start | bytes 28
  0.0 40.8 %copy-start.4 = (s32[8]{0:T(128)S(1)}, s32[8]{0:T(128)}, u32[]{:S(2)}) copy-start(s32[8]{0:T(128)} %param.14) | copy-start | bytes 100
  0.0 50.3 %copy-start.5 = (s32[16]{0:T(128)S(1)}, s32[16]{0:T(128)}, u32[]{:S(2)}) copy-start(s32[16]{0:T(128)} %param.15) | copy-start | bytes 196
  0.0 54.2 %copy-start.2 = (bf16[16,128]{1,0:T(8,128)(2,1)S(1)}, bf16[16,128]{1,0:T(8,128)(2,1)}, u32[]{:S(2)}) copy-start(bf16[16,128]{1,0:T(8,128)(2,1)} %codes_ref.1) | copy-start | bytes 12292
  1.1 15.9 %collective-permute-start.1 = (bf16[1280,128]{1,0:T(8,128)(2,1)S(1)}, bf16[1280,128]{1,0:T(8,128)(2,1)S(1)}, u32[]{:S(2)}, u32[]{:S(2)}) collective-permute-start(bf16[1280,128]{1,0:T(8,128)(2,1)S(1)} %constant_dynamic-slice_fusion), channel_id=1, source_target_pairs={{0,1},{1,0},{2,3},{3,2},{4,5},{5,4},{6,7},{7,6},{8,9},{9,8},{10,11... | collective-permute-start | bytes 983048 | tf_op jit(solution)/shard_map/ppermute | solution.py:58
  3.3 13.7 %collective-permute-start.2 = (bf16[1280,128]{1,0:T(8,128)(2,1)S(1)}, bf16[1280,128]{1,0:T(8,128)(2,1)S(1)}, u32[]{:S(2)}, u32[]{:S(2)}) collective-permute-start(bf16[1280,128]{1,0:T(8,128)(2,1)S(1)} %constant_dynamic-slice_fusion), channel_id=1, source_target_pairs={{0,2},{1,3},{2,0},{3,1},{4,6},{5,7},{6,4},{7,5},{8,10},{9,11},{10,... | collective-permute-start | bytes 983048 | tf_op jit(solution)/shard_map/ppermute | solution.py:58
  5.6 21.1 %collective-permute-start.3 = (bf16[1280,128]{1,0:T(8,128)(2,1)S(1)}, bf16[1280,128]{1,0:T(8,128)(2,1)S(1)}, u32[]{:S(2)}, u32[]{:S(2)}) collective-permute-start(bf16[1280,128]{1,0:T(8,128)(2,1)S(1)} %constant_dynamic-slice_fusion), channel_id=1, source_target_pairs={{0,3},{1,2},{2,1},{3,0},{4,7},{5,6},{6,5},{7,4},{8,11},{9,10},{10,... | collective-permute-start | bytes 983048 | tf_op jit(solution)/shard_map/ppermute | solution.py:58
  5.6 67.1 %collective-permute-start = (bf16[256,5120]{1,0:T(8,128)(2,1)}, bf16[256,5120]{1,0:T(8,128)(2,1)}, u32[]{:S(2)}, u32[]{:S(2)}) collective-permute-start(bf16[256,5120]{1,0:T(8,128)(2,1)} %tokens_ref.1), channel_id=1, source_target_pairs={{0,4},{4,0},{8,12},{12,8},{16,20},{20,16},{24,28},{28,24},{1,5},{5... | collective-permute-start | bytes 7864328 | tf_op jit(solution)/shard_map/ppermute | solution.py:58
  26.7 20.2 %collective-permute-start.4 = (bf16[3840,128]{1,0:T(8,128)(2,1)S(1)}, bf16[3840,128]{1,0:T(8,128)(2,1)S(1)}, u32[]{:S(2)}, u32[]{:S(2)}) collective-permute-start(bf16[3840,128]{1,0:T(8,128)(2,1)S(1)} %constant_dynamic-update-slice_fusion.refs_0_), channel_id=1, source_target_pairs={{0,8},{4,12},{8,0},{12,4},{16,24},{20,28},{24,16},{28,20},{1,9},{5... | collective-permute-start | bytes 2949128 | tf_op jit(solution)/shard_map/ppermute | solution.py:58
  28.0 20.3 %collective-permute-start.5 = (bf16[3840,128]{1,0:T(8,128)(2,1)S(1)}, bf16[3840,128]{1,0:T(8,128)(2,1)S(1)}, u32[]{:S(2)}, u32[]{:S(2)}) collective-permute-start(bf16[3840,128]{1,0:T(8,128)(2,1)S(1)} %constant_dynamic-update-slice_fusion.refs_0_), channel_id=1, source_target_pairs={{0,16},{4,20},{8,24},{12,28},{16,0},{20,4},{24,8},{28,12},{1,17},{... | collective-permute-start | bytes 2949128 | tf_op jit(solution)/shard_map/ppermute | solution.py:58
  29.8 24.1 %all-to-all-start = ((s32[32,1,2]{2,1,0:T(1,128)}), s32[32,1,2]{2,1,0:T(1,128)S(1)}, u32[]{:S(2)}, u32[]{:S(2)}) async-start(s32[32,1,2]{2,1,0:T(1,128)} %broadcast_in_dim.21), calls=%async_computation | async-start | bytes 32768 | tf_op jit(solution)/shard_map/all_to_all | solution.py:237
  47.0 24.4 %collective-permute-start.6 = (bf16[1920,128]{1,0:T(8,128)(2,1)S(1)}, bf16[1920,128]{1,0:T(8,128)(2,1)}, u32[]{:S(2)}, u32[]{:S(2)}) collective-permute-start(bf16[1920,128]{1,0:T(8,128)(2,1)S(1)} %slice.15), channel_id=1, source_target_pairs={{0,16},{4,20},{8,24},{12,28},{16,0},{20,4},{24,8},{28,12},{1,17},{... | collective-permute-start | bytes 1474568 | tf_op jit(solution)/shard_map/ppermute | solution.py:58
  49.1 22.3 %collective-permute-start.7 = (bf16[1920,128]{1,0:T(8,128)(2,1)}, bf16[1920,128]{1,0:T(8,128)(2,1)}, u32[]{:S(2)}, u32[]{:S(2)}) collective-permute-start(bf16[1920,128]{1,0:T(8,128)(2,1)} %slice.16), channel_id=1, source_target_pairs={{0,8},{4,12},{8,0},{12,4},{16,24},{20,28},{24,16},{28,20},{1,9},{5... | collective-permute-start | bytes 1474568 | tf_op jit(solution)/shard_map/ppermute | solution.py:58
  54.2 1.4 %copy-start = (bf16[128,6144]{1,0:T(8,128)(2,1)S(1)}, bf16[128,6144]{1,0:T(8,128)(2,1)}, u32[]{:S(2)}) copy-start(bf16[128,6144]{1,0:T(8,128)(2,1)} %weight_ref.3) | copy-start | bytes 4718596
  57.6 32.6 %all-to-all-start.1 = ((bf16[32,2,48,128]{3,2,1,0:T(8,128)(2,1)}), bf16[32,2,48,128]{3,2,1,0:T(8,128)(2,1)}, u32[]{:S(2)}, u32[]{:S(2)}) async-start(bf16[32,2,48,128]{3,2,1,0:T(8,128)(2,1)} %bitcast.8), calls=%async_computation.1 | async-start | bytes 1572864 | tf_op jit(solution)/shard_map/all_to_all | solution.py:274
  80.0 14.4 %collective-permute-start.8 = (f32[256,512]{1,0:T(8,128)}, f32[256,512]{1,0:T(8,128)S(1)}, u32[]{:S(2)}, u32[]{:S(2)}) collective-permute-start(f32[256,512]{1,0:T(8,128)} %get-tuple-element.11), channel_id=1, source_target_pairs={{0,4},{4,0},{8,12},{12,8},{16,20},{20,16},{24,28},{28,24},{1,5},{5... | collective-permute-start | bytes 1572872 | tf_op jit(solution)/shard_map/ppermute | solution.py:58
  80.4 14.1 %copy-start.1 = (bf16[256,1024]{1,0:T(8,128)(2,1)S(1)}, bf16[256,1024]{1,0:T(8,128)(2,1)}, u32[]{:S(2)}) copy-start(bf16[256,1024]{1,0:T(8,128)(2,1)} %teacher_ref.1) | copy-start | bytes 1572868
  99.7 24.0 %all-to-all-start.2 = ((bf16[32,2,48,128]{3,2,1,0:T(8,128)(2,1)}), bf16[32,2,48,128]{3,2,1,0:T(8,128)(2,1)S(1)}, u32[]{:S(2)}, u32[]{:S(2)}) async-start(bf16[32,2,48,128]{3,2,1,0:T(8,128)(2,1)} %shard_map.85), calls=%async_computation.2 | async-start | bytes 1572864 | tf_op jit(solution)/shard_map/all_to_all | solution.py:328

commit v2 on v1

--- a/solution.py
+++ b/solution.py
@@ -11,9 +11,11 @@
 D = 5120
 KV = 1024
 R = 32
+TPG = 4
 SEQ_LEN = 128
 LANES = 128
 PACK = LANES // R
+SLOT_ROWS = 16
 A_ROWS = D * R // LANES
 B_ROWS = R * KV // LANES
 COL_TILES = KV // LANES
@@ -23,7 +25,7 @@
 RANK_SCALE = 1.0 / math.sqrt(R)
 F32 = jnp.float32
 BF16 = jnp.bfloat16
-VMEM_LIMIT = 48 * 1024 * 1024
+VMEM_LIMIT = 16 * 1024 * 1024
 
 
 def dot(a, b):
@@ -58,25 +60,92 @@
     return lax.ppermute(array, axis, [(i, i ^ mask) for i in range(lax.axis_size(axis))])
 
 
-def adapters_kernel(tiles, task_ref, codes_ref, weight_ref, out_ref, scr):
-    rows = task_ref.shape[0]
+def chunk_kernel(place_ref, slot_ref, weight_ref, near_ref, top_ref, bottom_ref, sems):
+    depth = weight_ref.shape[0]
+    width = near_ref.shape[1]
+    mid = depth // 2
+    half = weight_ref.shape[1] // 2
+    at = pl.ds(pl.multiple_of(place_ref[1] * half + place_ref[2] * width, LANES), width)
+    copies = [
+        pltpu.make_async_copy(
+            weight_ref.at[pl.ds(first, size), at], out.at[pl.ds(0, size), :], sems.at[i]
+        )
+        for i, (first, size, out) in enumerate(
+            [(0, depth, near_ref), (0, mid, top_ref), (mid, mid, bottom_ref)]
+        )
+    ]
+    for copy in copies:
+        copy.start()
+    row = lax.broadcasted_iota(jnp.int32, (SLOT_ROWS, width), 0)
+    note = jnp.zeros((SLOT_ROWS, width), jnp.int32)
+    for s in range(slot_ref.shape[0]):
+        note = jnp.where(row == s, slot_ref[s], note)
+    note = note.astype(F32).astype(BF16)
+    near_ref[depth:, :] = note
+    top_ref[mid:, :] = note
+    bottom_ref[mid:, :] = note
+    for copy in copies:
+        copy.wait()
+
+
+def adapters_kernel(tiles, share_ref, codes_ref, weight_ref, out_ref, scr):
+    groups, tpg = out_ref.shape[:2]
+    rows = groups * tpg
     tasks = codes_ref.shape[0]
-    pick = (task_ref[...] == lax.broadcasted_iota(jnp.int32, (rows, tasks), 1)).astype(BF16)
+    row = lax.broadcasted_iota(jnp.int32, (rows, 1), 0)
+    group, task = row // tpg, row % tpg
+    live = jnp.zeros((rows, 1), jnp.int32)
+    for g in range(groups):
+        task = task + jnp.where(group > g, share_ref[g], 0)
+        live = live + jnp.where(group == g, share_ref[g], 0)
+    task = jnp.where(row % tpg < live, task, -1)
+    pick = (task == lax.broadcasted_iota(jnp.int32, (rows, tasks), 1)).astype(BF16)
     chosen = dot(pick, codes_ref[...]).astype(BF16)
     for k in range(tiles):
         part = dot(chosen, weight_ref[:, k * LANES : (k + 1) * LANES])
         scr[pl.ds(k, rows, stride=tiles), :] = part
-    for i in range(rows):
-        out_ref[i] = scr[i * tiles : (i + 1) * tiles, :].astype(BF16)
-
-
-def low_rank_kernel(adapt_ref, tokens_ref, low_ref, b4_ref, tok_t_ref, scr, held):
+    for g in range(groups):
+        for i in range(tpg):
+            at = (g * tpg + i) * tiles
+            out_ref[g, i] = scr[at : at + tiles, :].astype(BF16)
+
+
+def choose_kernel(n_smem, n, *refs):
+    slot_refs, got_ref, out_refs = refs[:n], refs[n], refs[n + 1 :]
+    for at, (slots, out) in enumerate(zip(slot_refs, out_refs)):
+        if at >= n_smem:
+            rows = slots.shape[0]
+            notes = slots[rows - SLOT_ROWS :, :].astype(F32)
+        for s in range(out.shape[1]):
+            if at < n_smem:
+                slot = slots[s]
+            else:
+                slot = jnp.max(notes[s : s + 1, :].astype(jnp.int32))
+            out[:, s] = got_ref[:, slot]
+
+
+def codes_kernel(group_seqs, share_ref, slots_ref, codes_ref, out_ref):
+    rows = slots_ref.shape[0]
+    task = slots_ref[...]
+    group = lax.broadcasted_iota(jnp.int32, (rows, 1), 0) // group_seqs
+    for g in range(share_ref.shape[0] - 1):
+        task = task + jnp.where(group > g, share_ref[g], 0)
+    tasks = codes_ref.shape[0]
+    pick = (task == lax.broadcasted_iota(jnp.int32, (rows, tasks), 1)).astype(BF16)
+    out_ref[...] = dot(pick, codes_ref[...]).T.astype(BF16)
+
+
+def low_rank_kernel(n, place_ref, *refs):
+    adapt_refs, (tokens_ref, low_ref, b4_ref, tok_t_ref, scr, held) = refs[:n], refs[n:]
     seqs = b4_ref.shape[0]
+    adapt_ref = adapt_refs[0]
     if len(adapt_ref.shape) == 4:
-        tiles = adapt_ref.shape[2]
-        for i in range(adapt_ref.shape[0]):
-            for s in range(seqs):
-                held[s, i * tiles : (i + 1) * tiles, :] = adapt_ref[i, s]
+        groups, _, tiles, _ = adapt_ref.shape
+        for k, part in enumerate(adapt_refs):
+            for g in range(groups):
+                at = pl.multiple_of((g * n + (place_ref[0] ^ k)) * tiles, 16)
+                for s in range(seqs):
+                    held[s, pl.ds(at, tiles), :] = part[g, s]
         adapt_ref = held
     lane = lax.broadcasted_iota(jnp.int32, (BLOCK_D, LANES * seqs), 1)
     row = lax.broadcasted_iota(jnp.int32, (BLOCK_D, LANES * seqs), 0)
@@ -111,41 +180,81 @@
                 b4_ref[s, j * R : (j + 1) * R, c * LANES : (c + 1) * LANES] = piece
 
 
-def frozen_kernel(members, place_ref, weight_ref, own_ref, other_ref, *refs):
-    pieces, (out_own, out_other) = refs[:-2], refs[-2:]
-    half = out_own.shape[1]
-    depth = weight_ref.shape[0]
-    width = pieces[0].shape[1]
+def frozen_kernel(n_tok, depth, own, layout, has_acc, place_ref, *refs):
+    refs = iter(refs)
+    token_refs = [next(refs) for _ in range(n_tok)]
+    weight_ref = next(refs) if own else None
+    sets = [
+        ([[next(refs) for _ in range(n)] for n in counts], segments) for counts, segments in layout
+    ]
+    accs = [next(refs) for _ in range(n_tok)] if has_acc else [None] * n_tok
+    outs = list(refs)
     me, core, chip = place_ref[0], place_ref[1], place_ref[2]
-    rows = own_ref.shape[0]
-
-    def both(block):
-        cols = pl.ds(pl.multiple_of(block * depth, LANES), depth)
-        return jnp.concatenate([own_ref[:, cols], other_ref[:, cols]], axis=0)
-
-    first = dot(both(me), weight_ref[:, pl.ds(pl.multiple_of(core * half, LANES), half)])
-    out_own[...] = first[:rows]
-    out_other[...] = first[rows:]
-    for k in range(1, members):
-        left = both(me ^ k)
-        span = slice((k - 1) * depth, k * depth)
-        for m in range(0, len(pieces), 2):
-            pair = range(m, min(m + 2, len(pieces)))
-            right = jnp.concatenate([pieces[i][span, :] for i in pair], axis=1)
-            part = dot(left, right)
+    half = outs[0].shape[1]
+    width = sets[0][0][0][0].shape[1]
+    chips = len(sets[0][0])
+
+    def cols(k, first, size):
+        return pl.ds(pl.multiple_of((me ^ k) * depth + first, LANES), size)
+
+    for tok, acc, out in zip(token_refs, accs, outs):
+        if own:
+            block = weight_ref[:, pl.ds(pl.multiple_of(core * half, LANES), half)]
+            out[...] = dot(tok[:, cols(0, 0, depth)], block)
+        else:
+            out[...] = acc[...]
+        for m in range(0, chips, 2):
+            pair = range(m, min(m + 2, chips))
+            total = None
+            for pieces, segments in sets:
+                at = 0
+                for k, first, size in segments:
+                    parts = []
+                    for i in pair:
+                        n = pieces[i][0].shape[0]
+                        piece, row = (pieces[i][0], at) if at < n else (pieces[i][1], at - n)
+                        parts.append(piece[row : row + size, :])
+                    part = dot(tok[:, cols(k, first, size)], jnp.concatenate(parts, axis=1))
+                    total = part if total is None else total + part
+                    at += size
             for at, i in enumerate(pair):
-                cols = pl.ds(pl.multiple_of((chip ^ i) * width, LANES), width)
-                out_own[:, cols] += part[:rows, at * width : (at + 1) * width]
-                out_other[:, cols] += part[rows:, at * width : (at + 1) * width]
+                where = pl.ds(pl.multiple_of((chip ^ i) * width, LANES), width)
+                out[:, where] += total[:, at * width : (at + 1) * width]
+
+
+def frozen_call(place, depth, half, tokens, weight, sets, accs):
+    rows = tokens[0].shape[0]
+    layout = [([len(x) for x in pieces], segments) for pieces, segments in sets]
+    flat = [x for pieces, _ in sets for piece in pieces for x in piece]
+    deep = sum(size for _, segments in sets for _, _, size in segments)
+    deep += 0 if weight is None else depth
+    weights = [] if weight is None else [weight]
+    return call(
+        functools.partial(
+            frozen_kernel, len(tokens), depth, weight is not None, layout, bool(accs)
+        ),
+        [sds((rows, half), F32)] * len(tokens),
+        n_smem=1,
+        n_in=len(tokens) + len(weights) + len(flat) + len(accs),
+        flops=2 * rows * half * deep * len(tokens),
+        nbytes=2 * deep * half + 4 * rows * half * len(tokens),
+    )(place, *tokens, *weights, *flat, *accs)
 
 
 def backward_kernel(
-    place_ref, scale_ref, mine_ref, theirs_ref, teacher_ref, low_ref, b4_ref, tok_t_ref, out_ref,
+    loss_scale, place_ref, share_ref, slot_ref, counts_ref, mine_ref, theirs_ref, teacher_ref, low_ref, b4_ref, tok_t_ref, out_ref,
     values, spaced, grads,
 ):
     seqs = b4_ref.shape[0]
     half = mine_ref.shape[1]
-    core = place_ref[1]
+    core, group = place_ref[1], place_ref[3]
+    n_tasks = counts_ref.shape[0]
+    first_task = jnp.int32(0)
+    for g in range(share_ref.shape[0]):
+        first_task = first_task + jnp.where(g < group, share_ref[g], 0)
+    all_counts = counts_ref[0]
+    for t in range(1, n_tasks):
+        all_counts = all_counts + counts_ref[t]
     values[:, pl.ds(pl.multiple_of(core * half, LANES), half)] = mine_ref[...]
     values[:, pl.ds(pl.multiple_of((1 - core) * half, LANES), half)] = theirs_ref[...]
     blocks = []
@@ -154,7 +263,9 @@
         low = low_ref[rows, :]
         b4 = b4_ref[s]
         error = values[rows, :] + dot(low, b4) * RANK_SCALE - teacher_ref[rows, :].astype(F32)
-        value_grad = (error * scale_ref[s]).astype(BF16)
+        count = jnp.full((1, KV), counts_ref[first_task + slot_ref[s]], jnp.int32).astype(F32)
+        mean = jnp.full((1, KV), all_counts, jnp.int32).astype(F32) / n_tasks
+        value_grad = (error * (mean / count * loss_scale)).astype(BF16)
         blocks.append((dot_nt(value_grad, b4) * RANK_SCALE).astype(BF16))
         second = dot(low.T, value_grad)[:R] * RANK_SCALE
         for c in range(COL_TILES):
@@ -207,6 +318,10 @@
         out_ref[:, k * LANES : (k + 1) * LANES] = dot(codes_t, part)
 
 
+def tied(*groups):
+    return lax.optimization_barrier(groups)
+
+
 def shards(
     task_codes, hyper_weight, frozen_weight, tokens, teacher, seq_slot, task_share, token_counts
 ):
@@ -219,91 +334,145 @@
     depth = frozen_weight.shape[0]
     tiles = hyper_weight.shape[1] // LANES
     rows = A_ROWS + B_ROWS
-    n_tasks, width_h = task_codes.shape
+    width_h = task_codes.shape[1]
     loss_scale = 1.0 / math.sqrt(tok_dev * members)
     me_dp, me_mp = lax.axis_index("dp"), lax.axis_index("mp")
     core, chip = me_dp % 2, me_dp // 2
-    place = jnp.stack([me_mp, core, chip]).astype(jnp.int32)
+    place = jnp.stack([me_mp, core, chip, me_dp]).astype(jnp.int32)
     half = KV // 2
     width = half // chips
     whole_tiles = tiles % 16 == 0
 
-    chunk = lax.dynamic_slice_in_dim(frozen_weight, core * half + chip * width, width, 1)
-    arrived = jnp.concatenate(
-        [xor_permute(chunk, "mp", k) for k in range(1, members)], axis=0
-    )
     other_tokens = xor_permute(tokens, "dp", 1)
-
-    slots = lax.all_to_all(
-        jnp.broadcast_to(seq_slot[None], (devices, seqs)), ("dp", "mp"), 0, 0, tiled=True
-    ).reshape(-1)
-    offsets = jnp.cumsum(task_share) - task_share
-    task_of = jnp.repeat(offsets, members * seqs) + slots
-    codes_t = jnp.dot(
-        task_codes.T, (jnp.arange(n_tasks)[:, None] == task_of[None, :]).astype(BF16),
-        preferred_element_type=F32,
-    ).astype(BF16)
-    counts = token_counts.astype(F32)
-    task_weight = jnp.mean(counts) / counts
-    own_task = jnp.take(offsets, me_dp) + seq_slot
-    scale = jnp.take(task_weight, own_task) * loss_scale
-
-    held = {0: arrived}
-    middle = arrived.shape[0] // 2
-    for m in range(1, chips):
-        low_bit, high_bit = m & -m, 1 << (m.bit_length() - 1)
-        if low_bit == high_bit:
-            held[m] = xor_permute(arrived, "dp", m << 1)
-        else:
-            held[m] = jnp.concatenate(
-                [
-                    xor_permute(held[m ^ high_bit][:middle], "dp", high_bit << 1),
-                    xor_permute(held[m ^ low_bit][middle:], "dp", low_bit << 1),
-                ],
-                axis=0,
-            )
-
+    mid = depth // 2
+    fits = width % LANES == 0 and mid % LANES == 0 and members == 4
+    near_rows = [(1, 0, mid), (1, mid, mid)]
+    if fits:
+        near, top, bottom = pl.pallas_call(
+            chunk_kernel,
+            in_specs=[pl.BlockSpec(memory_space=pltpu.SMEM)] * 2
+            + [pl.BlockSpec(memory_space=pl.ANY)],
+            out_specs=[pl.BlockSpec(memory_space=pltpu.VMEM)] * 3,
+            out_shape=[sds((n + SLOT_ROWS, width), BF16) for n in (depth, mid, mid)],
+            scratch_shapes=[pltpu.SemaphoreType.DMA((3,))],
+            compiler_params=pltpu.CompilerParams(vmem_limit_bytes=VMEM_LIMIT),
+        )(place, seq_slot, frozen_weight)
+        near = xor_permute(near, "mp", 1)
+        top = xor_permute(top, "mp", 2)
+        bottom = xor_permute(bottom, "mp", 3)
+        far = jnp.concatenate([top[:mid], bottom[:mid]], axis=0)
+        rest = jnp.concatenate([far, xor_permute(far, "mp", 1)], axis=0)
+        rest_rows = [(2, 0, mid), (3, mid, mid), (3, 0, mid), (2, mid, mid)]
+        member_slots, n_smem = [seq_slot, near, top, bottom], 1
+    else:
+        chunk = lax.dynamic_slice_in_dim(frozen_weight, core * half + chip * width, width, 1)
+        near = xor_permute(chunk, "mp", 1)
+        rest = jnp.concatenate(
+            [xor_permute(chunk, "mp", k) for k in range(2, members)], axis=0
+        )
+        rest_rows = [(k, at, mid) for k in range(2, members) for at in (0, mid)]
+        member_slots = [seq_slot] + [xor_permute(seq_slot, "mp", k) for k in range(1, members)]
+        n_smem = members
+
+    def halves(parts):
+        if len(parts) == 2:
+            return parts
+        middle = parts[0].shape[0] // (2 * mid) * mid
+        return [parts[0][:middle], parts[0][middle:]]
+
+    def direct(block):
+        held = {0: [block]}
+        for m in range(1, chips):
+            if m & (m - 1) == 0:
+                held[m] = [xor_permute(block, "dp", m << 1)]
+        return held
+
+    def forwarded(held):
+        for m in range(1, chips):
+            if m not in held:
+                low_bit, high_bit = m & -m, 1 << (m.bit_length() - 1)
+                held[m] = [
+                    xor_permute(halves(held[m ^ high_bit])[0], "dp", high_bit << 1),
+                    xor_permute(halves(held[m ^ low_bit])[1], "dp", low_bit << 1),
+                ]
+        return [held[m] for m in range(chips)]
+
+    near_pieces = forwarded(direct(near))
+
+    split = (groups, TPG, tiles, LANES)
     sent = call(
         functools.partial(adapters_kernel, tiles),
-        [sds((devices * seqs, tiles, LANES), BF16)],
-        scratch=[pltpu.VMEM((devices * seqs * tiles, LANES), F32)],
-        n_in=3,
-        flops=2 * devices * seqs * hyper_weight.size,
+        [sds(split, BF16)],
+        scratch=[pltpu.VMEM((groups * TPG * tiles, LANES), F32)],
+        n_smem=1,
+        n_in=2,
+        flops=2 * groups * TPG * hyper_weight.size,
         nbytes=4 * hyper_weight.size,
-    )(task_of[:, None], task_codes, hyper_weight)[0]
-    adapt = lax.all_to_all(
-        sent.reshape(devices, seqs, tiles, LANES), ("dp", "mp"), 0, 0, tiled=True
+    )(task_share, task_codes, hyper_weight)[0]
+    got = lax.all_to_all(sent, "dp", 0, 0, tiled=True)
+    chosen = call(
+        functools.partial(choose_kernel, n_smem, members),
+        [sds((groups, seqs, tiles, LANES), BF16)] * members,
+        n_smem=n_smem,
+        n_in=members - n_smem + 1,
+        nbytes=8 * hyper_weight.size,
+    )(*member_slots, got)
+    near_pieces, rest, chosen = tied(near_pieces, rest, chosen)
+    adapt = [chosen[0]] + [xor_permute(chosen[k], "mp", k) for k in range(1, members)]
+    if not whole_tiles:
+        adapt = jnp.take(jnp.stack(adapt), jnp.arange(members) ^ me_mp, axis=0)
+        adapt = [adapt.transpose(2, 1, 0, 3, 4).reshape(seqs, rows, LANES)]
+
+    rest_held = direct(rest)
+    accs = []
+    if fits:
+        accs = frozen_call(
+            place, depth, half, [tokens, other_tokens], frozen_weight, [(near_pieces, near_rows)], []
+        )
+    later_slot, accs = tied(seq_slot, accs)
+    slots = lax.all_to_all(
+        jnp.broadcast_to(later_slot[None], (devices, seqs)), ("dp", "mp"), 0, 0, tiled=True
     )
-    if not whole_tiles:
-        adapt = adapt.transpose(1, 0, 2, 3).reshape(seqs, rows, LANES)
+    codes_t = call(
+        functools.partial(codes_kernel, members * seqs),
+        [sds((width_h, devices * seqs), BF16)],
+        n_smem=1,
+        n_in=2,
+    )(task_share, slots.reshape(-1, 1), task_codes)[0]
+    rest_held, accs, codes_t, adapt = tied(rest_held, accs, codes_t, adapt)
+    rest_pieces = forwarded(rest_held)
+
     low, b4, tok_t = call(
-        low_rank_kernel,
+        functools.partial(low_rank_kernel, len(adapt)),
         [
             sds((tok_dev, LANES), BF16),
             sds((seqs, LANES, KV), BF16),
             sds((D, tok_dev), BF16),
         ],
         scratch=[pltpu.VMEM((B_ROWS, LANES), F32), pltpu.VMEM((seqs, rows, LANES), BF16)],
-        n_in=2,
+        n_smem=1,
+        n_in=len(adapt) + 1,
         flops=4 * tokens.size * LANES * seqs,
         nbytes=4 * tokens.size + 4 * seqs * rows * LANES,
-    )(adapt, tokens)
-
-    if width % LANES == 0 and depth % LANES == 0:
-        mine, theirs = call(
-            functools.partial(frozen_kernel, members),
-            [sds((tok_dev, half), F32)] * 2,
-            n_smem=1,
-            n_in=3 + chips,
-            flops=4 * tokens.size * half,
-            nbytes=4 * tokens.size + 2 * D * half,
-        )(place, frozen_weight, tokens, other_tokens, *[held[m] for m in range(chips)])
+    )(place, *adapt, tokens)
+
+    if fits:
+        accs, low = tied(accs, low)
+        late = [(rest_pieces, rest_rows)]
+        theirs = frozen_call(place, depth, half, [other_tokens], None, late, accs[1:])[0]
+        mine = frozen_call(place, depth, half, [tokens], None, late, accs[:1])[0]
     else:
         own_half = lax.dynamic_slice_in_dim(frozen_weight, core * half, half, 1)
-        moved = jnp.stack([held[m].reshape(members - 1, depth, width) for m in range(chips)], 1)
-        moved = jnp.take(moved, jnp.arange(chips) ^ chip, axis=1)
-        moved = moved.transpose(0, 2, 1, 3).reshape(members - 1, depth, half)
-        blocks = jnp.concatenate([own_half[None], moved], axis=0)
+        order = jnp.arange(chips) ^ chip
+        found = {(0, 0): own_half[:mid], (0, mid): own_half[mid:]}
+        for pieces, segments in ((near_pieces, near_rows), (rest_pieces, rest_rows)):
+            joined = jnp.stack([jnp.concatenate(x, axis=0) for x in pieces])
+            joined = jnp.take(joined, order, axis=0).transpose(1, 0, 2).reshape(-1, half)
+            for at, (k, first, size) in enumerate(segments):
+                found[k, first] = joined[at * size : (at + 1) * size]
+        blocks = jnp.stack(
+            [jnp.concatenate([found[k, 0], found[k, mid]], axis=0) for k in range(members)]
+        )
         weight = jnp.take(blocks, jnp.arange(members) ^ me_mp, axis=0).reshape(D, half)
         mine = jnp.dot(tokens, weight, preferred_element_type=F32)
         theirs = jnp.dot(other_tokens, weight, preferred_element_type=F32)
@@ -311,18 +480,18 @@
 
     split = (devices, seqs, tiles, LANES)
     grads = call(
-        backward_kernel,
+        functools.partial(backward_kernel, loss_scale),
         [sds(split if whole_tiles else (seqs, rows, LANES), BF16)],
         scratch=[
             pltpu.VMEM((tok_dev, KV), F32),
             pltpu.VMEM((B_ROWS, LANES), F32),
             pltpu.VMEM((seqs, rows, LANES), BF16),
         ],
-        n_smem=2,
+        n_smem=4,
         n_in=6,
         flops=4 * tokens.size * LANES * seqs,
         nbytes=4 * tokens.size,
-    )(place, scale, mine, received, teacher, low, b4, tok_t)[0]
+    )(place, task_share, seq_slot, token_counts, mine, received, teacher, low, b4, tok_t)[0]
     if not whole_tiles:
         grads = grads.reshape(seqs, devices, tiles, LANES).transpose(1, 0, 2, 3)
     routed = lax.all_to_all(grads, ("dp", "mp"), 0, 0, tiled=True)

time: 127 us -> 117 us (0.921)
  waiting for transfers between devices: 56.9 us -> 18 us
  blocking collectives: 0 us -> 35.6 us
  starting transfers between devices: 36.9 us -> 22.5 us
  local copies, waits for them, and re-layouts: 6.49 us -> 12.3 us
  Pallas kernels: 21.6 us -> 24.7 us
    all_to_all x0 -> x2, blocking collectives: none -> 35.6 us  [the longest x1 22.4 us: shards(): routed = lax.all_to_all(grads, ('dp', 'mp'), 0, 0, tiled=True)]
    all_to_all x3 -> x1, waiting for transfers between devices: 31.2 us -> 0.01 us  [shards(): got = lax.all_to_all(sent, 'dp', 0, 0, tiled=True)]
    all_to_all x3 -> x1, starting transfers between devices: 25.8 us -> 4.52 us  [shards(): got = lax.all_to_all(sent, 'dp', 0, 0, tiled=True)]
    ppermute x9 -> x17, waiting for transfers between devices: 25.7 us -> 18 us  [xor_permute(): lax.ppermute(array, axis, [(i, i ^ mask) for i in range(lax.axis_size(axi...]
    ppermute x9 -> x17, starting transfers between devices: 11.1 us -> 18 us  [xor_permute(): lax.ppermute(array, axis, [(i, i ^ mask) for i in range(lax.axis_size(axi...]
    unnamed x14 -> x44, local copies, waits for them, and re-layouts: 1.49 us -> 7.83 us
    pallas_call x4 -> x9, Pallas kernels: 18.9 us -> 22 us  [the longest x3 9.21 us: frozen_call(): call(functools.partial(frozen_kernel, len(tokens), depth, weight is not N...]
    slice x2 -> x6, local copies, waits for them, and re-layouts: 0.85 us -> 3.87 us  [the longest x4 3.84 us: halves(): return [parts[0][:middle], parts[0][middle:]]]
  transfers between devices with their start and end apart: 12 -> 18, of which waited for: 6 -> 6; matrix products, arithmetic and copies ran while one was open for 6% -> 5% of each run, Pallas kernels for 11% -> 12%
where the time goes in v2:
time: 117 us; the launch traced here: 116 us
  blocking collectives  35.6 us (30%)
  Pallas kernels  24.7 us (21%)
  starting transfers between devices  22.5 us (19%)
  waiting for transfers between devices  18 us (15%)
  local copies, waits for them, and re-layouts  12.3 us (11%)
  other arithmetic  2.62 us (2%)
    all_to_all x1, blocking collectives, shards(): routed = lax.all_to_all(grads, ('dp', 'mp'), 0, 0, tiled=True)  22.4 us
    ppermute x17, starting transfers between devices, xor_permute(): lax.ppermute(array, axis, [(i, i ^ mask) for i in range(lax.axis_size(axi...  18 us
    ppermute x17, waiting for transfers between devices, xor_permute(): lax.ppermute(array, axis, [(i, i ^ mask) for i in range(lax.axis_size(axi...  18 us
    all_to_all x1, blocking collectives, shards(): lax.all_to_all(jnp.broadcast_to(later_slot[None], (devices, seqs)), ('dp'...  13.2 us
    pallas_call x3, Pallas kernels, frozen_call(): call(functools.partial(frozen_kernel, len(tokens), depth, weight is not N...  9.21 us
    unnamed x44, local copies, waits for them, and re-layouts  7.83 us
    all_to_all x1, starting transfers between devices, shards(): got = lax.all_to_all(sent, 'dp', 0, 0, tiled=True)  4.52 us
    pallas_call x1, Pallas kernels, shards(): call(functools.partial(backward_kernel, loss_scale), [sds(split if whole_...  4.47 us
  transfers between devices with their start and end apart: 18, of which 6 were waited for; matrix products, arithmetic and copies ran while one was open for 5% of the time, Pallas kernels for 12%

profile of v2, /device:TPU:1, one launch (start us, length us, event | category | flops | bytes accessed | tf_op | source)
XLA Modules:
  0.0 116.1 jit_solution(16065697743085881885)
XLA Ops:
  0.1 1.7 %copy-done.1 = bf16[1280,1024]{1,0:T(8,128)(2,1)S(1)} copy-done((bf16[1280,1024]{1,0:T(8,128)(2,1)S(1)}, bf16[1280,1024]{1,0:T(8,128)(2,1)}, u32[]{:S(2)}) %copy-start.1) | copy-done | bytes 2621464
  3.3 2.8 %collective-permute-start = (bf16[1296,128]{1,0:T(8,128)(2,1)S(1)}, bf16[1296,128]{1,0:T(8,128)(2,1)S(1)}, u32[]{:S(2)}, u32[]{:S(2)}) collective-permute-start(bf16[1296,128]{1,0:T(8,128)(2,1)S(1)} %get-tuple-element.43), channel_id=1, source_target_pairs={{0,1},{1,0},{2,3},{3,2},{4,5},{5,4},{6,7},{7,6},{8,9},{9,8},{10,11... | collective-permute-start | bytes 995336 | tf_op jit(solution)/shard_map/ppermute | solution.py:60
  6.1 2.3 %collective-permute-start.5 = (bf16[656,128]{1,0:T(8,128)(2,1)S(1)}, bf16[656,128]{1,0:T(8,128)(2,1)S(1)}, u32[]{:S(2)}, u32[]{:S(2)}) collective-permute-start(bf16[656,128]{1,0:T(8,128)(2,1)S(1)} %get-tuple-element.44), channel_id=1, source_target_pairs={{0,2},{1,3},{2,0},{3,1},{4,6},{5,7},{6,4},{7,5},{8,10},{9,11},{10,... | collective-permute-start | bytes 503816 | tf_op jit(solution)/shard_map/ppermute | solution.py:60
  8.5 2.0 %shard_map.83 = bf16[8,4,48,128]{3,2,1,0:T(8,128)(2,1)} custom-call(s32[8]{0:T(128)S(1)} %copy-done.16, bf16[16,128]{1,0:T(8,128)(2,1)S(1)} %copy-done.13, bf16[128,6144]{1,0:T(8,128)(2,1)S(1)} %copy-done.3), custom_call_target="tpu_custom_call" | custom-call | flops 50331648 | bytes 3145728 | tf_op jit(solution)/shard_map/pallas_call | solution.py:403
  10.4 4.5 %all-to-all-start = ((bf16[8,4,48,128]{3,2,1,0:T(8,128)(2,1)}), bf16[8,4,48,128]{3,2,1,0:T(8,128)(2,1)S(1)}, u32[]{:S(2)}, u32[]{:S(2)}) async-start(bf16[8,4,48,128]{3,2,1,0:T(8,128)(2,1)} %shard_map.83), calls=%async_computation | async-start | bytes 786432 | tf_op jit(solution)/shard_map/all_to_all | solution.py:412
  15.0 2.0 %collective-permute-done.5.refs_2_ = bf16[656,128]{1,0:T(8,128)(2,1)S(1)} collective-permute-done((bf16[656,128]{1,0:T(8,128)(2,1)S(1)}, bf16[656,128]{1,0:T(8,128)(2,1)S(1)}, u32[]{:S(2)}, u32[]{:S(2)}) %collective-permute-start.5) | collective-permute-done | bytes 167968 | tf_op jit(solution)/shard_map/ppermute | solution.py:60
  17.0 6.5 %collective-permute-done.6.refs_3_ = bf16[656,128]{1,0:T(8,128)(2,1)S(1)} collective-permute-done((bf16[656,128]{1,0:T(8,128)(2,1)S(1)}, bf16[656,128]{1,0:T(8,128)(2,1)S(1)}, u32[]{:S(2)}, u32[]{:S(2)}) %collective-permute-start.6) | collective-permute-done | bytes 167968 | tf_op jit(solution)/shard_map/ppermute | solution.py:60
  27.9 1.6 %shard_map.84 = (bf16[8,2,48,128]{3,2,1,0:T(8,128)(2,1)S(1)}, bf16[8,2,48,128]{3,2,1,0:T(8,128)(2,1)}, bf16[8,2,48,128]{3,2,1,0:T(8,128)(2,1)}, bf16[8,2,48,128]{3,2,1,0:T(8,128)(2,1)}) custom-call(s32[2]{0:T(128)S(1)} %copy-done.15, bf16[1296,128]{1,0:T(8,128)(2,1)S(1)} %collective-permute-done.refs_1_.refs_3_, ...), custom_call_target="tpu_custom_call" | custom-call | bytes 6291456 | tf_op jit(solution)/shard_map/pallas_call | solution.py:413
  29.5 2.6 %collective-permute-done.2.refs_5_ = bf16[1296,128]{1,0:T(8,128)(2,1)} collective-permute-done((bf16[1296,128]{1,0:T(8,128)(2,1)S(1)}, bf16[1296,128]{1,0:T(8,128)(2,1)}, u32[]{:S(2)}, u32[]{:S(2)}) %collective-permute-start.2) | collective-permute-done | bytes 331808 | tf_op jit(solution)/shard_map/ppermute | solution.py:60
  35.3 1.3 %collective-permute-start.3 = (bf16[640,128]{1,0:T(8,128)(2,1)S(1)}, bf16[640,128]{1,0:T(8,128)(2,1)S(1)}, u32[]{:S(2)}, u32[]{:S(2)}) collective-permute-start(bf16[640,128]{1,0:T(8,128)(2,1)S(1)} %slice.24), channel_id=1, source_target_pairs={{0,16},{4,20},{8,24},{12,28},{16,0},{20,4},{24,8},{28,12},{1,17},{... | collective-permute-start | bytes 491528 | tf_op jit(solution)/shard_map/ppermute | solution.py:60
  37.7 2.1 %collective-permute-done.3.refs_6_ = bf16[640,128]{1,0:T(8,128)(2,1)S(1)} collective-permute-done((bf16[640,128]{1,0:T(8,128)(2,1)S(1)}, bf16[640,128]{1,0:T(8,128)(2,1)S(1)}, u32[]{:S(2)}, u32[]{:S(2)}) %collective-permute-start.3) | collective-permute-done | bytes 163872 | tf_op jit(solution)/shard_map/ppermute | solution.py:60
  41.3 1.3 %collective-permute-start.12 = (bf16[8,2,48,128]{3,2,1,0:T(8,128)(2,1)}, bf16[8,2,48,128]{3,2,1,0:T(8,128)(2,1)}, u32[]{:S(2)}, u32[]{:S(2)}) collective-permute-start(bf16[8,2,48,128]{3,2,1,0:T(8,128)(2,1)} %get-tuple-element.63), channel_id=1, source_target_pairs={{0,2},{1,3},{2,0},{3,1},{4,6},{5,7},{6,4},{7,5},{8,10},{9,11},{10,... | collective-permute-start | bytes 589832 | tf_op jit(solution)/shard_map/ppermute | solution.py:60
  42.7 2.2 %collective-permute-start.13 = (bf16[8,2,48,128]{3,2,1,0:T(8,128)(2,1)}, bf16[8,2,48,128]{3,2,1,0:T(8,128)(2,1)}, u32[]{:S(2)}, u32[]{:S(2)}) collective-permute-start(bf16[8,2,48,128]{3,2,1,0:T(8,128)(2,1)} %get-tuple-element.64), channel_id=1, source_target_pairs={{0,3},{1,2},{2,1},{3,0},{4,7},{5,6},{6,5},{7,4},{8,11},{9,10},{10,... | collective-permute-start | bytes 589832 | tf_op jit(solution)/shard_map/ppermute | solution.py:60
  44.9 1.7 %copy-done.2 = bf16[1280,1024]{1,0:T(8,128)(2,1)S(1)} copy-done((bf16[1280,1024]{1,0:T(8,128)(2,1)S(1)}, bf16[1280,1024]{1,0:T(8,128)(2,1)}, u32[]{:S(2)}) %copy-start.2) | copy-done | bytes 2621464
  47.6 3.7 %shard_map.85 = (f32[256,512]{1,0:T(8,128)S(1)}, f32[256,512]{1,0:T(8,128)S(1)}) custom-call(s32[4]{0:T(128)S(1)} %pad_add_fusion.place_ref, bf16[256,5120]{1,0:T(8,128)(2,1)S(1)} %copy-done, bf16[256,5120]{1,0:T(8,128)(2,1)} %collective-permute-done.10.refs_1_.refs_0_, bf16[1280,1024]{1,0:T(8,128)(2,1)S(1)} %copy-done.2, bf16[1296,128]{1,0:T(8,128)(2,1)S(1)} %copy-done.5, ...), custom_call_target="tpu_custom_call" | custom-call | flops 1342177280 | bytes 3670016 | tf_op jit(solution)/shard_map/pallas_call | solution.py:232
  52.9 13.2 %all_to_all.16 = s32[32,1,2]{2,1,0:T(1,128)S(1)} all-to-all(s32[32,1,2]{2,1,0:T(1,128)S(1)} %broadcast_in_dim.2), channel_id=1, replica_groups=mesh['dp'=8,'mp'=4] {'dp','mp'}, dimensions={0} | all-to-all | bytes 512 | tf_op jit(solution)/shard_map/all_to_all | solution.py:433
  71.0 3.2 %shard_map.87 = (bf16[256,128]{1,0:T(8,128)(2,1)S(1)}, bf16[2,128,1024]{2,1,0:T(8,128)(2,1)S(1)}, bf16[5120,256]{1,0:T(8,128)(2,1)S(1)}) custom-call(s32[4]{0:T(128)S(1)} %pad_add_fusion.place_ref, bf16[8,2,48,128]{3,2,1,0:T(8,128)(2,1)S(1)} %copy-done.19, bf16[8,2,48,128]{3,2,1,0:T(8,128)(2,1)} %collective-permute-done.11.refs_1_, ...), custom_call_target="tpu_custom_call" | custom-call | flops 1342177280 | bytes 6815744 | tf_op jit(solution)/shard_map/pallas_call | solution.py:445
  74.2 3.7 %collective-permute-done.14.refs_4_ = bf16[1280,128]{1,0:T(8,128)(2,1)S(1)} collective-permute-done((bf16[1280,128]{1,0:T(8,128)(2,1)S(1)}, bf16[1280,128]{1,0:T(8,128)(2,1)S(1)}, u32[]{:S(2)}, u32[]{:S(2)}) %collective-permute-start.14) | collective-permute-done | bytes 327712 | tf_op jit(solution)/shard_map/ppermute | solution.py:60
  79.0 3.1 %shard_map.89 = f32[256,512]{1,0:T(8,128)S(1)} custom-call(s32[4]{0:T(128)S(1)} %pad_add_fusion.place_ref, bf16[256,5120]{1,0:T(8,128)(2,1)} %collective-permute-done.10.refs_1_.refs_0_, bf16[2560,128]{1,0:T(8,128)(2,1)S(1)} %pad_maximum_fusion.refs_1_, bf16[2560,128]{1,0:T(8,128)(2,1)} %collective-permute-done.8.refs_2_, ...), custom_call_target="tpu_custom_call" | custom-call | flops 671088640 | bytes 3145728 | tf_op jit(solution)/shard_map/pallas_call | solution.py:232
  82.1 2.0 %collective-permute-start.16 = (f32[256,512]{1,0:T(8,128)S(1)}, f32[256,512]{1,0:T(8,128)S(1)}, u32[]{:S(2)}, u32[]{:S(2)}) collective-permute-start(f32[256,512]{1,0:T(8,128)S(1)} %shard_map.89), channel_id=1, source_target_pairs={{0,4},{4,0},{8,12},{12,8},{16,20},{20,16},{24,28},{28,24},{1,5},{5... | collective-permute-start | bytes 1572872 | tf_op jit(solution)/shard_map/ppermute | solution.py:60
  84.1 2.4 %shard_map.88.mine_ref = f32[256,512]{1,0:T(8,128)S(1)} custom-call(s32[4]{0:T(128)S(1)} %pad_add_fusion.place_ref, bf16[256,5120]{1,0:T(8,128)(2,1)S(1)} %copy-done, bf16[2560,128]{1,0:T(8,128)(2,1)S(1)} %pad_maximum_fusion.refs_1_, bf16[2560,128]{1,0:T(8,128)(2,1)} %collective-permute-done.8.refs_2_, bf16[2560,128]{1,0:T(8,128)(2,1)} %collective-permute-done.9.refs_3_, ...), custom_call_target="tpu_custom_call" | custom-call | flops 671088640 | bytes 3145728 | tf_op jit(solution)/shard_map/pallas_call | solution.py:232
  86.5 4.5 %shard_map.90 = bf16[32,2,48,128]{3,2,1,0:T(8,128)(2,1)S(1)} custom-call(s32[4]{0:T(128)S(1)} %pad_add_fusion.place_ref, s32[8]{0:T(128)S(1)} %copy-done.16, s32[2]{0:T(128)S(1)} %copy-done.15, s32[16]{0:T(128)S(1)} %copy-done.17, f32[256,512]{1,0:T(8,128)S(1)} %shard_map.88.mine_ref, f32[256,512]{1,0:T(8,128)S(1)} %collective-permute-done.16.theirs_ref, ...), custom_call_target="tpu_custom_call" | custom-call | flops 1342177280 | bytes 5242880 | tf_op jit(solution)/shard_map/pallas_call | solution.py:482
  91.0 22.4 %all_to_all.17.grads_ref = bf16[32,2,48,128]{3,2,1,0:T(8,128)(2,1)S(1)} all-to-all(bf16[32,2,48,128]{3,2,1,0:T(8,128)(2,1)S(1)} %shard_map.90), channel_id=1, replica_groups=mesh['dp'=8,'mp'=4] {'dp','mp'}, dimensions={0} | all-to-all | bytes 1572864 | tf_op jit(solution)/shard_map/all_to_all | solution.py:497
  113.4 2.7 %shard_map.91 = f32[128,6144]{1,0:T(8,128)} custom-call(bf16[128,64]{1,0:T(8,128)(2,1)S(1)} %shard_map.86.codes_t_ref, bf16[32,2,48,128]{3,2,1,0:T(8,128)(2,1)S(1)} %all_to_all.17.grads_ref), custom_call_target="tpu_custom_call" | custom-call | tf_op jit(solution)/shard_map/pallas_call | solution.py:499
  (81 shorter events, 20.2 us)
Async XLA Ops:
  0.0 42.6 %collective-permute-start.10 = (bf16[256,5120]{1,0:T(8,128)(2,1)}, bf16[256,5120]{1,0:T(8,128)(2,1)}, u32[]{:S(2)}, u32[]{:S(2)}) collective-permute-start(bf16[256,5120]{1,0:T(8,128)(2,1)} %refs_0_.5), channel_id=1, source_target_pairs={{0,4},{4,0},{8,12},{12,8},{16,20},{20,16},{24,28},{28,24},{1,5},{5... | collective-permute-start | bytes 7864328 | tf_op jit(solution)/shard_map/ppermute | solution.py:60
  3.3 20.2 %collective-permute-start = (bf16[1296,128]{1,0:T(8,128)(2,1)S(1)}, bf16[1296,128]{1,0:T(8,128)(2,1)S(1)}, u32[]{:S(2)}, u32[]{:S(2)}) collective-permute-start(bf16[1296,128]{1,0:T(8,128)(2,1)S(1)} %get-tuple-element.43), channel_id=1, source_target_pairs={{0,1},{1,0},{2,3},{3,2},{4,5},{5,4},{6,7},{7,6},{8,9},{9,8},{10,11... | collective-permute-start | bytes 995336 | tf_op jit(solution)/shard_map/ppermute | solution.py:60
  6.1 10.8 %collective-permute-start.5 = (bf16[656,128]{1,0:T(8,128)(2,1)S(1)}, bf16[656,128]{1,0:T(8,128)(2,1)S(1)}, u32[]{:S(2)}, u32[]{:S(2)}) collective-permute-start(bf16[656,128]{1,0:T(8,128)(2,1)S(1)} %get-tuple-element.44), channel_id=1, source_target_pairs={{0,2},{1,3},{2,0},{3,1},{4,6},{5,7},{6,4},{7,5},{8,10},{9,11},{10,... | collective-permute-start | bytes 503816 | tf_op jit(solution)/shard_map/ppermute | solution.py:60
  8.4 18.4 %copy-start.15 = (s32[2]{0:T(128)S(1)}, s32[2]{0:T(128)}, u32[]{:S(2)}) copy-start(s32[2]{0:T(128)} %slot_ref.3) | copy-start | bytes 28
  8.4 15.1 %collective-permute-start.6 = (bf16[656,128]{1,0:T(8,128)(2,1)S(1)}, bf16[656,128]{1,0:T(8,128)(2,1)S(1)}, u32[]{:S(2)}, u32[]{:S(2)}) collective-permute-start(bf16[656,128]{1,0:T(8,128)(2,1)S(1)} %get-tuple-element.45), channel_id=1, source_target_pairs={{0,3},{1,2},{2,1},{3,0},{4,7},{5,6},{6,5},{7,4},{8,11},{9,10},{10,... | collective-permute-start | bytes 503816 | tf_op jit(solution)/shard_map/ppermute | solution.py:60
  10.4 16.4 %all-to-all-start = ((bf16[8,4,48,128]{3,2,1,0:T(8,128)(2,1)}), bf16[8,4,48,128]{3,2,1,0:T(8,128)(2,1)S(1)}, u32[]{:S(2)}, u32[]{:S(2)}) async-start(bf16[8,4,48,128]{3,2,1,0:T(8,128)(2,1)} %shard_map.83), calls=%async_computation | async-start | bytes 786432 | tf_op jit(solution)/shard_map/all_to_all | solution.py:412
  23.5 13.1 %copy-start.4 = (bf16[1296,128]{1,0:T(8,128)(2,1)}, bf16[1296,128]{1,0:T(8,128)(2,1)S(1)}, u32[]{:S(2)}) copy-start(bf16[1296,128]{1,0:T(8,128)(2,1)S(1)} %collective-permute-done.refs_1_.refs_3_) | copy-start | bytes 995332
  23.5 8.6 %collective-permute-start.2 = (bf16[1296,128]{1,0:T(8,128)(2,1)S(1)}, bf16[1296,128]{1,0:T(8,128)(2,1)}, u32[]{:S(2)}, u32[]{:S(2)}) collective-permute-start(bf16[1296,128]{1,0:T(8,128)(2,1)S(1)} %collective-permute-done.refs_1_.refs_3_), channel_id=1, source_target_pairs={{0,16},{4,20},{8,24},{12,28},{16,0},{20,4},{24,8},{28,12},{1,17},{... | collective-permute-start | bytes 995336 | tf_op jit(solution)/shard_map/ppermute | solution.py:60
  24.8 9.5 %collective-permute-start.1 = (bf16[1296,128]{1,0:T(8,128)(2,1)S(1)}, bf16[1296,128]{1,0:T(8,128)(2,1)}, u32[]{:S(2)}, u32[]{:S(2)}) collective-permute-start(bf16[1296,128]{1,0:T(8,128)(2,1)S(1)} %collective-permute-done.refs_1_.refs_3_), channel_id=1, source_target_pairs={{0,8},{4,12},{8,0},{12,4},{16,24},{20,28},{24,16},{28,20},{1,9},{5... | collective-permute-start | bytes 995336 | tf_op jit(solution)/shard_map/ppermute | solution.py:60
  26.8 18.0 %copy-start = (bf16[256,5120]{1,0:T(8,128)(2,1)S(1)}, bf16[256,5120]{1,0:T(8,128)(2,1)}, u32[]{:S(2)}) copy-start(bf16[256,5120]{1,0:T(8,128)(2,1)} %refs_0_.5) | copy-start | bytes 7864324
  26.8 9.8 %collective-permute-start.7 = (bf16[1280,128]{1,0:T(8,128)(2,1)}, bf16[1280,128]{1,0:T(8,128)(2,1)}, u32[]{:S(2)}, u32[]{:S(2)}) collective-permute-start(bf16[1280,128]{1,0:T(8,128)(2,1)} %pad_maximum_fusion.1), channel_id=1, source_target_pairs={{0,1},{1,0},{2,3},{3,2},{4,5},{5,4},{6,7},{7,6},{8,9},{9,8},{10,11... | collective-permute-start | bytes 983048 | tf_op jit(solution)/shard_map/ppermute | solution.py:60
  29.5 13.1 %copy-start.18 = (bf16[8,2,48,128]{3,2,1,0:T(8,128)(2,1)}, bf16[8,2,48,128]{3,2,1,0:T(8,128)(2,1)S(1)}, u32[]{:S(2)}) copy-start(bf16[8,2,48,128]{3,2,1,0:T(8,128)(2,1)S(1)} %get-tuple-element.71.refs_0_) | copy-start | bytes 589828
  33.1 6.7 %collective-permute-start.4 = (bf16[656,128]{1,0:T(8,128)(2,1)S(1)}, bf16[656,128]{1,0:T(8,128)(2,1)S(1)}, u32[]{:S(2)}, u32[]{:S(2)}) collective-permute-start(bf16[656,128]{1,0:T(8,128)(2,1)S(1)} %slice.25), channel_id=1, source_target_pairs={{0,8},{4,12},{8,0},{12,4},{16,24},{20,28},{24,16},{28,20},{1,9},{5... | collective-permute-start | bytes 503816 | tf_op jit(solution)/shard_map/ppermute | solution.py:60
  35.3 4.5 %collective-permute-start.3 = (bf16[640,128]{1,0:T(8,128)(2,1)S(1)}, bf16[640,128]{1,0:T(8,128)(2,1)S(1)}, u32[]{:S(2)}, u32[]{:S(2)}) collective-permute-start(bf16[640,128]{1,0:T(8,128)(2,1)S(1)} %slice.24), channel_id=1, source_target_pairs={{0,16},{4,20},{8,24},{12,28},{16,0},{20,4},{24,8},{28,12},{1,17},{... | collective-permute-start | bytes 491528 | tf_op jit(solution)/shard_map/ppermute | solution.py:60
  39.8 28.5 %collective-permute-start.8 = (bf16[2560,128]{1,0:T(8,128)(2,1)S(1)}, bf16[2560,128]{1,0:T(8,128)(2,1)}, u32[]{:S(2)}, u32[]{:S(2)}) collective-permute-start(bf16[2560,128]{1,0:T(8,128)(2,1)S(1)} %pad_maximum_fusion.refs_1_), channel_id=1, source_target_pairs={{0,8},{4,12},{8,0},{12,4},{16,24},{20,28},{24,16},{28,20},{1,9},{5... | collective-permute-start | bytes 1966088 | tf_op jit(solution)/shard_map/ppermute | solution.py:60
  40.1 28.2 %collective-permute-start.9 = (bf16[2560,128]{1,0:T(8,128)(2,1)S(1)}, bf16[2560,128]{1,0:T(8,128)(2,1)}, u32[]{:S(2)}, u32[]{:S(2)}) collective-permute-start(bf16[2560,128]{1,0:T(8,128)(2,1)S(1)} %pad_maximum_fusion.refs_1_), channel_id=1, source_target_pairs={{0,16},{4,20},{8,24},{12,28},{16,0},{20,4},{24,8},{28,12},{1,17},{... | collective-permute-start | bytes 1966088 | tf_op jit(solution)/shard_map/ppermute | solution.py:60
  41.3 27.0 %collective-permute-start.11 = (bf16[8,2,48,128]{3,2,1,0:T(8,128)(2,1)}, bf16[8,2,48,128]{3,2,1,0:T(8,128)(2,1)}, u32[]{:S(2)}, u32[]{:S(2)}) collective-permute-start(bf16[8,2,48,128]{3,2,1,0:T(8,128)(2,1)} %get-tuple-element.62), channel_id=1, source_target_pairs={{0,1},{1,0},{2,3},{3,2},{4,5},{5,4},{6,7},{7,6},{8,9},{9,8},{10,11... | collective-permute-start | bytes 589832 | tf_op jit(solution)/shard_map/ppermute | solution.py:60
  41.3 27.0 %collective-permute-start.12 = (bf16[8,2,48,128]{3,2,1,0:T(8,128)(2,1)}, bf16[8,2,48,128]{3,2,1,0:T(8,128)(2,1)}, u32[]{:S(2)}, u32[]{:S(2)}) collective-permute-start(bf16[8,2,48,128]{3,2,1,0:T(8,128)(2,1)} %get-tuple-element.63), channel_id=1, source_target_pairs={{0,2},{1,3},{2,0},{3,1},{4,6},{5,7},{6,4},{7,5},{8,10},{9,11},{10,... | collective-permute-start | bytes 589832 | tf_op jit(solution)/shard_map/ppermute | solution.py:60
  42.7 25.7 %collective-permute-start.13 = (bf16[8,2,48,128]{3,2,1,0:T(8,128)(2,1)}, bf16[8,2,48,128]{3,2,1,0:T(8,128)(2,1)}, u32[]{:S(2)}, u32[]{:S(2)}) collective-permute-start(bf16[8,2,48,128]{3,2,1,0:T(8,128)(2,1)} %get-tuple-element.64), channel_id=1, source_target_pairs={{0,3},{1,2},{2,1},{3,0},{4,7},{5,6},{6,5},{7,4},{8,11},{9,10},{10,... | collective-permute-start | bytes 589832 | tf_op jit(solution)/shard_map/ppermute | solution.py:60
  47.6 23.4 %copy-start.19 = (bf16[8,2,48,128]{3,2,1,0:T(8,128)(2,1)S(1)}, bf16[8,2,48,128]{3,2,1,0:T(8,128)(2,1)}, u32[]{:S(2)}) copy-start(bf16[8,2,48,128]{3,2,1,0:T(8,128)(2,1)} %copy-done.18) | copy-start | bytes 589828
  69.3 8.6 %collective-permute-start.14 = (bf16[1280,128]{1,0:T(8,128)(2,1)S(1)}, bf16[1280,128]{1,0:T(8,128)(2,1)S(1)}, u32[]{:S(2)}, u32[]{:S(2)}) collective-permute-start(bf16[1280,128]{1,0:T(8,128)(2,1)S(1)} %slice.22), channel_id=1, source_target_pairs={{0,16},{4,20},{8,24},{12,28},{16,0},{20,4},{24,8},{28,12},{1,17},{... | collective-permute-start | bytes 983048 | tf_op jit(solution)/shard_map/ppermute | solution.py:60
  70.7 8.2 %collective-permute-start.15 = (bf16[1280,128]{1,0:T(8,128)(2,1)S(1)}, bf16[1280,128]{1,0:T(8,128)(2,1)S(1)}, u32[]{:S(2)}, u32[]{:S(2)}) collective-permute-start(bf16[1280,128]{1,0:T(8,128)(2,1)S(1)} %slice.23), channel_id=1, source_target_pairs={{0,8},{4,12},{8,0},{12,4},{16,24},{20,28},{24,16},{28,20},{1,9},{5... | collective-permute-start | bytes 983048 | tf_op jit(solution)/shard_map/ppermute | solution.py:60
  74.2 9.9 %copy-start.10 = (f32[256,512]{1,0:T(8,128)S(1)}, f32[256,512]{1,0:T(8,128)}, u32[]{:S(2)}) copy-start(f32[256,512]{1,0:T(8,128)} %copy-done.9) | copy-start | bytes 1572868
  82.1 4.4 %collective-permute-start.16 = (f32[256,512]{1,0:T(8,128)S(1)}, f32[256,512]{1,0:T(8,128)S(1)}, u32[]{:S(2)}, u32[]{:S(2)}) collective-permute-start(f32[256,512]{1,0:T(8,128)S(1)} %shard_map.89), channel_id=1, source_target_pairs={{0,4},{4,0},{8,12},{12,8},{16,20},{20,16},{24,28},{28,24},{1,5},{5... | collective-permute-start | bytes 1572872 | tf_op jit(solution)/shard_map/ppermute | solution.py:60
  (16 other events, 61.9 us)

commit v3 on v2

v3 whole, which is shorter than its diff:
```python
import functools
import math

import jax
import jax.numpy as jnp
from jax import lax
from jax.experimental import pallas as pl
from jax.experimental.pallas import tpu as pltpu
from jax.sharding import PartitionSpec as P

D = 5120
KV = 1024
R = 32
TPG = 4
SEQ_LEN = 128
LANES = 128
PACK = LANES // R
SLOT_ROWS = 16
A_ROWS = D * R // LANES
B_ROWS = R * KV // LANES
COL_TILES = KV // LANES
BLOCK_D = 512
BLOCK_Q = BLOCK_D // PACK
SHRINK = 1.0 / math.sqrt(D)
RANK_SCALE = 1.0 / math.sqrt(R)
F32 = jnp.float32
BF16 = jnp.bfloat16
VMEM_LIMIT = 16 * 1024 * 1024
ALL_VMEM = 56 * 1024 * 1024


def dot(a, b):
    return jnp.dot(a, b, preferred_element_type=F32)


def dot_nt(a, b):
    return lax.dot_general(a, b, (((1,), (1,)), ((), ())), preferred_element_type=F32)


def call(body, outs, scratch=(), n_smem=0, n_in=0, flops=0, nbytes=0, **kw):
    specs = [pl.BlockSpec(memory_space=pltpu.SMEM)] * n_smem
    specs += [pl.BlockSpec(memory_space=pltpu.VMEM)] * n_in
    out_specs = [pl.BlockSpec(memory_space=pltpu.VMEM)] * len(outs)
    return pl.pallas_call(
        body,
        out_shape=list(outs),
        in_specs=specs,
        out_specs=out_specs,
        scratch_shapes=list(scratch),
        compiler_params=pltpu.CompilerParams(vmem_limit_bytes=VMEM_LIMIT),
        cost_estimate=pl.CostEstimate(flops=flops, bytes_accessed=nbytes, transcendentals=0),
        **kw,
    )


def sds(shape, dtype):
    return jax.ShapeDtypeStruct(shape, dtype)


def xor_permute(array, axis, mask):
    return lax.ppermute(array, axis, [(i, i ^ mask) for i in range(lax.axis_size(axis))])


def chunk_kernel(place_ref, slot_hbm, weight_ref, near_ref, top_ref, bottom_ref, slot_ref, sems):
    depth = weight_ref.shape[0]
    width = near_ref.shape[1]
    mid = depth // 2
    half = weight_ref.shape[1] // 2
    at = pl.ds(pl.multiple_of(place_ref[1] * half + place_ref[2] * width, LANES), width)
    copies = [
        pltpu.make_async_copy(
            weight_ref.at[pl.ds(first, size), at], out.at[pl.ds(0, size), :], sems.at[i]
        )
        for i, (first, size, out) in enumerate(
            [(0, depth, near_ref), (0, mid, top_ref), (mid, mid, bottom_ref)]
        )
    ]
    for copy in copies:
        copy.start()
    slot_copy = pltpu.make_async_copy(slot_hbm, slot_ref, sems.at[3])
    slot_copy.start()
    slot_copy.wait()
    note = slot_note(slot_ref, width)
    near_ref[depth:, :] = note
    top_ref[mid:, :] = note
    bottom_ref[mid:, :] = note
    for copy in copies:
        copy.wait()


def slot_note(slot_ref, width):
    row = lax.broadcasted_iota(jnp.int32, (SLOT_ROWS, width), 0)
    note = jnp.zeros((SLOT_ROWS, width), jnp.int32)
    for s in range(slot_ref.shape[0]):
        note = jnp.where(row == s, slot_ref[s], note)
    return note.astype(F32).astype(BF16)


def adapters_kernel(tiles, share_ref, slot_ref, codes_ref, weight_ref, out_ref, scr):
    groups = out_ref.shape[0]
    rows = groups * TPG
    tasks = codes_ref.shape[0]
    row = lax.broadcasted_iota(jnp.int32, (rows, 1), 0)
    group, task = row // TPG, row % TPG
    live = jnp.zeros((rows, 1), jnp.int32)
    for g in range(groups):
        task = task + jnp.where(group > g, share_ref[g], 0)
        live = live + jnp.where(group == g, share_ref[g], 0)
    task = jnp.where(row % TPG < live, task, -1)
    pick = (task == lax.broadcasted_iota(jnp.int32, (rows, tasks), 1)).astype(BF16)
    chosen = dot(pick, codes_ref[...]).astype(BF16)
    for k in range(tiles):
        part = dot(chosen, weight_ref[:, k * LANES : (k + 1) * LANES])
        scr[pl.ds(k, rows, stride=tiles), :] = part
    note = slot_note(slot_ref, LANES)
    for g in range(groups):
        at = g * TPG * tiles
        out_ref[g, : TPG * tiles, :] = scr[at : at + TPG * tiles, :].astype(BF16)
        out_ref[g, TPG * tiles :, :] = note


def choose_kernel(tiles, n, slot_ref, *refs):
    note_refs, got_ref, out_refs = refs[: n - 1], refs[n - 1], refs[n:]
    seqs = slot_ref.shape[0]
    groups = got_ref.shape[0]
    row = lax.broadcasted_iota(jnp.int32, (groups * seqs, LANES), 0)
    table = jnp.zeros((groups * seqs, LANES), F32)
    for g in range(groups):
        notes = got_ref[g, TPG * tiles :, :].astype(F32)
        for s in range(seqs):
            table = jnp.where(row == g * seqs + s, notes[s : s + 1, :], table)
    table = table.astype(BF16)
    for k, out in enumerate(out_refs):
        if k > 0:
            note_ref = note_refs[k - 1]
            notes = note_ref[note_ref.shape[0] - SLOT_ROWS :, :].astype(F32).astype(jnp.int32)
        for s in range(seqs):
            slot = slot_ref[s] if k == 0 else jnp.max(notes[s : s + 1, :])
            rows = pl.ds(pl.multiple_of(slot * tiles, 16), tiles)
            for g in range(groups):
                at = (g * seqs + s) * tiles
                out[at : at + tiles, :] = got_ref[g, rows, :]
        out[groups * seqs * tiles :, :] = table


def low_rank_kernel(
    tiles, place_ref, share_ref, codes_ref, adapt_refs, tokens_ref,
    low_ref, b4_ref, tok_t_ref, codes_t_ref, scr, held, table,
):
    n = len(adapt_refs)
    seqs = b4_ref.shape[0]
    groups = share_ref.shape[0]
    per_part = groups * seqs
    for k, part in enumerate(adapt_refs):
        table[k * per_part : (k + 1) * per_part, :] = part[per_part * tiles :, :].astype(F32)
        for g in range(groups):
            at = pl.multiple_of((g * n + (place_ref[0] ^ k)) * tiles, 16)
            for s in range(seqs):
                first = (g * seqs + s) * tiles
                held[s, pl.ds(at, tiles), :] = part[first : first + tiles, :]
    rows, tasks = table.shape[0], codes_ref.shape[0]
    task = table[:, :1].astype(jnp.int32)
    group = lax.broadcasted_iota(jnp.int32, (rows, 1), 0) % per_part // seqs
    for g in range(groups - 1):
        task = task + jnp.where(group > g, share_ref[g], 0)
    pick = (task == lax.broadcasted_iota(jnp.int32, (rows, tasks), 1)).astype(BF16)
    codes = dot(pick, codes_ref[...]).astype(BF16)
    at = lax.broadcasted_iota(jnp.int32, (rows, rows), 1)
    source = at % per_part // seqs * n + (place_ref[0] ^ (at // per_part))
    order = source * seqs + at % seqs == lax.broadcasted_iota(jnp.int32, (rows, rows), 0)
    codes_t_ref[...] = dot(order.astype(BF16), codes).T.astype(BF16)
    low_rank_body(held, tokens_ref, low_ref, b4_ref, tok_t_ref, scr)


def low_rank_body(adapt_ref, tokens_ref, low_ref, b4_ref, tok_t_ref, scr):
    seqs = b4_ref.shape[0]
    lane = lax.broadcasted_iota(jnp.int32, (BLOCK_D, LANES * seqs), 1)
    row = lax.broadcasted_iota(jnp.int32, (BLOCK_D, LANES * seqs), 0)
    keep = (lane % LANES) // R == row % PACK
    spread = (
        lax.broadcasted_iota(jnp.int32, (BLOCK_D, BLOCK_Q), 0) // PACK
        == lax.broadcasted_iota(jnp.int32, (BLOCK_D, BLOCK_Q), 1)
    ).astype(BF16)
    to = lax.broadcasted_iota(jnp.int32, (BLOCK_D, BLOCK_D), 0)
    sort = (
        to % BLOCK_Q * PACK + to // BLOCK_Q
        == lax.broadcasted_iota(jnp.int32, (BLOCK_D, BLOCK_D), 1)
    ).astype(BF16)
    acc = jnp.zeros((tokens_ref.shape[0], LANES * seqs), F32)
    for b in range(D // BLOCK_D):
        cols = slice(b * BLOCK_D, (b + 1) * BLOCK_D)
        part = jnp.concatenate(
            [adapt_ref[s, b * BLOCK_Q : (b + 1) * BLOCK_Q, :] for s in range(seqs)], axis=1
        )
        wide = jnp.where(keep, dot(spread, part), 0.0).astype(BF16)
        block = tokens_ref[:, cols]
        acc = acc + dot(block, wide)
        turned = dot_nt(sort, block).astype(BF16)
        for j in range(PACK):
            tok_t_ref[
                b * BLOCK_Q : (b + 1) * BLOCK_Q, j * block.shape[0] : (j + 1) * block.shape[0]
            ] = turned[j * BLOCK_Q : (j + 1) * BLOCK_Q, :]
    first = lax.broadcasted_iota(jnp.int32, (SEQ_LEN, LANES), 1) < R
    for s in range(seqs):
        z = acc[s * SEQ_LEN : (s + 1) * SEQ_LEN, s * LANES : (s + 1) * LANES]
        total = z
        for j in range(1, PACK):
            total = total + pltpu.roll(z, j * R, 1)
        low_ref[s * SEQ_LEN : (s + 1) * SEQ_LEN, :] = jnp.where(first, total * SHRINK, 0.0).astype(
            BF16
        )
        scr[...] = adapt_ref[s, A_ROWS:, :].astype(F32)
        for c in range(COL_TILES):
            piece = scr[pl.ds(c, R, stride=COL_TILES), :].astype(BF16)
            for j in range(PACK):
                b4_ref[s, j * R : (j + 1) * R, c * LANES : (c + 1) * LANES] = piece


def frozen_kernel(n_tok, depth, own, layout, has_acc, place_ref, *refs):
    refs = iter(refs)
    token_refs = [next(refs) for _ in range(n_tok)]
    weight_ref = next(refs) if own else None
    sets = [
        ([(m, next(refs)) for m in masks], segments) for masks, segments in layout
    ]
    accs = [next(refs) for _ in range(n_tok)] if has_acc else [None] * n_tok
    outs = list(refs)
    me, core, chip = place_ref[0], place_ref[1], place_ref[2]
    width = sets[0][0][0][1].shape[1]

    def cols(k, first, size):
        return pl.ds(pl.multiple_of((me ^ k) * depth + first, LANES), size)

    for tok, acc, out in zip(token_refs, accs, outs):
        if own:
            half = out.shape[1]
            block = weight_ref[:, pl.ds(pl.multiple_of(core * half, LANES), half)]
            out[...] = dot(tok[:, cols(0, 0, depth)], block)
        else:
            out[...] = acc[...]
        for pieces, segments in sets:
            for first_chip in range(0, len(pieces), 2):
                pair = pieces[first_chip : first_chip + 2]
                part = None
                for k, first, size, row in segments:
                    right = jnp.concatenate([x[row : row + size, :] for _, x in pair], axis=1)
                    term = dot(tok[:, cols(k, first, size)], right)
                    part = term if part is None else part + term
                for at, (mask, _) in enumerate(pair):
                    where = pl.ds(pl.multiple_of((chip ^ mask) * width, LANES), width)
                    out[:, where] += part[:, at * width : (at + 1) * width]


def frozen_layout(sets):
    layout = [([m for m, _ in pieces], segments) for pieces, segments in sets]
    return layout, [x for pieces, _ in sets for _, x in pieces]


def frozen_call(place, depth, half, tokens, weight, sets, accs):
    rows = tokens[0].shape[0]
    layout, flat = frozen_layout(sets)
    size = 2 * rows * sum(x.size for x in flat) + (0 if weight is None else 2 * rows * depth * half)
    weights = [] if weight is None else [weight]
    return call(
        functools.partial(
            frozen_kernel, len(tokens), depth, weight is not None, layout, bool(accs)
        ),
        [sds((rows, half), F32)] * len(tokens),
        n_smem=1,
        n_in=len(tokens) + len(weights) + len(flat) + len(accs),
        flops=size * len(tokens),
        nbytes=2 * sum(x.size for x in flat) + 4 * rows * half * len(tokens),
    )(place, *tokens, *weights, *flat, *accs)


def backward_kernel(
    loss_scale, place_ref, share_ref, slot_ref, counts_ref, mine_ref, theirs_ref, teacher_ref, low_ref, b4_ref, tok_t_ref, out_ref,
    values, spaced, grads,
):
    seqs = b4_ref.shape[0]
    half = mine_ref.shape[1]
    core, group = place_ref[1], place_ref[3]
    n_tasks = counts_ref.shape[0]
    first_task = jnp.int32(0)
    for g in range(share_ref.shape[0]):
        first_task = first_task + jnp.where(g < group, share_ref[g], 0)
    all_counts = counts_ref[0]
    for t in range(1, n_tasks):
        all_counts = all_counts + counts_ref[t]
    values[:, pl.ds(pl.multiple_of(core * half, LANES), half)] = mine_ref[...]
    values[:, pl.ds(pl.multiple_of((1 - core) * half, LANES), half)] = theirs_ref[...]
    blocks = []
    for s in range(seqs):
        rows = slice(s * SEQ_LEN, (s + 1) * SEQ_LEN)
        low = low_ref[rows, :]
        b4 = b4_ref[s]
        error = values[rows, :] + dot(low, b4) * RANK_SCALE - teacher_ref[rows, :].astype(F32)
        count = jnp.full((1, KV), counts_ref[first_task + slot_ref[s]], jnp.int32).astype(F32)
        mean = jnp.full((1, KV), all_counts, jnp.int32).astype(F32) / n_tasks
        value_grad = (error * (mean / count * loss_scale)).astype(BF16)
        blocks.append((dot_nt(value_grad, b4) * RANK_SCALE).astype(BF16))
        second = dot(low.T, value_grad)[:R] * RANK_SCALE
        for c in range(COL_TILES):
            spaced[pl.ds(c, R, stride=COL_TILES), :] = second[:, c * LANES : (c + 1) * LANES]
        grads[s, A_ROWS:, :] = spaced[...].astype(BF16)
    zero = jnp.zeros_like(blocks[0])
    low_grad = jnp.concatenate(
        [
            jnp.concatenate([blocks[s] if s == i else zero for i in range(seqs)], axis=1)
            for s in range(seqs)
        ],
        axis=0,
    )
    group = lax.broadcasted_iota(jnp.int32, low_grad.shape, 1) % LANES // R
    low_grad = jnp.concatenate(
        [jnp.where(group == j, low_grad, jnp.zeros_like(low_grad)) for j in range(PACK)], axis=0
    )
    first = (dot(tok_t_ref[...], low_grad) * SHRINK).astype(BF16)
    for s in range(seqs):
        grads[s, :A_ROWS, :] = first[:, s * LANES : (s + 1) * LANES]
    store_grads(grads, out_ref)


def store_grads(grads, out_ref):
    if len(out_ref.shape) == 3:
        out_ref[...] = grads[...]
        return
    tiles = out_ref.shape[2]
    for i in range(out_ref.shape[0]):
        for s in range(out_ref.shape[1]):
            out_ref[i, s] = grads[s, i * tiles : (i + 1) * tiles, :]


def hyper_kernel(step, codes_t_ref, grads_ref, out_ref, scr, done, sems):
    devices, seqs, tiles, _ = grads_ref.shape
    rows = devices * seqs
    for i in range(devices):
        for s in range(seqs):
            at = (i * seqs + s) * tiles
            scr[at : at + tiles, :] = grads_ref[i, s].astype(F32)
    codes_t = codes_t_ref[...]
    copies = []
    for k in range(tiles):
        part = scr[pl.ds(k, rows, stride=tiles), :].astype(BF16)
        done[:, k * LANES : (k + 1) * LANES] = dot(codes_t, part)
        if (k + 1) % step == 0:
            cols = slice((k + 1 - step) * LANES, (k + 1) * LANES)
            copies.append(
                pltpu.make_async_copy(done.at[:, cols], out_ref.at[:, cols], sems.at[k // step])
            )
            copies[-1].start()
    for copy in copies:
        copy.wait()


def tied(*groups):
    return lax.optimization_barrier(groups)


def shards(
    task_codes, hyper_weight, frozen_weight, tokens, teacher, seq_slot, task_share, token_counts
):
    groups = lax.axis_size("dp")
    members = lax.axis_size("mp")
    devices = groups * members
    chips = groups // 2
    tok_dev = tokens.shape[0]
    seqs = seq_slot.shape[0]
    depth = frozen_weight.shape[0]
    tiles = hyper_weight.shape[1] // LANES
    rows = A_ROWS + B_ROWS
    width_h = task_codes.shape[1]
    loss_scale = 1.0 / math.sqrt(tok_dev * members)
    me_dp, me_mp = lax.axis_index("dp"), lax.axis_index("mp")
    core, chip = me_dp % 2, me_dp // 2
    place = jnp.stack([me_mp, core, chip, me_dp]).astype(jnp.int32)
    half = KV // 2
    width = half // chips
    whole_tiles = tiles % 16 == 0

    mid = depth // 2

    def direct(block):
        return {
            m: xor_permute(block, "dp", m << 1) if m else block
            for m in range(chips)
            if m & (m - 1) == 0
        }

    def forwarded(held, by_high):
        held = dict(held)
        for m in range(1, chips):
            if m not in held:
                bit = 1 << (m.bit_length() - 1) if by_high else m & -m
                held[m] = xor_permute(held[m ^ bit], "dp", bit << 1)
        return held

    other_tokens = xor_permute(tokens, "dp", 1)
    fits = width % LANES == 0 and mid % LANES == 0 and members == 4 and chips == 4
    fits = fits and whole_tiles and groups * seqs % 16 == 0
    near_rows = [(1, 0, depth, 0)]
    if fits:
        near, top, bottom = pl.pallas_call(
            chunk_kernel,
            in_specs=[pl.BlockSpec(memory_space=pltpu.SMEM)]
            + [pl.BlockSpec(memory_space=pltpu.HBM)] * 2,
            out_specs=[pl.BlockSpec(memory_space=pltpu.VMEM)] * 3,
            out_shape=[sds((n + SLOT_ROWS, width), BF16) for n in (depth, mid, mid)],
            scratch_shapes=[
                pltpu.SMEM(seq_slot.shape, jnp.int32),
                pltpu.SemaphoreType.DMA((4,)),
            ],
            compiler_params=pltpu.CompilerParams(vmem_limit_bytes=ALL_VMEM),
        )(place, seq_slot, frozen_weight)
        near, top, bottom, task_codes = tied(near, top, bottom, task_codes)
        other_tokens, task_codes = tied(other_tokens, task_codes)
        near = xor_permute(near, "mp", 1)
        top = xor_permute(top, "mp", 2)
        bottom = xor_permute(bottom, "mp", 3)
        near_held = direct(near)
        far = jnp.concatenate([top, bottom], axis=0)
        at = mid + SLOT_ROWS
        far_rows = [(2, 0, mid, 0), (3, mid, mid, at)]
        third_rows = [(3, 0, mid, 0), (2, mid, mid, at)]
        note_parts = [near, top, bottom]
    else:
        chunk = lax.dynamic_slice_in_dim(frozen_weight, core * half + chip * width, width, 1)
        near = xor_permute(chunk, "mp", 1)
        near_held = direct(near)
        far = jnp.concatenate(
            [xor_permute(chunk, "mp", k) for k in range(2, members)], axis=0
        )
        far_rows = [(k, 0, depth, (k - 2) * depth) for k in range(2, members)]

    if fits:
        sent = call(
            functools.partial(adapters_kernel, tiles),
            [sds((groups, TPG * tiles + SLOT_ROWS, LANES), BF16)],
            scratch=[pltpu.VMEM((groups * TPG * tiles, LANES), F32)],
            n_smem=2,
            n_in=2,
            flops=2 * groups * TPG * hyper_weight.size,
            nbytes=4 * hyper_weight.size,
        )(task_share, seq_slot, task_codes, hyper_weight)[0]
        got = lax.all_to_all(sent, "dp", 0, 0, tiled=True)
        chosen = call(
            functools.partial(choose_kernel, tiles, members),
            [sds((groups * seqs * (tiles + 1), LANES), BF16)] * members,
            n_smem=1,
            n_in=members,
            nbytes=8 * hyper_weight.size,
        )(seq_slot, *note_parts, got)
        near_held, far, chosen = tied(near_held, far, chosen)
        third = xor_permute(far, "mp", 1)
        near_pieces = forwarded(near_held, True)
        adapt = [chosen[0]] + [xor_permute(chosen[k], "mp", k) for k in range(1, members)]
    else:
        near_pieces = forwarded(near_held, True)
        slots = lax.all_to_all(
            jnp.broadcast_to(seq_slot[None], (devices, seqs)), ("dp", "mp"), 0, 0, tiled=True
        ).reshape(-1)
        offsets = jnp.cumsum(task_share) - task_share
        task_of = jnp.repeat(offsets, members * seqs) + slots
        pick = (jnp.arange(task_codes.shape[0])[:, None] == task_of[None, :]).astype(BF16)
        codes_t = dot(task_codes.T, pick).astype(BF16)
        sent = dot(codes_t.T, hyper_weight).astype(BF16).reshape(devices, seqs, tiles, LANES)
        adapt = lax.all_to_all(sent, ("dp", "mp"), 0, 0, tiled=True)
        adapt = adapt.transpose(1, 0, 2, 3).reshape(seqs, rows, LANES)

    far_held = direct(far)
    if fits:
        third_held = direct(third)
        sets = [(list(near_pieces.items()), near_rows)]
        accs = frozen_call(place, depth, half, [tokens, other_tokens], frozen_weight, sets, [])
        third_held, far_held, accs, adapt = tied(third_held, far_held, accs, adapt)
        third_pieces = forwarded(third_held, True)
    far_pieces = forwarded(far_held, False)

    low_outs = [
        sds((tok_dev, LANES), BF16),
        sds((seqs, LANES, KV), BF16),
        sds((D // PACK, PACK * tok_dev), BF16),
    ]
    low_cost = dict(
        flops=4 * tokens.size * LANES * seqs, nbytes=4 * tokens.size + 4 * seqs * rows * LANES
    )
    low_scratch = [pltpu.VMEM((B_ROWS, LANES), F32)]
    if fits:
        last = chips - 1
        sets = [
            ([(m, far_held[m]) for m in far_held], far_rows),
            ([(m, third_held[m]) for m in third_held], third_rows),
        ]
        layout, flat = frozen_layout(sets)
        n_flat, n_adapt = len(flat), len(adapt)

        def middle(*refs):
            refs = list(refs)
            place_ref, share_ref, codes_ref = refs[:3]
            token_refs, refs = refs[3:5], refs[5:]
            piece_refs, refs = refs[:n_flat], refs[n_flat:]
            acc_refs, refs = refs[:2], refs[2:]
            adapt_refs, refs = refs[:n_adapt], refs[n_adapt:]
            out_refs, refs = refs[:2], refs[2:]
            low_rank_kernel(
                tiles, place_ref, share_ref, codes_ref, adapt_refs, token_refs[0], *refs
            )
            frozen_kernel(
                2, depth, False, layout, True, place_ref, *token_refs, *piece_refs, *acc_refs,
                *out_refs,
            )

        *accs, low, b4, tok_t, codes_t = call(
            middle,
            [sds((tok_dev, half), F32)] * 2
            + low_outs
            + [sds((width_h, devices * seqs), BF16)],
            scratch=low_scratch
            + [
                pltpu.VMEM((seqs, rows, LANES), BF16),
                pltpu.VMEM((devices * seqs, LANES), F32),
            ],
            n_smem=2,
            n_in=5 + n_flat + n_adapt,
        )(place, task_share, task_codes, tokens, other_tokens, *flat, *accs, *adapt)
        sets = [([(last, far_pieces[last])], far_rows), ([(last, third_pieces[last])], third_rows)]
        theirs = frozen_call(place, depth, half, [other_tokens], None, sets, accs[1:])[0]
        mine = frozen_call(place, depth, half, [tokens], None, sets, accs[:1])[0]
    else:
        low, b4, tok_t = call(
            low_rank_body, low_outs, scratch=low_scratch, n_in=2, **low_cost
        )(adapt, tokens)
        own_half = lax.dynamic_slice_in_dim(frozen_weight, core * half, half, 1)
        order = jnp.arange(chips) ^ chip
        found = {0: own_half}
        for pieces, segments in ((near_pieces, near_rows), (far_pieces, far_rows)):
            joined = jnp.stack([pieces[m] for m in range(chips)])
            joined = jnp.take(joined, order, axis=0).transpose(1, 0, 2).reshape(-1, half)
            for k, _, size, row in segments:
                found[k] = joined[row : row + size]
        blocks = jnp.stack([found[k] for k in range(members)])
        weight = jnp.take(blocks, jnp.arange(members) ^ me_mp, axis=0).reshape(D, half)
        mine = jnp.dot(tokens, weight, preferred_element_type=F32)
        theirs = jnp.dot(other_tokens, weight, preferred_element_type=F32)
    received = xor_permute(theirs, "dp", 1)

    split = (devices, seqs, tiles, LANES)
    grads = call(
        functools.partial(backward_kernel, loss_scale),
        [sds(split if whole_tiles else (seqs, rows, LANES), BF16)],
        scratch=[
            pltpu.VMEM((tok_dev, KV), F32),
            pltpu.VMEM((B_ROWS, LANES), F32),
            pltpu.VMEM((seqs, rows, LANES), BF16),
        ],
        n_smem=4,
        n_in=6,
        flops=4 * tokens.size * LANES * seqs,
        nbytes=4 * tokens.size,
    )(place, task_share, seq_slot, token_counts, mine, received, teacher, low, b4, tok_t)[0]
    if not whole_tiles:
        grads = grads.reshape(seqs, devices, tiles, LANES).transpose(1, 0, 2, 3)
    routed = lax.all_to_all(grads, ("dp", "mp"), 0, 0, tiled=True)
    step = 8 if whole_tiles else tiles
    return pl.pallas_call(
        functools.partial(hyper_kernel, step),
        out_shape=sds((width_h, tiles * LANES), F32),
        in_specs=[pl.BlockSpec(memory_space=pltpu.VMEM)] * 2,
        out_specs=pl.BlockSpec(memory_space=pl.ANY),
        scratch_shapes=[
            pltpu.VMEM((devices * seqs * tiles, LANES), F32),
            pltpu.VMEM((width_h, tiles * LANES), F32),
            pltpu.SemaphoreType.DMA((tiles // step,)),
        ],
        compiler_params=pltpu.CompilerParams(vmem_limit_bytes=VMEM_LIMIT),
    )(codes_t, routed)


def solution(mesh):
    placed = (
        P(),
        P(None, ("dp", "mp")),
        P("mp", None),
        P(("dp", "mp"), None),
        P(("dp", "mp"), None),
        P(("dp", "mp")),
        P(),
        P(),
    )
    return jax.shard_map(
        shards, mesh=mesh, in_specs=placed, out_specs=P(None, ("dp", "mp")), check_vma=False
    )
```

time: 117 us -> 105 us (0.90)
  blocking collectives: 35.6 us -> 23.2 us
  waiting for transfers between devices: 18 us -> 29.1 us
  local copies, waits for them, and re-layouts: 12.3 us -> 2.44 us
    all_to_all x1 -> x0, blocking collectives: 13.2 us -> none  [shards(): lax.all_to_all(jnp.broadcast_to(later_slot[None], (devices, seqs)), ('dp'...]
    ppermute x17 -> x18, waiting for transfers between devices: 18 us -> 29.1 us  [xor_permute(): lax.ppermute(array, axis, [(i, i ^ mask) for i in range(lax.axis_size(axi...]
    unnamed x44 -> x26, local copies, waits for them, and re-layouts: 7.83 us -> 2.44 us
    slice x6 -> x0, local copies, waits for them, and re-layouts: 3.87 us -> none  [the longest x4 3.84 us: halves(): return [parts[0][:middle], parts[0][middle:]]]
    pallas_call x3, Pallas kernels: 9.21 us -> 6.96 us  [frozen_call(): call(functools.partial(frozen_kernel, len(tokens), depth, weight is not N...]
    pallas_call x1, Pallas kernels: 4.47 us -> 2.31 us  [shards(): call(functools.partial(backward_kernel, loss_scale), [sds(split if whole_...]
    pallas_call x5 -> x4, Pallas kernels: 10.3 us -> 12.3 us  [the longest x1 6.98 us: shards(): call(middle, [sds((tok_dev, half), F32)] * 2 + low_outs + [sds((width_h,...]
    pallas_call x1, Pallas kernels: 0.77 us -> 2.65 us  [shards(): pl.pallas_call(chunk_kernel, in_specs=[pl.BlockSpec(memory_space=pltpu.SM...]
  transfers between devices with their start and end apart: 18 -> 19, of which waited for: 6 -> 8; matrix products, arithmetic and copies ran while one was open for 5% -> 1% of each run, Pallas kernels for 12% -> 17%
where the time goes in v3:
time: 105 us; the launch traced here: 104 us
  waiting for transfers between devices  29.1 us (28%)
  Pallas kernels  24.2 us (23%)
  starting transfers between devices  23.6 us (22%)
  blocking collectives  23.2 us (22%)
  local copies, waits for them, and re-layouts  2.44 us (2%)
  other arithmetic  1.54 us (1%)
    ppermute x18, waiting for transfers between devices, xor_permute(): lax.ppermute(array, axis, [(i, i ^ mask) for i in range(lax.axis_size(axi...  29.1 us
    all_to_all x1, blocking collectives, shards(): routed = lax.all_to_all(grads, ('dp', 'mp'), 0, 0, tiled=True)  23.2 us
    ppermute x18, starting transfers between devices, xor_permute(): lax.ppermute(array, axis, [(i, i ^ mask) for i in range(lax.axis_size(axi...  19.1 us
    pallas_call x1, Pallas kernels, shards(): call(middle, [sds((tok_dev, half), F32)] * 2 + low_outs + [sds((width_h,...  6.98 us
    pallas_call x3, Pallas kernels, frozen_call(): call(functools.partial(frozen_kernel, len(tokens), depth, weight is not N...  6.96 us
    all_to_all x1, starting transfers between devices, shards(): got = lax.all_to_all(sent, 'dp', 0, 0, tiled=True)  4.54 us
    pallas_call x1, Pallas kernels, shards(): pl.pallas_call(chunk_kernel, in_specs=[pl.BlockSpec(memory_space=pltpu.SM...  2.65 us
    unnamed x26, local copies, waits for them, and re-layouts  2.44 us
  transfers between devices with their start and end apart: 19, of which 8 were waited for; matrix products, arithmetic and copies ran while one was open for 1% of the time, Pallas kernels for 17%

profile of v3, /device:TPU:1, one launch (start us, length us, event | category | flops | bytes accessed | tf_op | source)
XLA Modules:
  0.0 104.4 jit_solution(16925646980756755494)
XLA Ops:
  0.7 2.6 %shard_map.82 = (bf16[1296,128]{1,0:T(8,128)(2,1)}, bf16[656,128]{1,0:T(8,128)(2,1)}, bf16[656,128]{1,0:T(8,128)(2,1)}) custom-call(s32[4]{0:T(128)} %pad_add_fusion.place_ref.refs_0_, s32[2]{0:T(128)} %slot_ref.5, bf16[1280,1024]{1,0:T(8,128)(2,1)} %refs_2_.1), custom_call_target="tpu_custom_call" | custom-call | tf_op jit(solution)/shard_map/pallas_call | solution.py:403
  3.4 2.8 %collective-permute-start.1 = (bf16[1296,128]{1,0:T(8,128)(2,1)}, bf16[1296,128]{1,0:T(8,128)(2,1)}, u32[]{:S(2)}, u32[]{:S(2)}) collective-permute-start(bf16[1296,128]{1,0:T(8,128)(2,1)} %get-tuple-element.52), channel_id=1, source_target_pairs={{0,1},{1,0},{2,3},{3,2},{4,5},{5,4},{6,7},{7,6},{8,9},{9,8},{10,11... | collective-permute-start | bytes 995336 | tf_op jit(solution)/shard_map/ppermute | solution.py:61
  6.2 2.3 %collective-permute-start.4 = (bf16[656,128]{1,0:T(8,128)(2,1)}, bf16[656,128]{1,0:T(8,128)(2,1)S(1)}, u32[]{:S(2)}, u32[]{:S(2)}) collective-permute-start(bf16[656,128]{1,0:T(8,128)(2,1)} %get-tuple-element.53), channel_id=1, source_target_pairs={{0,2},{1,3},{2,0},{3,1},{4,6},{5,7},{6,4},{7,5},{8,10},{9,11},{10,... | collective-permute-start | bytes 503816 | tf_op jit(solution)/shard_map/ppermute | solution.py:61
  8.6 2.0 %shard_map.83 = bf16[8,208,128]{2,1,0:T(8,128)(2,1)} custom-call(s32[8]{0:T(128)S(1)} %copy-done.10, s32[2]{0:T(128)S(1)} %copy-done.7, bf16[16,128]{1,0:T(8,128)(2,1)S(1)} %copy-done.5, bf16[128,6144]{1,0:T(8,128)(2,1)S(1)} %copy-done.2), custom_call_target="tpu_custom_call" | custom-call | flops 50331648 | bytes 3145728 | tf_op jit(solution)/shard_map/pallas_call | solution.py:436
  10.6 4.5 %all-to-all-start = ((bf16[8,208,128]{2,1,0:T(8,128)(2,1)}), bf16[8,208,128]{2,1,0:T(8,128)(2,1)S(1)}, u32[]{:S(2)}, u32[]{:S(2)}) async-start(bf16[8,208,128]{2,1,0:T(8,128)(2,1)} %shard_map.83), calls=%async_computation | async-start | bytes 851968 | tf_op jit(solution)/shard_map/all_to_all | solution.py:445
  15.1 3.2 %collective-permute-done.1.refs_0_.refs_3_ = bf16[1296,128]{1,0:T(8,128)(2,1)} collective-permute-done((bf16[1296,128]{1,0:T(8,128)(2,1)}, bf16[1296,128]{1,0:T(8,128)(2,1)}, u32[]{:S(2)}, u32[]{:S(2)}) %collective-permute-start.1) | collective-permute-done | bytes 331808 | tf_op jit(solution)/shard_map/ppermute | solution.py:61
  18.3 1.3 %collective-permute-start.2 = (bf16[1296,128]{1,0:T(8,128)(2,1)}, bf16[1296,128]{1,0:T(8,128)(2,1)}, u32[]{:S(2)}, u32[]{:S(2)}) collective-permute-start(bf16[1296,128]{1,0:T(8,128)(2,1)} %collective-permute-done.1.refs_0_.refs_3_), channel_id=1, source_target_pairs={{0,8},{4,12},{8,0},{12,4},{16,24},{20,28},{24,16},{28,20},{1,9},{5... | collective-permute-start | bytes 995336 | tf_op jit(solution)/shard_map/ppermute | solution.py:61
  20.7 3.2 %collective-permute-done.5.refs_2_ = bf16[656,128]{1,0:T(8,128)(2,1)} collective-permute-done((bf16[656,128]{1,0:T(8,128)(2,1)}, bf16[656,128]{1,0:T(8,128)(2,1)}, u32[]{:S(2)}, u32[]{:S(2)}) %collective-permute-start.5) | collective-permute-done | bytes 167968 | tf_op jit(solution)/shard_map/ppermute | solution.py:61
  25.5 1.3 %shard_map.84 = (bf16[784,128]{1,0:T(8,128)(2,1)S(1)}, bf16[784,128]{1,0:T(8,128)(2,1)S(1)}, bf16[784,128]{1,0:T(8,128)(2,1)S(1)}, bf16[784,128]{1,0:T(8,128)(2,1)S(1)}) custom-call(s32[2]{0:T(128)S(1)} %copy-done.8, bf16[1296,128]{1,0:T(8,128)(2,1)} %collective-permute-done.1.refs_0_.refs_3_, bf16[656,128]{1,0:T(8,128)(2,1)S(1)} %collective-permute-done.4.refs_1_, ...), custom_call_target="tpu_custom_call" | custom-call | bytes 6291456 | tf_op jit(solution)/shard_map/pallas_call | solution.py:446
  26.8 2.5 %collective-permute-done.2.refs_4_ = bf16[1296,128]{1,0:T(8,128)(2,1)} collective-permute-done((bf16[1296,128]{1,0:T(8,128)(2,1)}, bf16[1296,128]{1,0:T(8,128)(2,1)}, u32[]{:S(2)}, u32[]{:S(2)}) %collective-permute-start.2) | collective-permute-done | bytes 331808 | tf_op jit(solution)/shard_map/ppermute | solution.py:61
  29.7 1.5 %collective-permute-start.12 = (bf16[784,128]{1,0:T(8,128)(2,1)S(1)}, bf16[784,128]{1,0:T(8,128)(2,1)S(1)}, u32[]{:S(2)}, u32[]{:S(2)}) collective-permute-start(bf16[784,128]{1,0:T(8,128)(2,1)S(1)} %get-tuple-element.66), channel_id=1, source_target_pairs={{0,1},{1,0},{2,3},{3,2},{4,5},{5,4},{6,7},{7,6},{8,9},{9,8},{10,11... | collective-permute-start | bytes 602120 | tf_op jit(solution)/shard_map/ppermute | solution.py:61
  31.2 1.1 %collective-permute-start.13 = (bf16[784,128]{1,0:T(8,128)(2,1)S(1)}, bf16[784,128]{1,0:T(8,128)(2,1)S(1)}, u32[]{:S(2)}, u32[]{:S(2)}) collective-permute-start(bf16[784,128]{1,0:T(8,128)(2,1)S(1)} %get-tuple-element.67), channel_id=1, source_target_pairs={{0,2},{1,3},{2,0},{3,1},{4,6},{5,7},{6,4},{7,5},{8,10},{9,11},{10,... | collective-permute-start | bytes 602120 | tf_op jit(solution)/shard_map/ppermute | solution.py:61
  33.8 12.7 %collective-permute-done.12.refs_14_ = bf16[784,128]{1,0:T(8,128)(2,1)S(1)} collective-permute-done((bf16[784,128]{1,0:T(8,128)(2,1)S(1)}, bf16[784,128]{1,0:T(8,128)(2,1)S(1)}, u32[]{:S(2)}, u32[]{:S(2)}) %collective-permute-start.12) | collective-permute-done | bytes 200736 | tf_op jit(solution)/shard_map/ppermute | solution.py:61
  46.5 1.2 %collective-permute-start.9 = (bf16[1312,128]{1,0:T(8,128)(2,1)S(1)}, bf16[1312,128]{1,0:T(8,128)(2,1)S(1)}, u32[]{:S(2)}, u32[]{:S(2)}) collective-permute-start(bf16[1312,128]{1,0:T(8,128)(2,1)S(1)} %pad_maximum_fusion.refs_5_), channel_id=1, source_target_pairs={{0,8},{4,12},{8,0},{12,4},{16,24},{20,28},{24,16},{28,20},{1,9},{5... | collective-permute-start | bytes 1007624 | tf_op jit(solution)/shard_map/ppermute | solution.py:61
  49.0 1.7 %copy-done.1 = bf16[1280,1024]{1,0:T(8,128)(2,1)S(1)} copy-done((bf16[1280,1024]{1,0:T(8,128)(2,1)S(1)}, bf16[1280,1024]{1,0:T(8,128)(2,1)}, u32[]{:S(2)}) %copy-start.1) | copy-done | bytes 2621464
  50.7 3.6 %shard_map.85 = (f32[256,512]{1,0:T(8,128)S(1)}, f32[256,512]{1,0:T(8,128)S(1)}) custom-call(s32[4]{0:T(128)S(1)} %copy-done.4, bf16[256,5120]{1,0:T(8,128)(2,1)S(1)} %copy-done, bf16[256,5120]{1,0:T(8,128)(2,1)} %collective-permute-done.refs_1_.refs_4_.refs_0_, bf16[1280,1024]{1,0:T(8,128)(2,1)S(1)} %copy-done.1, ...), custom_call_target="tpu_custom_call" | custom-call | flops 1350565888 | bytes 2375680 | tf_op jit(solution)/shard_map/pallas_call | solution.py:264
  55.4 5.6 %collective-permute-done.7.refs_9_ = bf16[1312,128]{1,0:T(8,128)(2,1)S(1)} collective-permute-done((bf16[1312,128]{1,0:T(8,128)(2,1)S(1)}, bf16[1312,128]{1,0:T(8,128)(2,1)S(1)}, u32[]{:S(2)}, u32[]{:S(2)}) %collective-permute-start.7) | collective-permute-done | bytes 335904 | tf_op jit(solution)/shard_map/ppermute | solution.py:61
  61.0 1.6 %collective-permute-start.15 = (bf16[1312,128]{1,0:T(8,128)(2,1)S(1)}, bf16[1312,128]{1,0:T(8,128)(2,1)S(1)}, u32[]{:S(2)}, u32[]{:S(2)}) collective-permute-start(bf16[1312,128]{1,0:T(8,128)(2,1)S(1)} %collective-permute-done.10.refs_7_), channel_id=1, source_target_pairs={{0,8},{4,12},{8,0},{12,4},{16,24},{20,28},{24,16},{28,20},{1,9},{5... | collective-permute-start | bytes 1007624 | tf_op jit(solution)/shard_map/ppermute | solution.py:61
  62.6 7.0 %shard_map.86 = (f32[256,512]{1,0:T(8,128)S(1)}, f32[256,512]{1,0:T(8,128)S(1)}, bf16[256,128]{1,0:T(8,128)(2,1)S(1)}, bf16[2,128,1024]{2,1,0:T(8,128)(2,1)S(1)}...) custom-call(s32[4]{0:T(128)S(1)} %copy-done.4, s32[8]{0:T(128)S(1)} %copy-done.11, ...), custom_call_target="tpu_custom_call" | custom-call | tf_op jit(solution)/shard_map/pallas_call | solution.py:513
  69.6 2.3 %shard_map.88 = f32[256,512]{1,0:T(8,128)S(1)} custom-call(s32[4]{0:T(128)S(1)} %copy-done.4, bf16[256,5120]{1,0:T(8,128)(2,1)} %collective-permute-done.refs_1_.refs_4_.refs_0_, bf16[1312,128]{1,0:T(8,128)(2,1)S(1)} %collective-permute-done.15.refs_1_, bf16[1312,128]{1,0:T(8,128)(2,1)S(1)} %collective-permute-done.16.refs_2_, ...), custom_call_target="tpu_custom_call" | custom-call | flops 171966464 | bytes 1196032 | tf_op jit(solution)/shard_map/pallas_call | solution.py:264
  71.9 3.3 %collective-permute-start.17 = (f32[256,512]{1,0:T(8,128)S(1)}, f32[256,512]{1,0:T(8,128)S(1)}, u32[]{:S(2)}, u32[]{:S(2)}) collective-permute-start(f32[256,512]{1,0:T(8,128)S(1)} %shard_map.88), channel_id=1, source_target_pairs={{0,4},{4,0},{8,12},{12,8},{16,20},{20,16},{24,28},{28,24},{1,5},{5... | collective-permute-start | bytes 1572872 | tf_op jit(solution)/shard_map/ppermute | solution.py:61
  76.8 2.3 %shard_map.89 = bf16[32,2,48,128]{3,2,1,0:T(8,128)(2,1)S(1)} custom-call(s32[4]{0:T(128)S(1)} %copy-done.4, s32[8]{0:T(128)S(1)} %copy-done.11, s32[2]{0:T(128)S(1)} %copy-done.9, s32[16]{0:T(128)S(1)} %copy-done.12, f32[256,512]{1,0:T(8,128)S(1)} %shard_map.87.mine_ref, f32[256,512]{1,0:T(8,128)S(1)} %collective-permute-done.17.theirs_ref, ...), custom_call_target="tpu_custom_call" | custom-call | flops 1342177280 | bytes 5242880 | tf_op jit(solution)/shard_map/pallas_call | solution.py:548
  79.1 23.2 %all_to_all.10.grads_ref = bf16[32,2,48,128]{3,2,1,0:T(8,128)(2,1)S(1)} all-to-all(bf16[32,2,48,128]{3,2,1,0:T(8,128)(2,1)S(1)} %shard_map.89), channel_id=1, replica_groups=mesh['dp'=8,'mp'=4] {'dp','mp'}, dimensions={0} | all-to-all | bytes 1572864 | tf_op jit(solution)/shard_map/all_to_all | solution.py:563
  102.3 2.0 %shard_map.90 = f32[128,6144]{1,0:T(8,128)} custom-call(bf16[128,64]{1,0:T(8,128)(2,1)S(1)} %get-tuple-element.81.codes_t_ref, bf16[32,2,48,128]{3,2,1,0:T(8,128)(2,1)S(1)} %all_to_all.10.grads_ref), custom_call_target="tpu_custom_call" | custom-call | tf_op jit(solution)/shard_map/pallas_call | solution.py:565
  (52 shorter events, 9.2 us)
Async XLA Ops:
  0.0 8.6 %copy-start.10 = (s32[8]{0:T(128)S(1)}, s32[8]{0:T(128)}, u32[]{:S(2)}) copy-start(s32[8]{0:T(128)} %share_ref.3) | copy-start | bytes 100
  0.0 8.5 %collective-permute-start = (bf16[256,5120]{1,0:T(8,128)(2,1)}, bf16[256,5120]{1,0:T(8,128)(2,1)}, u32[]{:S(2)}, u32[]{:S(2)}) collective-permute-start(bf16[256,5120]{1,0:T(8,128)(2,1)} %refs_0_.3), channel_id=1, source_target_pairs={{0,4},{4,0},{8,12},{12,8},{16,20},{20,16},{24,28},{28,24},{1,5},{5... | collective-permute-start | bytes 7864328 | tf_op jit(solution)/shard_map/ppermute | solution.py:61
  3.4 45.6 %copy-start = (bf16[256,5120]{1,0:T(8,128)(2,1)S(1)}, bf16[256,5120]{1,0:T(8,128)(2,1)}, u32[]{:S(2)}) copy-start(bf16[256,5120]{1,0:T(8,128)(2,1)} %refs_0_.3) | copy-start | bytes 7864324
  3.4 45.6 %copy-start.4 = (s32[4]{0:T(128)S(1)}, s32[4]{0:T(128)}, u32[]{:S(2)}) copy-start(s32[4]{0:T(128)} %pad_add_fusion.place_ref.refs_0_) | copy-start | bytes 52
  3.4 14.9 %collective-permute-start.1 = (bf16[1296,128]{1,0:T(8,128)(2,1)}, bf16[1296,128]{1,0:T(8,128)(2,1)}, u32[]{:S(2)}, u32[]{:S(2)}) collective-permute-start(bf16[1296,128]{1,0:T(8,128)(2,1)} %get-tuple-element.52), channel_id=1, source_target_pairs={{0,1},{1,0},{2,3},{3,2},{4,5},{5,4},{6,7},{7,6},{8,9},{9,8},{10,11... | collective-permute-start | bytes 995336 | tf_op jit(solution)/shard_map/ppermute | solution.py:61
  6.2 14.5 %collective-permute-start.4 = (bf16[656,128]{1,0:T(8,128)(2,1)}, bf16[656,128]{1,0:T(8,128)(2,1)S(1)}, u32[]{:S(2)}, u32[]{:S(2)}) collective-permute-start(bf16[656,128]{1,0:T(8,128)(2,1)} %get-tuple-element.53), channel_id=1, source_target_pairs={{0,2},{1,3},{2,0},{3,1},{4,6},{5,7},{6,4},{7,5},{8,10},{9,11},{10,... | collective-permute-start | bytes 503816 | tf_op jit(solution)/shard_map/ppermute | solution.py:61
  8.5 15.4 %collective-permute-start.5 = (bf16[656,128]{1,0:T(8,128)(2,1)}, bf16[656,128]{1,0:T(8,128)(2,1)}, u32[]{:S(2)}, u32[]{:S(2)}) collective-permute-start(bf16[656,128]{1,0:T(8,128)(2,1)} %get-tuple-element.54), channel_id=1, source_target_pairs={{0,3},{1,2},{2,1},{3,0},{4,7},{5,6},{6,5},{7,4},{8,11},{9,10},{10,... | collective-permute-start | bytes 503816 | tf_op jit(solution)/shard_map/ppermute | solution.py:61
  10.6 14.3 %all-to-all-start = ((bf16[8,208,128]{2,1,0:T(8,128)(2,1)}), bf16[8,208,128]{2,1,0:T(8,128)(2,1)S(1)}, u32[]{:S(2)}, u32[]{:S(2)}) async-start(bf16[8,208,128]{2,1,0:T(8,128)(2,1)} %shard_map.83), calls=%async_computation | async-start | bytes 851968 | tf_op jit(solution)/shard_map/all_to_all | solution.py:445
  18.3 11.0 %collective-permute-start.2 = (bf16[1296,128]{1,0:T(8,128)(2,1)}, bf16[1296,128]{1,0:T(8,128)(2,1)}, u32[]{:S(2)}, u32[]{:S(2)}) collective-permute-start(bf16[1296,128]{1,0:T(8,128)(2,1)} %collective-permute-done.1.refs_0_.refs_3_), channel_id=1, source_target_pairs={{0,8},{4,12},{8,0},{12,4},{16,24},{20,28},{24,16},{28,20},{1,9},{5... | collective-permute-start | bytes 995336 | tf_op jit(solution)/shard_map/ppermute | solution.py:61
  19.5 10.2 %collective-permute-start.3 = (bf16[1296,128]{1,0:T(8,128)(2,1)}, bf16[1296,128]{1,0:T(8,128)(2,1)}, u32[]{:S(2)}, u32[]{:S(2)}) collective-permute-start(bf16[1296,128]{1,0:T(8,128)(2,1)} %collective-permute-done.1.refs_0_.refs_3_), channel_id=1, source_target_pairs={{0,16},{4,20},{8,24},{12,28},{16,0},{20,4},{24,8},{28,12},{1,17},{... | collective-permute-start | bytes 995336 | tf_op jit(solution)/shard_map/ppermute | solution.py:61
  29.7 32.9 %copy-start.6 = (bf16[16,128]{1,0:T(8,128)(2,1)S(1)}, bf16[16,128]{1,0:T(8,128)(2,1)}, u32[]{:S(2)}) copy-start(bf16[16,128]{1,0:T(8,128)(2,1)} %refs_2_.2) | copy-start | bytes 12292
  29.7 32.9 %copy-start.11 = (s32[8]{0:T(128)S(1)}, s32[8]{0:T(128)}, u32[]{:S(2)}) copy-start(s32[8]{0:T(128)} %share_ref.3) | copy-start | bytes 100
  29.7 18.0 %collective-permute-start.6 = (bf16[1312,128]{1,0:T(8,128)(2,1)S(1)}, bf16[1312,128]{1,0:T(8,128)(2,1)S(1)}, u32[]{:S(2)}, u32[]{:S(2)}) collective-permute-start(bf16[1312,128]{1,0:T(8,128)(2,1)S(1)} %pad_maximum_fusion.refs_5_), channel_id=1, source_target_pairs={{0,1},{1,0},{2,3},{3,2},{4,5},{5,4},{6,7},{7,6},{8,9},{9,8},{10,11... | collective-permute-start | bytes 1007624 | tf_op jit(solution)/shard_map/ppermute | solution.py:61
  29.7 16.8 %collective-permute-start.12 = (bf16[784,128]{1,0:T(8,128)(2,1)S(1)}, bf16[784,128]{1,0:T(8,128)(2,1)S(1)}, u32[]{:S(2)}, u32[]{:S(2)}) collective-permute-start(bf16[784,128]{1,0:T(8,128)(2,1)S(1)} %get-tuple-element.66), channel_id=1, source_target_pairs={{0,1},{1,0},{2,3},{3,2},{4,5},{5,4},{6,7},{7,6},{8,9},{9,8},{10,11... | collective-permute-start | bytes 602120 | tf_op jit(solution)/shard_map/ppermute | solution.py:61
  31.2 16.8 %collective-permute-start.13 = (bf16[784,128]{1,0:T(8,128)(2,1)S(1)}, bf16[784,128]{1,0:T(8,128)(2,1)S(1)}, u32[]{:S(2)}, u32[]{:S(2)}) collective-permute-start(bf16[784,128]{1,0:T(8,128)(2,1)S(1)} %get-tuple-element.67), channel_id=1, source_target_pairs={{0,2},{1,3},{2,0},{3,1},{4,6},{5,7},{6,4},{7,5},{8,10},{9,11},{10,... | collective-permute-start | bytes 602120 | tf_op jit(solution)/shard_map/ppermute | solution.py:61
  32.3 16.6 %collective-permute-start.11 = (bf16[1296,128]{1,0:T(8,128)(2,1)}, bf16[1296,128]{1,0:T(8,128)(2,1)S(1)}, u32[]{:S(2)}, u32[]{:S(2)}) collective-permute-start(bf16[1296,128]{1,0:T(8,128)(2,1)} %collective-permute-done.2.refs_4_), channel_id=1, source_target_pairs={{0,16},{4,20},{8,24},{12,28},{16,0},{20,4},{24,8},{28,12},{1,17},{... | collective-permute-start | bytes 995336 | tf_op jit(solution)/shard_map/ppermute | solution.py:61
  33.4 22.1 %collective-permute-start.10 = (bf16[1312,128]{1,0:T(8,128)(2,1)S(1)}, bf16[1312,128]{1,0:T(8,128)(2,1)S(1)}, u32[]{:S(2)}, u32[]{:S(2)}) collective-permute-start(bf16[1312,128]{1,0:T(8,128)(2,1)S(1)} %pad_maximum_fusion.refs_5_), channel_id=1, source_target_pairs={{0,16},{4,20},{8,24},{12,28},{16,0},{20,4},{24,8},{28,12},{1,17},{... | collective-permute-start | bytes 1007624 | tf_op jit(solution)/shard_map/ppermute | solution.py:61
  46.5 8.9 %collective-permute-start.9 = (bf16[1312,128]{1,0:T(8,128)(2,1)S(1)}, bf16[1312,128]{1,0:T(8,128)(2,1)S(1)}, u32[]{:S(2)}, u32[]{:S(2)}) collective-permute-start(bf16[1312,128]{1,0:T(8,128)(2,1)S(1)} %pad_maximum_fusion.refs_5_), channel_id=1, source_target_pairs={{0,8},{4,12},{8,0},{12,4},{16,24},{20,28},{24,16},{28,20},{1,9},{5... | collective-permute-start | bytes 1007624 | tf_op jit(solution)/shard_map/ppermute | solution.py:61
  47.7 13.3 %collective-permute-start.7 = (bf16[1312,128]{1,0:T(8,128)(2,1)S(1)}, bf16[1312,128]{1,0:T(8,128)(2,1)S(1)}, u32[]{:S(2)}, u32[]{:S(2)}) collective-permute-start(bf16[1312,128]{1,0:T(8,128)(2,1)S(1)} %collective-permute-done.6.refs_8_), channel_id=1, source_target_pairs={{0,8},{4,12},{8,0},{12,4},{16,24},{20,28},{24,16},{28,20},{1,9},{5... | collective-permute-start | bytes 1007624 | tf_op jit(solution)/shard_map/ppermute | solution.py:61
  48.0 13.0 %collective-permute-start.8 = (bf16[1312,128]{1,0:T(8,128)(2,1)S(1)}, bf16[1312,128]{1,0:T(8,128)(2,1)S(1)}, u32[]{:S(2)}, u32[]{:S(2)}) collective-permute-start(bf16[1312,128]{1,0:T(8,128)(2,1)S(1)} %collective-permute-done.6.refs_8_), channel_id=1, source_target_pairs={{0,16},{4,20},{8,24},{12,28},{16,0},{20,4},{24,8},{28,12},{1,17},{... | collective-permute-start | bytes 1007624 | tf_op jit(solution)/shard_map/ppermute | solution.py:61
  49.0 6.5 %collective-permute-start.14 = (bf16[784,128]{1,0:T(8,128)(2,1)S(1)}, bf16[784,128]{1,0:T(8,128)(2,1)S(1)}, u32[]{:S(2)}, u32[]{:S(2)}) collective-permute-start(bf16[784,128]{1,0:T(8,128)(2,1)S(1)} %get-tuple-element.68), channel_id=1, source_target_pairs={{0,3},{1,2},{2,1},{3,0},{4,7},{5,6},{6,5},{7,4},{8,11},{9,10},{10,... | collective-permute-start | bytes 602120 | tf_op jit(solution)/shard_map/ppermute | solution.py:61
  61.0 8.6 %collective-permute-start.15 = (bf16[1312,128]{1,0:T(8,128)(2,1)S(1)}, bf16[1312,128]{1,0:T(8,128)(2,1)S(1)}, u32[]{:S(2)}, u32[]{:S(2)}) collective-permute-start(bf16[1312,128]{1,0:T(8,128)(2,1)S(1)} %collective-permute-done.10.refs_7_), channel_id=1, source_target_pairs={{0,8},{4,12},{8,0},{12,4},{16,24},{20,28},{24,16},{28,20},{1,9},{5... | collective-permute-start | bytes 1007624 | tf_op jit(solution)/shard_map/ppermute | solution.py:61
  62.6 7.0 %collective-permute-start.16 = (bf16[1312,128]{1,0:T(8,128)(2,1)S(1)}, bf16[1312,128]{1,0:T(8,128)(2,1)S(1)}, u32[]{:S(2)}, u32[]{:S(2)}) collective-permute-start(bf16[1312,128]{1,0:T(8,128)(2,1)S(1)} %collective-permute-done.7.refs_9_), channel_id=1, source_target_pairs={{0,16},{4,20},{8,24},{12,28},{16,0},{20,4},{24,8},{28,12},{1,17},{... | collective-permute-start | bytes 1007624 | tf_op jit(solution)/shard_map/ppermute | solution.py:61
  71.9 4.9 %collective-permute-start.17 = (f32[256,512]{1,0:T(8,128)S(1)}, f32[256,512]{1,0:T(8,128)S(1)}, u32[]{:S(2)}, u32[]{:S(2)}) collective-permute-start(f32[256,512]{1,0:T(8,128)S(1)} %shard_map.88), channel_id=1, source_target_pairs={{0,4},{4,0},{8,12},{12,8},{16,20},{20,16},{24,28},{28,24},{1,5},{5... | collective-permute-start | bytes 1572872 | tf_op jit(solution)/shard_map/ppermute | solution.py:61
  (8 other events, 42.7 us)

commit v4 on v3

--- a/solution.py
+++ b/solution.py
@@ -119,8 +119,7 @@
         out_ref[g, TPG * tiles :, :] = note
 
 
-def choose_kernel(tiles, n, slot_ref, *refs):
-    note_refs, got_ref, out_refs = refs[: n - 1], refs[n - 1], refs[n:]
+def choose_kernel(tiles, slot_ref, near_ref, far_ref, got_ref, *out_refs):
     seqs = slot_ref.shape[0]
     groups = got_ref.shape[0]
     row = lax.broadcasted_iota(jnp.int32, (groups * seqs, LANES), 0)
@@ -130,10 +129,15 @@
         for s in range(seqs):
             table = jnp.where(row == g * seqs + s, notes[s : s + 1, :], table)
     table = table.astype(BF16)
+    far_rows = far_ref.shape[0]
+    out_refs[1][:far_rows, :] = far_ref[...]
+    note_ends = [None, (near_ref, near_ref.shape[0]), (far_ref, far_rows // 2), (far_ref, far_rows)]
     for k, out in enumerate(out_refs):
         if k > 0:
-            note_ref = note_refs[k - 1]
-            notes = note_ref[note_ref.shape[0] - SLOT_ROWS :, :].astype(F32).astype(jnp.int32)
+            note_ref, end = note_ends[k]
+            notes = note_ref[end - SLOT_ROWS : end, :].astype(F32).astype(jnp.int32)
+        if k == 1:
+            out = out.at[far_rows:, :]
         for s in range(seqs):
             slot = slot_ref[s] if k == 0 else jnp.max(notes[s : s + 1, :])
             rows = pl.ds(pl.multiple_of(slot * tiles, 16), tiles)
@@ -152,6 +156,7 @@
     groups = share_ref.shape[0]
     per_part = groups * seqs
     for k, part in enumerate(adapt_refs):
+        part = part.at[part.shape[0] - per_part * (tiles + 1) :, :]
         table[k * per_part : (k + 1) * per_part, :] = part[per_part * tiles :, :].astype(F32)
         for g in range(groups):
             at = pl.multiple_of((g * n + (place_ref[0] ^ k)) * tiles, 16)
@@ -422,7 +427,6 @@
         at = mid + SLOT_ROWS
         far_rows = [(2, 0, mid, 0), (3, mid, mid, at)]
         third_rows = [(3, 0, mid, 0), (2, mid, mid, at)]
-        note_parts = [near, top, bottom]
     else:
         chunk = lax.dynamic_slice_in_dim(frozen_weight, core * half + chip * width, width, 1)
         near = xor_permute(chunk, "mp", 1)
@@ -444,16 +448,19 @@
         )(task_share, seq_slot, task_codes, hyper_weight)[0]
         got = lax.all_to_all(sent, "dp", 0, 0, tiled=True)
         chosen = call(
-            functools.partial(choose_kernel, tiles, members),
-            [sds((groups * seqs * (tiles + 1), LANES), BF16)] * members,
+            functools.partial(choose_kernel, tiles),
+            [
+                sds((groups * seqs * (tiles + 1) + (far.shape[0] if k == 1 else 0), LANES), BF16)
+                for k in range(members)
+            ],
             n_smem=1,
-            n_in=members,
+            n_in=3,
             nbytes=8 * hyper_weight.size,
-        )(seq_slot, *note_parts, got)
+        )(seq_slot, near, far, got)
         near_held, far, chosen = tied(near_held, far, chosen)
-        third = xor_permute(far, "mp", 1)
         near_pieces = forwarded(near_held, True)
         adapt = [chosen[0]] + [xor_permute(chosen[k], "mp", k) for k in range(1, members)]
+        third = adapt[1][: far.shape[0]]
     else:
         near_pieces = forwarded(near_held, True)
         slots = lax.all_to_all(

time: 105 us -> 101 us (0.962)
  waiting for transfers between devices: 29.1 us -> 20.3 us
  starting transfers between devices: 23.6 us -> 27.8 us
  blocking collectives: 23.2 us -> 24.3 us
    ppermute x18 -> x17, waiting for transfers between devices: 29.1 us -> 20.3 us  [xor_permute(): lax.ppermute(array, axis, [(i, i ^ mask) for i in range(lax.axis_size(axi...]
    ppermute x18 -> x17, starting transfers between devices: 19.1 us -> 23.4 us  [xor_permute(): lax.ppermute(array, axis, [(i, i ^ mask) for i in range(lax.axis_size(axi...]
    all_to_all x1, blocking collectives: 23.2 us -> 24.3 us  [shards(): routed = lax.all_to_all(grads, ('dp', 'mp'), 0, 0, tiled=True)]
    unnamed x26 -> x19, local copies, waits for them, and re-layouts: 2.44 us -> 2.71 us
  transfers between devices with their start and end apart: 19 -> 18, of which waited for: 8 -> 6; matrix products, arithmetic and copies ran while one was open for 1% -> 2% of each run, Pallas kernels for 17% -> 18%
where the time goes in v4:
time: 101 us; the launch traced here: 100 us
  starting transfers between devices  27.8 us (28%)
  blocking collectives  24.3 us (24%)
  Pallas kernels  24.1 us (24%)
  waiting for transfers between devices  20.3 us (20%)
  local copies, waits for them, and re-layouts  2.75 us (3%)
    all_to_all x1, blocking collectives, shards(): routed = lax.all_to_all(grads, ('dp', 'mp'), 0, 0, tiled=True)  24.3 us
    ppermute x17, starting transfers between devices, xor_permute(): lax.ppermute(array, axis, [(i, i ^ mask) for i in range(lax.axis_size(axi...  23.4 us
    ppermute x17, waiting for transfers between devices, xor_permute(): lax.ppermute(array, axis, [(i, i ^ mask) for i in range(lax.axis_size(axi...  20.3 us
    pallas_call x1, Pallas kernels, shards(): call(middle, [sds((tok_dev, half), F32)] * 2 + low_outs + [sds((width_h,...  6.98 us
    pallas_call x3, Pallas kernels, frozen_call(): call(functools.partial(frozen_kernel, len(tokens), depth, weight is not N...  6.95 us
    all_to_all x1, starting transfers between devices, shards(): got = lax.all_to_all(sent, 'dp', 0, 0, tiled=True)  4.32 us
    unnamed x19, local copies, waits for them, and re-layouts  2.71 us
    pallas_call x1, Pallas kernels, shards(): pl.pallas_call(chunk_kernel, in_specs=[pl.BlockSpec(memory_space=pltpu.SM...  2.66 us
  transfers between devices with their start and end apart: 18, of which 6 were waited for; matrix products, arithmetic and copies ran while one was open for 2% of the time, Pallas kernels for 18%

profile of v4, /device:TPU:1, one launch (start us, length us, event | category | flops | bytes accessed | tf_op | source)
XLA Modules:
  0.0 100.1 jit_solution(16063572342269782708)
XLA Ops:
  0.7 2.7 %shard_map.82 = (bf16[1296,128]{1,0:T(8,128)(2,1)}, bf16[656,128]{1,0:T(8,128)(2,1)}, bf16[656,128]{1,0:T(8,128)(2,1)}) custom-call(s32[4]{0:T(128)} %pad_add_fusion.place_ref.refs_0_, s32[2]{0:T(128)} %slot_ref.5, bf16[1280,1024]{1,0:T(8,128)(2,1)} %refs_2_.1), custom_call_target="tpu_custom_call" | custom-call | tf_op jit(solution)/shard_map/pallas_call | solution.py:408
  3.4 2.8 %collective-permute-start.1 = (bf16[1296,128]{1,0:T(8,128)(2,1)}, bf16[1296,128]{1,0:T(8,128)(2,1)}, u32[]{:S(2)}, u32[]{:S(2)}) collective-permute-start(bf16[1296,128]{1,0:T(8,128)(2,1)} %get-tuple-element.52), channel_id=1, source_target_pairs={{0,1},{1,0},{2,3},{3,2},{4,5},{5,4},{6,7},{7,6},{8,9},{9,8},{10,11... | collective-permute-start | bytes 995336 | tf_op jit(solution)/shard_map/ppermute | solution.py:61
  6.2 2.3 %collective-permute-start.4 = (bf16[656,128]{1,0:T(8,128)(2,1)}, bf16[656,128]{1,0:T(8,128)(2,1)}, u32[]{:S(2)}, u32[]{:S(2)}) collective-permute-start(bf16[656,128]{1,0:T(8,128)(2,1)} %get-tuple-element.53), channel_id=1, source_target_pairs={{0,2},{1,3},{2,0},{3,1},{4,6},{5,7},{6,4},{7,5},{8,10},{9,11},{10,... | collective-permute-start | bytes 503816 | tf_op jit(solution)/shard_map/ppermute | solution.py:61
  8.5 2.0 %shard_map.83 = bf16[8,208,128]{2,1,0:T(8,128)(2,1)} custom-call(s32[8]{0:T(128)S(1)} %copy-done.7, s32[2]{0:T(128)S(1)} %copy-done.6, bf16[16,128]{1,0:T(8,128)(2,1)S(1)} %copy-done.5, bf16[128,6144]{1,0:T(8,128)(2,1)S(1)} %copy-done.2), custom_call_target="tpu_custom_call" | custom-call | flops 50331648 | bytes 3145728 | tf_op jit(solution)/shard_map/pallas_call | solution.py:440
  10.5 4.3 %all-to-all-start = ((bf16[8,208,128]{2,1,0:T(8,128)(2,1)}), bf16[8,208,128]{2,1,0:T(8,128)(2,1)S(1)}, u32[]{:S(2)}, u32[]{:S(2)}) async-start(bf16[8,208,128]{2,1,0:T(8,128)(2,1)} %shard_map.83), calls=%async_computation | async-start | bytes 851968 | tf_op jit(solution)/shard_map/all_to_all | solution.py:449
  14.8 3.4 %collective-permute-done.1.near_ref.refs_3_ = bf16[1296,128]{1,0:T(8,128)(2,1)} collective-permute-done((bf16[1296,128]{1,0:T(8,128)(2,1)}, bf16[1296,128]{1,0:T(8,128)(2,1)}, u32[]{:S(2)}, u32[]{:S(2)}) %collective-permute-start.1) | collective-permute-done | bytes 331808 | tf_op jit(solution)/shard_map/ppermute | solution.py:61
  18.2 1.3 %collective-permute-start.2 = (bf16[1296,128]{1,0:T(8,128)(2,1)}, bf16[1296,128]{1,0:T(8,128)(2,1)}, u32[]{:S(2)}, u32[]{:S(2)}) collective-permute-start(bf16[1296,128]{1,0:T(8,128)(2,1)} %collective-permute-done.1.near_ref.refs_3_), channel_id=1, source_target_pairs={{0,8},{4,12},{8,0},{12,4},{16,24},{20,28},{24,16},{28,20},{1,9},{5... | collective-permute-start | bytes 995336 | tf_op jit(solution)/shard_map/ppermute | solution.py:61
  19.5 1.1 %collective-permute-start.3 = (bf16[1296,128]{1,0:T(8,128)(2,1)}, bf16[1296,128]{1,0:T(8,128)(2,1)}, u32[]{:S(2)}, u32[]{:S(2)}) collective-permute-start(bf16[1296,128]{1,0:T(8,128)(2,1)} %collective-permute-done.1.near_ref.refs_3_), channel_id=1, source_target_pairs={{0,16},{4,20},{8,24},{12,28},{16,0},{20,4},{24,8},{28,12},{1,17},{... | collective-permute-start | bytes 995336 | tf_op jit(solution)/shard_map/ppermute | solution.py:61
  20.6 3.3 %collective-permute-start.5 = (bf16[656,128]{1,0:T(8,128)(2,1)}, bf16[656,128]{1,0:T(8,128)(2,1)S(1)}, u32[]{:S(2)}, u32[]{:S(2)}) collective-permute-start(bf16[656,128]{1,0:T(8,128)(2,1)} %get-tuple-element.54), channel_id=1, source_target_pairs={{0,3},{1,2},{2,1},{3,0},{4,7},{5,6},{6,5},{7,4},{8,11},{9,10},{10,... | collective-permute-start | bytes 503816 | tf_op jit(solution)/shard_map/ppermute | solution.py:61
  24.9 2.1 %collective-permute-done.5 = bf16[656,128]{1,0:T(8,128)(2,1)S(1)} collective-permute-done((bf16[656,128]{1,0:T(8,128)(2,1)}, bf16[656,128]{1,0:T(8,128)(2,1)S(1)}, u32[]{:S(2)}, u32[]{:S(2)}) %collective-permute-start.5) | collective-permute-done | bytes 167968 | tf_op jit(solution)/shard_map/ppermute | solution.py:61
  27.1 1.2 %shard_map.84 = (bf16[784,128]{1,0:T(8,128)(2,1)S(1)}, bf16[2096,128]{1,0:T(8,128)(2,1)S(1)}, bf16[784,128]{1,0:T(8,128)(2,1)S(1)}, bf16[784,128]{1,0:T(8,128)(2,1)S(1)}) custom-call(s32[2]{0:T(128)S(1)} %copy-done.6, bf16[1296,128]{1,0:T(8,128)(2,1)} %collective-permute-done.1.near_ref.refs_3_, ...), custom_call_target="tpu_custom_call" | custom-call | bytes 6291456 | tf_op jit(solution)/shard_map/pallas_call | solution.py:450
  29.5 2.5 %collective-permute-start.12 = (bf16[784,128]{1,0:T(8,128)(2,1)S(1)}, bf16[784,128]{1,0:T(8,128)(2,1)S(1)}, u32[]{:S(2)}, u32[]{:S(2)}) collective-permute-start(bf16[784,128]{1,0:T(8,128)(2,1)S(1)} %get-tuple-element.67), channel_id=1, source_target_pairs={{0,2},{1,3},{2,0},{3,1},{4,6},{5,7},{6,4},{7,5},{8,10},{9,11},{10,... | collective-permute-start | bytes 602120 | tf_op jit(solution)/shard_map/ppermute | solution.py:61
  33.7 13.1 %collective-permute-done.6.refs_14_ = bf16[2096,128]{1,0:T(8,128)(2,1)S(1)} collective-permute-done((bf16[2096,128]{1,0:T(8,128)(2,1)S(1)}, bf16[2096,128]{1,0:T(8,128)(2,1)S(1)}, u32[]{:S(2)}, u32[]{:S(2)}) %collective-permute-start.6) | collective-permute-done | bytes 536608 | tf_op jit(solution)/shard_map/ppermute | solution.py:61
  47.6 2.7 %collective-permute-start.13 = (bf16[784,128]{1,0:T(8,128)(2,1)S(1)}, bf16[784,128]{1,0:T(8,128)(2,1)S(1)}, u32[]{:S(2)}, u32[]{:S(2)}) collective-permute-start(bf16[784,128]{1,0:T(8,128)(2,1)S(1)} %get-tuple-element.68), channel_id=1, source_target_pairs={{0,3},{1,2},{2,1},{3,0},{4,7},{5,6},{6,5},{7,4},{8,11},{9,10},{10,... | collective-permute-start | bytes 602120 | tf_op jit(solution)/shard_map/ppermute | solution.py:61
  50.3 1.7 %copy-done.1 = bf16[1280,1024]{1,0:T(8,128)(2,1)S(1)} copy-done((bf16[1280,1024]{1,0:T(8,128)(2,1)S(1)}, bf16[1280,1024]{1,0:T(8,128)(2,1)}, u32[]{:S(2)}) %copy-start.1) | copy-done | bytes 2621464
  52.1 3.6 %shard_map.85 = (f32[256,512]{1,0:T(8,128)S(1)}, f32[256,512]{1,0:T(8,128)S(1)}) custom-call(s32[4]{0:T(128)S(1)} %copy-done.4, bf16[256,5120]{1,0:T(8,128)(2,1)S(1)} %copy-done, bf16[256,5120]{1,0:T(8,128)(2,1)} %collective-permute-done.refs_1_.refs_4_.refs_0_, bf16[1280,1024]{1,0:T(8,128)(2,1)S(1)} %copy-done.1, ...), custom_call_target="tpu_custom_call" | custom-call | flops 1350565888 | bytes 2375680 | tf_op jit(solution)/shard_map/pallas_call | solution.py:269
  55.7 1.2 %collective-permute-start.14 = (bf16[1312,128]{1,0:T(8,128)(2,1)S(1)}, bf16[1312,128]{1,0:T(8,128)(2,1)S(1)}, u32[]{:S(2)}, u32[]{:S(2)}) collective-permute-start(bf16[1312,128]{1,0:T(8,128)(2,1)S(1)} %collective-permute-done.10.refs_7_), channel_id=1, source_target_pairs={{0,8},{4,12},{8,0},{12,4},{16,24},{20,28},{24,16},{28,20},{1,9},{5... | collective-permute-start | bytes 1007624 | tf_op jit(solution)/shard_map/ppermute | solution.py:61
  57.5 7.0 %shard_map.86 = (f32[256,512]{1,0:T(8,128)S(1)}, f32[256,512]{1,0:T(8,128)S(1)}, bf16[256,128]{1,0:T(8,128)(2,1)S(1)}, bf16[2,128,1024]{2,1,0:T(8,128)(2,1)S(1)}...) custom-call(s32[4]{0:T(128)S(1)} %copy-done.4, s32[8]{0:T(128)S(1)} %copy-done.7, ...), custom_call_target="tpu_custom_call" | custom-call | tf_op jit(solution)/shard_map/pallas_call | solution.py:520
  64.6 2.3 %shard_map.88 = f32[256,512]{1,0:T(8,128)S(1)} custom-call(s32[4]{0:T(128)S(1)} %copy-done.4, bf16[256,5120]{1,0:T(8,128)(2,1)} %collective-permute-done.refs_1_.refs_4_.refs_0_, bf16[1312,128]{1,0:T(8,128)(2,1)S(1)} %collective-permute-done.14.refs_1_, bf16[1312,128]{1,0:T(8,128)(2,1)S(1)} %collective-permute-done.15.refs_2_, ...), custom_call_target="tpu_custom_call" | custom-call | flops 171966464 | bytes 1196032 | tf_op jit(solution)/shard_map/pallas_call | solution.py:269
  66.9 3.0 %collective-permute-start.16 = (f32[256,512]{1,0:T(8,128)S(1)}, f32[256,512]{1,0:T(8,128)S(1)}, u32[]{:S(2)}, u32[]{:S(2)}) collective-permute-start(f32[256,512]{1,0:T(8,128)S(1)} %shard_map.88), channel_id=1, source_target_pairs={{0,4},{4,0},{8,12},{12,8},{16,20},{20,16},{24,28},{28,24},{1,5},{5... | collective-permute-start | bytes 1572872 | tf_op jit(solution)/shard_map/ppermute | solution.py:61
  69.9 1.1 %shard_map.87.mine_ref = f32[256,512]{1,0:T(8,128)S(1)} custom-call(s32[4]{0:T(128)S(1)} %copy-done.4, bf16[256,5120]{1,0:T(8,128)(2,1)S(1)} %copy-done, bf16[1312,128]{1,0:T(8,128)(2,1)S(1)} %collective-permute-done.14.refs_1_, bf16[1312,128]{1,0:T(8,128)(2,1)S(1)} %collective-permute-done.15.refs_2_, f32[256,512]{1,0:T(8,128)S(1)} %get-tuple-element.82.refs_3_), custom_call_target="tpu_custom_call" | custom-call | flops 171966464 | bytes 1196032 | tf_op jit(solution)/shard_map/pallas_call | solution.py:269
  71.4 2.3 %shard_map.89 = bf16[32,2,48,128]{3,2,1,0:T(8,128)(2,1)S(1)} custom-call(s32[4]{0:T(128)S(1)} %copy-done.4, s32[8]{0:T(128)S(1)} %copy-done.7, s32[2]{0:T(128)S(1)} %copy-done.6, s32[16]{0:T(128)S(1)} %copy-done.8, f32[256,512]{1,0:T(8,128)S(1)} %shard_map.87.mine_ref, f32[256,512]{1,0:T(8,128)S(1)} %collective-permute-done.16.theirs_ref, ...), custom_call_target="tpu_custom_call" | custom-call | flops 1342177280 | bytes 5242880 | tf_op jit(solution)/shard_map/pallas_call | solution.py:555
  73.7 24.3 %all_to_all.10.grads_ref = bf16[32,2,48,128]{3,2,1,0:T(8,128)(2,1)S(1)} all-to-all(bf16[32,2,48,128]{3,2,1,0:T(8,128)(2,1)S(1)} %shard_map.89), channel_id=1, replica_groups=mesh['dp'=8,'mp'=4] {'dp','mp'}, dimensions={0} | all-to-all | bytes 1572864 | tf_op jit(solution)/shard_map/all_to_all | solution.py:570
  98.0 2.0 %shard_map.90 = f32[128,6144]{1,0:T(8,128)} custom-call(bf16[128,64]{1,0:T(8,128)(2,1)S(1)} %get-tuple-element.81.codes_t_ref, bf16[32,2,48,128]{3,2,1,0:T(8,128)(2,1)S(1)} %all_to_all.10.grads_ref), custom_call_target="tpu_custom_call" | custom-call | tf_op jit(solution)/shard_map/pallas_call | solution.py:572
  (44 shorter events, 6.4 us)
Async XLA Ops:
  0.0 8.5 %copy-start.6 = (s32[2]{0:T(128)S(1)}, s32[2]{0:T(128)}, u32[]{:S(2)}) copy-start(s32[2]{0:T(128)} %slot_ref.5) | copy-start | bytes 28
  0.0 8.5 %copy-start.5 = (bf16[16,128]{1,0:T(8,128)(2,1)S(1)}, bf16[16,128]{1,0:T(8,128)(2,1)}, u32[]{:S(2)}) copy-start(bf16[16,128]{1,0:T(8,128)(2,1)} %refs_2_.2) | copy-start | bytes 12292
  0.0 8.5 %copy-start.7 = (s32[8]{0:T(128)S(1)}, s32[8]{0:T(128)}, u32[]{:S(2)}) copy-start(s32[8]{0:T(128)} %share_ref.3) | copy-start | bytes 100
  0.0 8.5 %collective-permute-start = (bf16[256,5120]{1,0:T(8,128)(2,1)}, bf16[256,5120]{1,0:T(8,128)(2,1)}, u32[]{:S(2)}, u32[]{:S(2)}) collective-permute-start(bf16[256,5120]{1,0:T(8,128)(2,1)} %refs_0_.3), channel_id=1, source_target_pairs={{0,4},{4,0},{8,12},{12,8},{16,20},{20,16},{24,28},{28,24},{1,5},{5... | collective-permute-start | bytes 7864328 | tf_op jit(solution)/shard_map/ppermute | solution.py:61
  0.1 8.4 %copy-start.2 = (bf16[128,6144]{1,0:T(8,128)(2,1)S(1)}, bf16[128,6144]{1,0:T(8,128)(2,1)}, u32[]{:S(2)}) copy-start(bf16[128,6144]{1,0:T(8,128)(2,1)} %weight_ref.3) | copy-start | bytes 4718596
  3.3 47.0 %copy-start = (bf16[256,5120]{1,0:T(8,128)(2,1)S(1)}, bf16[256,5120]{1,0:T(8,128)(2,1)}, u32[]{:S(2)}) copy-start(bf16[256,5120]{1,0:T(8,128)(2,1)} %refs_0_.3) | copy-start | bytes 7864324
  3.4 47.0 %copy-start.4 = (s32[4]{0:T(128)S(1)}, s32[4]{0:T(128)}, u32[]{:S(2)}) copy-start(s32[4]{0:T(128)} %pad_add_fusion.place_ref.refs_0_) | copy-start | bytes 52
  3.4 14.9 %collective-permute-start.1 = (bf16[1296,128]{1,0:T(8,128)(2,1)}, bf16[1296,128]{1,0:T(8,128)(2,1)}, u32[]{:S(2)}, u32[]{:S(2)}) collective-permute-start(bf16[1296,128]{1,0:T(8,128)(2,1)} %get-tuple-element.52), channel_id=1, source_target_pairs={{0,1},{1,0},{2,3},{3,2},{4,5},{5,4},{6,7},{7,6},{8,9},{9,8},{10,11... | collective-permute-start | bytes 995336 | tf_op jit(solution)/shard_map/ppermute | solution.py:61
  6.2 17.8 %collective-permute-start.4 = (bf16[656,128]{1,0:T(8,128)(2,1)}, bf16[656,128]{1,0:T(8,128)(2,1)}, u32[]{:S(2)}, u32[]{:S(2)}) collective-permute-start(bf16[656,128]{1,0:T(8,128)(2,1)} %get-tuple-element.53), channel_id=1, source_target_pairs={{0,2},{1,3},{2,0},{3,1},{4,6},{5,7},{6,4},{7,5},{8,10},{9,11},{10,... | collective-permute-start | bytes 503816 | tf_op jit(solution)/shard_map/ppermute | solution.py:61
  10.5 16.5 %all-to-all-start = ((bf16[8,208,128]{2,1,0:T(8,128)(2,1)}), bf16[8,208,128]{2,1,0:T(8,128)(2,1)S(1)}, u32[]{:S(2)}, u32[]{:S(2)}) async-start(bf16[8,208,128]{2,1,0:T(8,128)(2,1)} %shard_map.83), calls=%async_computation | async-start | bytes 851968 | tf_op jit(solution)/shard_map/all_to_all | solution.py:449
  18.2 10.7 %collective-permute-start.2 = (bf16[1296,128]{1,0:T(8,128)(2,1)}, bf16[1296,128]{1,0:T(8,128)(2,1)}, u32[]{:S(2)}, u32[]{:S(2)}) collective-permute-start(bf16[1296,128]{1,0:T(8,128)(2,1)} %collective-permute-done.1.near_ref.refs_3_), channel_id=1, source_target_pairs={{0,8},{4,12},{8,0},{12,4},{16,24},{20,28},{24,16},{28,20},{1,9},{5... | collective-permute-start | bytes 995336 | tf_op jit(solution)/shard_map/ppermute | solution.py:61
  19.5 9.9 %collective-permute-start.3 = (bf16[1296,128]{1,0:T(8,128)(2,1)}, bf16[1296,128]{1,0:T(8,128)(2,1)}, u32[]{:S(2)}, u32[]{:S(2)}) collective-permute-start(bf16[1296,128]{1,0:T(8,128)(2,1)} %collective-permute-done.1.near_ref.refs_3_), channel_id=1, source_target_pairs={{0,16},{4,20},{8,24},{12,28},{16,0},{20,4},{24,8},{28,12},{1,17},{... | collective-permute-start | bytes 995336 | tf_op jit(solution)/shard_map/ppermute | solution.py:61
  20.6 6.4 %collective-permute-start.5 = (bf16[656,128]{1,0:T(8,128)(2,1)}, bf16[656,128]{1,0:T(8,128)(2,1)S(1)}, u32[]{:S(2)}, u32[]{:S(2)}) collective-permute-start(bf16[656,128]{1,0:T(8,128)(2,1)} %get-tuple-element.54), channel_id=1, source_target_pairs={{0,3},{1,2},{2,1},{3,0},{4,7},{5,6},{6,5},{7,4},{8,11},{9,10},{10,... | collective-permute-start | bytes 503816 | tf_op jit(solution)/shard_map/ppermute | solution.py:61
  29.4 17.3 %collective-permute-start.6 = (bf16[2096,128]{1,0:T(8,128)(2,1)S(1)}, bf16[2096,128]{1,0:T(8,128)(2,1)S(1)}, u32[]{:S(2)}, u32[]{:S(2)}) collective-permute-start(bf16[2096,128]{1,0:T(8,128)(2,1)S(1)} %get-tuple-element.59), channel_id=1, source_target_pairs={{0,1},{1,0},{2,3},{3,2},{4,5},{5,4},{6,7},{7,6},{8,9},{9,8},{10,11... | collective-permute-start | bytes 1609736 | tf_op jit(solution)/shard_map/ppermute | solution.py:61
  29.5 17.4 %collective-permute-start.12 = (bf16[784,128]{1,0:T(8,128)(2,1)S(1)}, bf16[784,128]{1,0:T(8,128)(2,1)S(1)}, u32[]{:S(2)}, u32[]{:S(2)}) collective-permute-start(bf16[784,128]{1,0:T(8,128)(2,1)S(1)} %get-tuple-element.67), channel_id=1, source_target_pairs={{0,2},{1,3},{2,0},{3,1},{4,6},{5,7},{6,4},{7,5},{8,10},{9,11},{10,... | collective-permute-start | bytes 602120 | tf_op jit(solution)/shard_map/ppermute | solution.py:61
  31.9 15.7 %collective-permute-start.11 = (bf16[1296,128]{1,0:T(8,128)(2,1)}, bf16[1296,128]{1,0:T(8,128)(2,1)S(1)}, u32[]{:S(2)}, u32[]{:S(2)}) collective-permute-start(bf16[1296,128]{1,0:T(8,128)(2,1)} %collective-permute-done.2.refs_4_), channel_id=1, source_target_pairs={{0,16},{4,20},{8,24},{12,28},{16,0},{20,4},{24,8},{28,12},{1,17},{... | collective-permute-start | bytes 995336 | tf_op jit(solution)/shard_map/ppermute | solution.py:61
  32.7 23.0 %collective-permute-start.10 = (bf16[1312,128]{1,0:T(8,128)(2,1)S(1)}, bf16[1312,128]{1,0:T(8,128)(2,1)S(1)}, u32[]{:S(2)}, u32[]{:S(2)}) collective-permute-start(bf16[1312,128]{1,0:T(8,128)(2,1)S(1)} %constant_dynamic-update-slice_fusion.far_ref.refs_5_), channel_id=1, source_target_pairs={{0,16},{4,20},{8,24},{12,28},{16,0},{20,4},{24,8},{28,12},{1,17},{... | collective-permute-start | bytes 1007624 | tf_op jit(solution)/shard_map/ppermute | solution.py:61
  33.4 22.3 %collective-permute-start.9 = (bf16[1312,128]{1,0:T(8,128)(2,1)S(1)}, bf16[1312,128]{1,0:T(8,128)(2,1)S(1)}, u32[]{:S(2)}, u32[]{:S(2)}) collective-permute-start(bf16[1312,128]{1,0:T(8,128)(2,1)S(1)} %constant_dynamic-update-slice_fusion.far_ref.refs_5_), channel_id=1, source_target_pairs={{0,8},{4,12},{8,0},{12,4},{16,24},{20,28},{24,16},{28,20},{1,9},{5... | collective-permute-start | bytes 1007624 | tf_op jit(solution)/shard_map/ppermute | solution.py:61
  46.8 8.9 %collective-permute-start.7 = (bf16[1312,128]{1,0:T(8,128)(2,1)S(1)}, bf16[1312,128]{1,0:T(8,128)(2,1)S(1)}, u32[]{:S(2)}, u32[]{:S(2)}) collective-permute-start(bf16[1312,128]{1,0:T(8,128)(2,1)S(1)} %slice.4.refs_8_), channel_id=1, source_target_pairs={{0,8},{4,12},{8,0},{12,4},{16,24},{20,28},{24,16},{28,20},{1,9},{5... | collective-permute-start | bytes 1007624 | tf_op jit(solution)/shard_map/ppermute | solution.py:61
  46.9 8.9 %collective-permute-start.8 = (bf16[1312,128]{1,0:T(8,128)(2,1)S(1)}, bf16[1312,128]{1,0:T(8,128)(2,1)S(1)}, u32[]{:S(2)}, u32[]{:S(2)}) collective-permute-start(bf16[1312,128]{1,0:T(8,128)(2,1)S(1)} %slice.4.refs_8_), channel_id=1, source_target_pairs={{0,16},{4,20},{8,24},{12,28},{16,0},{20,4},{24,8},{28,12},{1,17},{... | collective-permute-start | bytes 1007624 | tf_op jit(solution)/shard_map/ppermute | solution.py:61
  47.6 8.1 %collective-permute-start.13 = (bf16[784,128]{1,0:T(8,128)(2,1)S(1)}, bf16[784,128]{1,0:T(8,128)(2,1)S(1)}, u32[]{:S(2)}, u32[]{:S(2)}) collective-permute-start(bf16[784,128]{1,0:T(8,128)(2,1)S(1)} %get-tuple-element.68), channel_id=1, source_target_pairs={{0,3},{1,2},{2,1},{3,0},{4,7},{5,6},{6,5},{7,4},{8,11},{9,10},{10,... | collective-permute-start | bytes 602120 | tf_op jit(solution)/shard_map/ppermute | solution.py:61
  55.7 8.8 %collective-permute-start.14 = (bf16[1312,128]{1,0:T(8,128)(2,1)S(1)}, bf16[1312,128]{1,0:T(8,128)(2,1)S(1)}, u32[]{:S(2)}, u32[]{:S(2)}) collective-permute-start(bf16[1312,128]{1,0:T(8,128)(2,1)S(1)} %collective-permute-done.10.refs_7_), channel_id=1, source_target_pairs={{0,8},{4,12},{8,0},{12,4},{16,24},{20,28},{24,16},{28,20},{1,9},{5... | collective-permute-start | bytes 1007624 | tf_op jit(solution)/shard_map/ppermute | solution.py:61
  57.0 7.6 %collective-permute-start.15 = (bf16[1312,128]{1,0:T(8,128)(2,1)S(1)}, bf16[1312,128]{1,0:T(8,128)(2,1)S(1)}, u32[]{:S(2)}, u32[]{:S(2)}) collective-permute-start(bf16[1312,128]{1,0:T(8,128)(2,1)S(1)} %collective-permute-done.7.refs_9_), channel_id=1, source_target_pairs={{0,16},{4,20},{8,24},{12,28},{16,0},{20,4},{24,8},{28,12},{1,17},{... | collective-permute-start | bytes 1007624 | tf_op jit(solution)/shard_map/ppermute | solution.py:61
  66.9 4.5 %collective-permute-start.16 = (f32[256,512]{1,0:T(8,128)S(1)}, f32[256,512]{1,0:T(8,128)S(1)}, u32[]{:S(2)}, u32[]{:S(2)}) collective-permute-start(f32[256,512]{1,0:T(8,128)S(1)} %shard_map.88), channel_id=1, source_target_pairs={{0,4},{4,0},{8,12},{12,8},{16,20},{20,16},{24,28},{28,24},{1,5},{5... | collective-permute-start | bytes 1572872 | tf_op jit(solution)/shard_map/ppermute | solution.py:61
  (3 other events, 10.9 us)

commit v5 on v4

--- a/solution.py
+++ b/solution.py
@@ -221,7 +221,7 @@
                 b4_ref[s, j * R : (j + 1) * R, c * LANES : (c + 1) * LANES] = piece
 
 
-def frozen_kernel(n_tok, depth, own, layout, has_acc, place_ref, *refs):
+def frozen_kernel(n_tok, depth, own, layout, has_acc, packed, place_ref, *refs):
     refs = iter(refs)
     token_refs = [next(refs) for _ in range(n_tok)]
     weight_ref = next(refs) if own else None
@@ -234,6 +234,8 @@
     width = sets[0][0][0][1].shape[1]
 
     def cols(k, first, size):
+        if packed:
+            return slice((k - packed) * depth + first, (k - packed) * depth + first + size)
         return pl.ds(pl.multiple_of((me ^ k) * depth + first, LANES), size)
 
     for tok, acc, out in zip(token_refs, accs, outs):
@@ -261,14 +263,14 @@
     return layout, [x for pieces, _ in sets for _, x in pieces]
 
 
-def frozen_call(place, depth, half, tokens, weight, sets, accs):
+def frozen_call(place, depth, half, tokens, weight, sets, accs, packed=0):
     rows = tokens[0].shape[0]
     layout, flat = frozen_layout(sets)
     size = 2 * rows * sum(x.size for x in flat) + (0 if weight is None else 2 * rows * depth * half)
     weights = [] if weight is None else [weight]
     return call(
         functools.partial(
-            frozen_kernel, len(tokens), depth, weight is not None, layout, bool(accs)
+            frozen_kernel, len(tokens), depth, weight is not None, layout, bool(accs), packed
         ),
         [sds((rows, half), F32)] * len(tokens),
         n_smem=1,
@@ -476,9 +478,11 @@
 
     far_held = direct(far)
     if fits:
+        sets = [(list(near_held.items()), near_rows)]
+        accs = frozen_call(place, depth, half, [tokens, other_tokens], frozen_weight, sets, [])
+        last = chips - 1
+        third, accs, near_last = tied(third, accs, near_pieces[last])
         third_held = direct(third)
-        sets = [(list(near_pieces.items()), near_rows)]
-        accs = frozen_call(place, depth, half, [tokens, other_tokens], frozen_weight, sets, [])
         third_held, far_held, accs, adapt = tied(third_held, far_held, accs, adapt)
         third_pieces = forwarded(third_held, True)
     far_pieces = forwarded(far_held, False)
@@ -495,6 +499,7 @@
     if fits:
         last = chips - 1
         sets = [
+            ([(last, near_last)], near_rows),
             ([(m, far_held[m]) for m in far_held], far_rows),
             ([(m, third_held[m]) for m in third_held], third_rows),
         ]
@@ -508,18 +513,22 @@
             piece_refs, refs = refs[:n_flat], refs[n_flat:]
             acc_refs, refs = refs[:2], refs[2:]
             adapt_refs, refs = refs[:n_adapt], refs[n_adapt:]
-            out_refs, refs = refs[:2], refs[2:]
+            out_refs, late_ref, refs = refs[:2], refs[2], refs[3:]
+            for k in range(2, members):
+                block = pl.ds(pl.multiple_of((place_ref[0] ^ k) * depth, LANES), depth)
+                late_ref[:, (k - 2) * depth : (k - 1) * depth] = token_refs[1][:, block]
             low_rank_kernel(
                 tiles, place_ref, share_ref, codes_ref, adapt_refs, token_refs[0], *refs
             )
             frozen_kernel(
-                2, depth, False, layout, True, place_ref, *token_refs, *piece_refs, *acc_refs,
+                2, depth, False, layout, True, 0, place_ref, *token_refs, *piece_refs, *acc_refs,
                 *out_refs,
             )
 
-        *accs, low, b4, tok_t, codes_t = call(
+        *accs, late_tokens, low, b4, tok_t, codes_t = call(
             middle,
             [sds((tok_dev, half), F32)] * 2
+            + [sds((tok_dev, (members - 2) * depth), BF16)]
             + low_outs
             + [sds((width_h, devices * seqs), BF16)],
             scratch=low_scratch
@@ -531,7 +540,7 @@
             n_in=5 + n_flat + n_adapt,
         )(place, task_share, task_codes, tokens, other_tokens, *flat, *accs, *adapt)
         sets = [([(last, far_pieces[last])], far_rows), ([(last, third_pieces[last])], third_rows)]
-        theirs = frozen_call(place, depth, half, [other_tokens], None, sets, accs[1:])[0]
+        theirs = frozen_call(place, depth, half, [late_tokens], None, sets, accs[1:], 2)[0]
         mine = frozen_call(place, depth, half, [tokens], None, sets, accs[:1])[0]
     else:
         low, b4, tok_t = call(

time: 101 us -> 99.4 us (0.984)
  waiting for transfers between devices: 20.3 us -> 17.1 us
  starting transfers between devices: 27.8 us -> 30.4 us
    ppermute x17, waiting for transfers between devices: 20.3 us -> 17.1 us  [xor_permute(): lax.ppermute(array, axis, [(i, i ^ mask) for i in range(lax.axis_size(axi...]
    ppermute x17, starting transfers between devices: 23.4 us -> 26 us  [xor_permute(): lax.ppermute(array, axis, [(i, i ^ mask) for i in range(lax.axis_size(axi...]
    pallas_call x3, Pallas kernels: 6.95 us -> 5.69 us  [frozen_call(): call(functools.partial(frozen_kernel, len(tokens), depth, weight is not N...]
where the time goes in v5:
time: 99.4 us; the launch traced here: 99 us
  starting transfers between devices  30.4 us (31%)
  blocking collectives  24.6 us (25%)
  Pallas kernels  23.4 us (24%)
  waiting for transfers between devices  17.1 us (17%)
  local copies, waits for them, and re-layouts  2.75 us (3%)
    ppermute x17, starting transfers between devices, xor_permute(): lax.ppermute(array, axis, [(i, i ^ mask) for i in range(lax.axis_size(axi...  26 us
    all_to_all x1, blocking collectives, shards(): routed = lax.all_to_all(grads, ('dp', 'mp'), 0, 0, tiled=True)  24.6 us
    ppermute x17, waiting for transfers between devices, xor_permute(): lax.ppermute(array, axis, [(i, i ^ mask) for i in range(lax.axis_size(axi...  17.1 us
    pallas_call x1, Pallas kernels, shards(): call(middle, [sds((tok_dev, half), F32)] * 2 + [sds((tok_dev, (members -...  7.46 us
    pallas_call x3, Pallas kernels, frozen_call(): call(functools.partial(frozen_kernel, len(tokens), depth, weight is not N...  5.69 us
    all_to_all x1, starting transfers between devices, shards(): got = lax.all_to_all(sent, 'dp', 0, 0, tiled=True)  4.32 us
    unnamed x19, local copies, waits for them, and re-layouts  2.71 us
    pallas_call x1, Pallas kernels, shards(): pl.pallas_call(chunk_kernel, in_specs=[pl.BlockSpec(memory_space=pltpu.SM...  2.66 us
  transfers between devices with their start and end apart: 18, of which 6 were waited for; matrix products, arithmetic and copies ran while one was open for 2% of the time, Pallas kernels for 18%

profile of v5, /device:TPU:1, one launch (start us, length us, event | category | flops | bytes accessed | tf_op | source)
XLA Modules:
  0.0 99.0 jit_solution(8709844818680775093)
XLA Ops:
  0.7 2.7 %shard_map.82 = (bf16[1296,128]{1,0:T(8,128)(2,1)}, bf16[656,128]{1,0:T(8,128)(2,1)}, bf16[656,128]{1,0:T(8,128)(2,1)}) custom-call(s32[4]{0:T(128)} %pad_add_fusion.place_ref.refs_0_, s32[2]{0:T(128)} %slot_ref.5, bf16[1280,1024]{1,0:T(8,128)(2,1)} %refs_2_.1), custom_call_target="tpu_custom_call" | custom-call | tf_op jit(solution)/shard_map/pallas_call | solution.py:410
  3.4 2.8 %collective-permute-start.1 = (bf16[1296,128]{1,0:T(8,128)(2,1)}, bf16[1296,128]{1,0:T(8,128)(2,1)}, u32[]{:S(2)}, u32[]{:S(2)}) collective-permute-start(bf16[1296,128]{1,0:T(8,128)(2,1)} %get-tuple-element.57), channel_id=1, source_target_pairs={{0,1},{1,0},{2,3},{3,2},{4,5},{5,4},{6,7},{7,6},{8,9},{9,8},{10,11... | collective-permute-start | bytes 995336 | tf_op jit(solution)/shard_map/ppermute | solution.py:61
  6.2 2.3 %collective-permute-start.4 = (bf16[656,128]{1,0:T(8,128)(2,1)}, bf16[656,128]{1,0:T(8,128)(2,1)}, u32[]{:S(2)}, u32[]{:S(2)}) collective-permute-start(bf16[656,128]{1,0:T(8,128)(2,1)} %get-tuple-element.58), channel_id=1, source_target_pairs={{0,2},{1,3},{2,0},{3,1},{4,6},{5,7},{6,4},{7,5},{8,10},{9,11},{10,... | collective-permute-start | bytes 503816 | tf_op jit(solution)/shard_map/ppermute | solution.py:61
  8.5 2.0 %shard_map.83 = bf16[8,208,128]{2,1,0:T(8,128)(2,1)} custom-call(s32[8]{0:T(128)S(1)} %copy-done.7, s32[2]{0:T(128)S(1)} %copy-done.6, bf16[16,128]{1,0:T(8,128)(2,1)S(1)} %copy-done.5, bf16[128,6144]{1,0:T(8,128)(2,1)S(1)} %copy-done.2), custom_call_target="tpu_custom_call" | custom-call | flops 50331648 | bytes 3145728 | tf_op jit(solution)/shard_map/pallas_call | solution.py:442
  10.5 4.3 %all-to-all-start = ((bf16[8,208,128]{2,1,0:T(8,128)(2,1)}), bf16[8,208,128]{2,1,0:T(8,128)(2,1)S(1)}, u32[]{:S(2)}, u32[]{:S(2)}) async-start(bf16[8,208,128]{2,1,0:T(8,128)(2,1)} %shard_map.83), calls=%async_computation | async-start | bytes 851968 | tf_op jit(solution)/shard_map/all_to_all | solution.py:451
  14.8 3.4 %collective-permute-done.1.near_ref.refs_3_ = bf16[1296,128]{1,0:T(8,128)(2,1)} collective-permute-done((bf16[1296,128]{1,0:T(8,128)(2,1)}, bf16[1296,128]{1,0:T(8,128)(2,1)}, u32[]{:S(2)}, u32[]{:S(2)}) %collective-permute-start.1) | collective-permute-done | bytes 331808 | tf_op jit(solution)/shard_map/ppermute | solution.py:61
  18.2 1.2 %collective-permute-start.3 = (bf16[1296,128]{1,0:T(8,128)(2,1)}, bf16[1296,128]{1,0:T(8,128)(2,1)}, u32[]{:S(2)}, u32[]{:S(2)}) collective-permute-start(bf16[1296,128]{1,0:T(8,128)(2,1)} %collective-permute-done.1.near_ref.refs_3_), channel_id=1, source_target_pairs={{0,16},{4,20},{8,24},{12,28},{16,0},{20,4},{24,8},{28,12},{1,17},{... | collective-permute-start | bytes 995336 | tf_op jit(solution)/shard_map/ppermute | solution.py:61
  19.4 1.2 %collective-permute-start.2 = (bf16[1296,128]{1,0:T(8,128)(2,1)}, bf16[1296,128]{1,0:T(8,128)(2,1)}, u32[]{:S(2)}, u32[]{:S(2)}) collective-permute-start(bf16[1296,128]{1,0:T(8,128)(2,1)} %collective-permute-done.1.near_ref.refs_3_), channel_id=1, source_target_pairs={{0,8},{4,12},{8,0},{12,4},{16,24},{20,28},{24,16},{28,20},{1,9},{5... | collective-permute-start | bytes 995336 | tf_op jit(solution)/shard_map/ppermute | solution.py:61
  20.6 3.3 %collective-permute-start.5 = (bf16[656,128]{1,0:T(8,128)(2,1)}, bf16[656,128]{1,0:T(8,128)(2,1)S(1)}, u32[]{:S(2)}, u32[]{:S(2)}) collective-permute-start(bf16[656,128]{1,0:T(8,128)(2,1)} %get-tuple-element.59), channel_id=1, source_target_pairs={{0,3},{1,2},{2,1},{3,0},{4,7},{5,6},{6,5},{7,4},{8,11},{9,10},{10,... | collective-permute-start | bytes 503816 | tf_op jit(solution)/shard_map/ppermute | solution.py:61
  24.9 2.1 %collective-permute-done.5 = bf16[656,128]{1,0:T(8,128)(2,1)S(1)} collective-permute-done((bf16[656,128]{1,0:T(8,128)(2,1)}, bf16[656,128]{1,0:T(8,128)(2,1)S(1)}, u32[]{:S(2)}, u32[]{:S(2)}) %collective-permute-start.5) | collective-permute-done | bytes 167968 | tf_op jit(solution)/shard_map/ppermute | solution.py:61
  27.1 1.2 %shard_map.84 = (bf16[784,128]{1,0:T(8,128)(2,1)S(1)}, bf16[2096,128]{1,0:T(8,128)(2,1)S(1)}, bf16[784,128]{1,0:T(8,128)(2,1)S(1)}, bf16[784,128]{1,0:T(8,128)(2,1)S(1)}) custom-call(s32[2]{0:T(128)S(1)} %copy-done.6, bf16[1296,128]{1,0:T(8,128)(2,1)} %collective-permute-done.1.near_ref.refs_3_, ...), custom_call_target="tpu_custom_call" | custom-call | bytes 6291456 | tf_op jit(solution)/shard_map/pallas_call | solution.py:452
  30.9 1.4 %collective-permute-start.10 = (bf16[1312,128]{1,0:T(8,128)(2,1)S(1)}, bf16[1312,128]{1,0:T(8,128)(2,1)S(1)}, u32[]{:S(2)}, u32[]{:S(2)}) collective-permute-start(bf16[1312,128]{1,0:T(8,128)(2,1)S(1)} %constant_dynamic-update-slice_fusion.far_ref.refs_6_), channel_id=1, source_target_pairs={{0,8},{4,12},{8,0},{12,4},{16,24},{20,28},{24,16},{28,20},{1,9},{5... | collective-permute-start | bytes 1007624 | tf_op jit(solution)/shard_map/ppermute | solution.py:61
  32.2 2.0 %collective-permute-start.12 = (bf16[784,128]{1,0:T(8,128)(2,1)S(1)}, bf16[784,128]{1,0:T(8,128)(2,1)S(1)}, u32[]{:S(2)}, u32[]{:S(2)}) collective-permute-start(bf16[784,128]{1,0:T(8,128)(2,1)S(1)} %get-tuple-element.76), channel_id=1, source_target_pairs={{0,2},{1,3},{2,0},{3,1},{4,6},{5,7},{6,4},{7,5},{8,10},{9,11},{10,... | collective-permute-start | bytes 602120 | tf_op jit(solution)/shard_map/ppermute | solution.py:61
  34.2 1.7 %copy-done.1 = bf16[1280,1024]{1,0:T(8,128)(2,1)S(1)} copy-done((bf16[1280,1024]{1,0:T(8,128)(2,1)S(1)}, bf16[1280,1024]{1,0:T(8,128)(2,1)}, u32[]{:S(2)}) %copy-start.1) | copy-done | bytes 2621464
  36.0 3.6 %shard_map.85 = (f32[256,512]{1,0:T(8,128)S(1)}, f32[256,512]{1,0:T(8,128)S(1)}) custom-call(s32[4]{0:T(128)S(1)} %copy-done.4, bf16[256,5120]{1,0:T(8,128)(2,1)S(1)} %copy-done, bf16[256,5120]{1,0:T(8,128)(2,1)} %collective-permute-done.refs_1_.refs_4_, bf16[1280,1024]{1,0:T(8,128)(2,1)S(1)} %copy-done.1, ...), custom_call_target="tpu_custom_call" | custom-call | flops 1180696576 | bytes 2043904 | tf_op jit(solution)/shard_map/pallas_call | solution.py:271
  39.6 5.3 %collective-permute-done.6.refs_15_ = bf16[2096,128]{1,0:T(8,128)(2,1)S(1)} collective-permute-done((bf16[2096,128]{1,0:T(8,128)(2,1)S(1)}, bf16[2096,128]{1,0:T(8,128)(2,1)S(1)}, u32[]{:S(2)}, u32[]{:S(2)}) %collective-permute-start.6) | collective-permute-done | bytes 536608 | tf_op jit(solution)/shard_map/ppermute | solution.py:61
  44.9 1.9 %collective-permute-start.9 = (bf16[1312,128]{1,0:T(8,128)(2,1)S(1)}, bf16[1312,128]{1,0:T(8,128)(2,1)S(1)}, u32[]{:S(2)}, u32[]{:S(2)}) collective-permute-start(bf16[1312,128]{1,0:T(8,128)(2,1)S(1)} %slice.4.refs_9_), channel_id=1, source_target_pairs={{0,16},{4,20},{8,24},{12,28},{16,0},{20,4},{24,8},{28,12},{1,17},{... | collective-permute-start | bytes 1007624 | tf_op jit(solution)/shard_map/ppermute | solution.py:61
  47.6 1.3 %collective-permute-start.13 = (bf16[784,128]{1,0:T(8,128)(2,1)S(1)}, bf16[784,128]{1,0:T(8,128)(2,1)S(1)}, u32[]{:S(2)}, u32[]{:S(2)}) collective-permute-start(bf16[784,128]{1,0:T(8,128)(2,1)S(1)} %get-tuple-element.77), channel_id=1, source_target_pairs={{0,3},{1,2},{2,1},{3,0},{4,7},{5,6},{6,5},{7,4},{8,11},{9,10},{10,... | collective-permute-start | bytes 602120 | tf_op jit(solution)/shard_map/ppermute | solution.py:61
  49.0 5.1 %collective-permute-done.13.refs_17_ = bf16[784,128]{1,0:T(8,128)(2,1)S(1)} collective-permute-done((bf16[784,128]{1,0:T(8,128)(2,1)S(1)}, bf16[784,128]{1,0:T(8,128)(2,1)S(1)}, u32[]{:S(2)}, u32[]{:S(2)}) %collective-permute-start.13) | collective-permute-done | bytes 200736 | tf_op jit(solution)/shard_map/ppermute | solution.py:61
  56.3 7.5 %shard_map.86 = (f32[256,512]{1,0:T(8,128)S(1)}, f32[256,512]{1,0:T(8,128)S(1)}, bf16[256,2560]{1,0:T(8,128)(2,1)S(1)}, bf16[256,128]{1,0:T(8,128)(2,1)S(1)}, bf...) custom-call(s32[4]{0:T(128)S(1)} %copy-done.4, s32[8]{0:T(128)S(1)} %copy-done.7, ...), custom_call_target="tpu_custom_call" | custom-call | tf_op jit(solution)/shard_map/pallas_call | solution.py:528
  64.9 3.6 %collective-permute-start.16 = (f32[256,512]{1,0:T(8,128)S(1)}, f32[256,512]{1,0:T(8,128)S(1)}, u32[]{:S(2)}, u32[]{:S(2)}) collective-permute-start(f32[256,512]{1,0:T(8,128)S(1)} %shard_map.88), channel_id=1, source_target_pairs={{0,4},{4,0},{8,12},{12,8},{16,20},{20,16},{24,28},{28,24},{1,5},{5... | collective-permute-start | bytes 1572872 | tf_op jit(solution)/shard_map/ppermute | solution.py:61
  70.1 2.3 %shard_map.89 = bf16[32,2,48,128]{3,2,1,0:T(8,128)(2,1)S(1)} custom-call(s32[4]{0:T(128)S(1)} %copy-done.4, s32[8]{0:T(128)S(1)} %copy-done.7, s32[2]{0:T(128)S(1)} %copy-done.6, s32[16]{0:T(128)S(1)} %copy-done.8, f32[256,512]{1,0:T(8,128)S(1)} %shard_map.87.mine_ref, f32[256,512]{1,0:T(8,128)S(1)} %collective-permute-done.16.theirs_ref, ...), custom_call_target="tpu_custom_call" | custom-call | flops 1342177280 | bytes 5242880 | tf_op jit(solution)/shard_map/pallas_call | solution.py:564
  72.4 24.6 %all_to_all.10.grads_ref = bf16[32,2,48,128]{3,2,1,0:T(8,128)(2,1)S(1)} all-to-all(bf16[32,2,48,128]{3,2,1,0:T(8,128)(2,1)S(1)} %shard_map.89), channel_id=1, replica_groups=mesh['dp'=8,'mp'=4] {'dp','mp'}, dimensions={0} | all-to-all | bytes 1572864 | tf_op jit(solution)/shard_map/all_to_all | solution.py:579
  96.9 2.0 %shard_map.90 = f32[128,6144]{1,0:T(8,128)} custom-call(bf16[128,64]{1,0:T(8,128)(2,1)S(1)} %get-tuple-element.90.codes_t_ref, bf16[32,2,48,128]{3,2,1,0:T(8,128)(2,1)S(1)} %all_to_all.10.grads_ref), custom_call_target="tpu_custom_call" | custom-call | tf_op jit(solution)/shard_map/pallas_call | solution.py:581
  (44 shorter events, 9.8 us)
Async XLA Ops:
  0.0 8.5 %copy-start.6 = (s32[2]{0:T(128)S(1)}, s32[2]{0:T(128)}, u32[]{:S(2)}) copy-start(s32[2]{0:T(128)} %slot_ref.5) | copy-start | bytes 28
  0.0 8.5 %copy-start.5 = (bf16[16,128]{1,0:T(8,128)(2,1)S(1)}, bf16[16,128]{1,0:T(8,128)(2,1)}, u32[]{:S(2)}) copy-start(bf16[16,128]{1,0:T(8,128)(2,1)} %refs_2_.2) | copy-start | bytes 12292
  0.0 8.5 %copy-start.7 = (s32[8]{0:T(128)S(1)}, s32[8]{0:T(128)}, u32[]{:S(2)}) copy-start(s32[8]{0:T(128)} %share_ref.3) | copy-start | bytes 100
  0.0 8.5 %collective-permute-start = (bf16[256,5120]{1,0:T(8,128)(2,1)}, bf16[256,5120]{1,0:T(8,128)(2,1)}, u32[]{:S(2)}, u32[]{:S(2)}) collective-permute-start(bf16[256,5120]{1,0:T(8,128)(2,1)} %refs_0_.3), channel_id=1, source_target_pairs={{0,4},{4,0},{8,12},{12,8},{16,20},{20,16},{24,28},{28,24},{1,5},{5... | collective-permute-start | bytes 7864328 | tf_op jit(solution)/shard_map/ppermute | solution.py:61
  0.1 8.4 %copy-start.2 = (bf16[128,6144]{1,0:T(8,128)(2,1)S(1)}, bf16[128,6144]{1,0:T(8,128)(2,1)}, u32[]{:S(2)}) copy-start(bf16[128,6144]{1,0:T(8,128)(2,1)} %weight_ref.3) | copy-start | bytes 4718596
  3.3 30.9 %copy-start = (bf16[256,5120]{1,0:T(8,128)(2,1)S(1)}, bf16[256,5120]{1,0:T(8,128)(2,1)}, u32[]{:S(2)}) copy-start(bf16[256,5120]{1,0:T(8,128)(2,1)} %refs_0_.3) | copy-start | bytes 7864324
  3.4 30.9 %copy-start.4 = (s32[4]{0:T(128)S(1)}, s32[4]{0:T(128)}, u32[]{:S(2)}) copy-start(s32[4]{0:T(128)} %pad_add_fusion.place_ref.refs_0_) | copy-start | bytes 52
  3.4 14.9 %collective-permute-start.1 = (bf16[1296,128]{1,0:T(8,128)(2,1)}, bf16[1296,128]{1,0:T(8,128)(2,1)}, u32[]{:S(2)}, u32[]{:S(2)}) collective-permute-start(bf16[1296,128]{1,0:T(8,128)(2,1)} %get-tuple-element.57), channel_id=1, source_target_pairs={{0,1},{1,0},{2,3},{3,2},{4,5},{5,4},{6,7},{7,6},{8,9},{9,8},{10,11... | collective-permute-start | bytes 995336 | tf_op jit(solution)/shard_map/ppermute | solution.py:61
  6.2 17.8 %collective-permute-start.4 = (bf16[656,128]{1,0:T(8,128)(2,1)}, bf16[656,128]{1,0:T(8,128)(2,1)}, u32[]{:S(2)}, u32[]{:S(2)}) collective-permute-start(bf16[656,128]{1,0:T(8,128)(2,1)} %get-tuple-element.58), channel_id=1, source_target_pairs={{0,2},{1,3},{2,0},{3,1},{4,6},{5,7},{6,4},{7,5},{8,10},{9,11},{10,... | collective-permute-start | bytes 503816 | tf_op jit(solution)/shard_map/ppermute | solution.py:61
  10.5 16.5 %all-to-all-start = ((bf16[8,208,128]{2,1,0:T(8,128)(2,1)}), bf16[8,208,128]{2,1,0:T(8,128)(2,1)S(1)}, u32[]{:S(2)}, u32[]{:S(2)}) async-start(bf16[8,208,128]{2,1,0:T(8,128)(2,1)} %shard_map.83), calls=%async_computation | async-start | bytes 851968 | tf_op jit(solution)/shard_map/all_to_all | solution.py:451
  18.2 10.7 %collective-permute-start.3 = (bf16[1296,128]{1,0:T(8,128)(2,1)}, bf16[1296,128]{1,0:T(8,128)(2,1)}, u32[]{:S(2)}, u32[]{:S(2)}) collective-permute-start(bf16[1296,128]{1,0:T(8,128)(2,1)} %collective-permute-done.1.near_ref.refs_3_), channel_id=1, source_target_pairs={{0,16},{4,20},{8,24},{12,28},{16,0},{20,4},{24,8},{28,12},{1,17},{... | collective-permute-start | bytes 995336 | tf_op jit(solution)/shard_map/ppermute | solution.py:61
  19.4 9.5 %collective-permute-start.2 = (bf16[1296,128]{1,0:T(8,128)(2,1)}, bf16[1296,128]{1,0:T(8,128)(2,1)}, u32[]{:S(2)}, u32[]{:S(2)}) collective-permute-start(bf16[1296,128]{1,0:T(8,128)(2,1)} %collective-permute-done.1.near_ref.refs_3_), channel_id=1, source_target_pairs={{0,8},{4,12},{8,0},{12,4},{16,24},{20,28},{24,16},{28,20},{1,9},{5... | collective-permute-start | bytes 995336 | tf_op jit(solution)/shard_map/ppermute | solution.py:61
  20.6 6.4 %collective-permute-start.5 = (bf16[656,128]{1,0:T(8,128)(2,1)}, bf16[656,128]{1,0:T(8,128)(2,1)S(1)}, u32[]{:S(2)}, u32[]{:S(2)}) collective-permute-start(bf16[656,128]{1,0:T(8,128)(2,1)} %get-tuple-element.59), channel_id=1, source_target_pairs={{0,3},{1,2},{2,1},{3,0},{4,7},{5,6},{6,5},{7,4},{8,11},{9,10},{10,... | collective-permute-start | bytes 503816 | tf_op jit(solution)/shard_map/ppermute | solution.py:61
  29.0 15.9 %collective-permute-start.6 = (bf16[2096,128]{1,0:T(8,128)(2,1)S(1)}, bf16[2096,128]{1,0:T(8,128)(2,1)S(1)}, u32[]{:S(2)}, u32[]{:S(2)}) collective-permute-start(bf16[2096,128]{1,0:T(8,128)(2,1)S(1)} %get-tuple-element.64), channel_id=1, source_target_pairs={{0,1},{1,0},{2,3},{3,2},{4,5},{5,4},{6,7},{7,6},{8,9},{9,8},{10,11... | collective-permute-start | bytes 1609736 | tf_op jit(solution)/shard_map/ppermute | solution.py:61
  29.4 15.5 %collective-permute-start.7 = (bf16[1296,128]{1,0:T(8,128)(2,1)}, bf16[1296,128]{1,0:T(8,128)(2,1)S(1)}, u32[]{:S(2)}, u32[]{:S(2)}) collective-permute-start(bf16[1296,128]{1,0:T(8,128)(2,1)} %collective-permute-done.2.refs_4_), channel_id=1, source_target_pairs={{0,16},{4,20},{8,24},{12,28},{16,0},{20,4},{24,8},{28,12},{1,17},{... | collective-permute-start | bytes 995336 | tf_op jit(solution)/shard_map/ppermute | solution.py:61
  30.3 23.8 %collective-permute-start.11 = (bf16[1312,128]{1,0:T(8,128)(2,1)S(1)}, bf16[1312,128]{1,0:T(8,128)(2,1)S(1)}, u32[]{:S(2)}, u32[]{:S(2)}) collective-permute-start(bf16[1312,128]{1,0:T(8,128)(2,1)S(1)} %constant_dynamic-update-slice_fusion.far_ref.refs_6_), channel_id=1, source_target_pairs={{0,16},{4,20},{8,24},{12,28},{16,0},{20,4},{24,8},{28,12},{1,17},{... | collective-permute-start | bytes 1007624 | tf_op jit(solution)/shard_map/ppermute | solution.py:61
  30.9 23.2 %collective-permute-start.10 = (bf16[1312,128]{1,0:T(8,128)(2,1)S(1)}, bf16[1312,128]{1,0:T(8,128)(2,1)S(1)}, u32[]{:S(2)}, u32[]{:S(2)}) collective-permute-start(bf16[1312,128]{1,0:T(8,128)(2,1)S(1)} %constant_dynamic-update-slice_fusion.far_ref.refs_6_), channel_id=1, source_target_pairs={{0,8},{4,12},{8,0},{12,4},{16,24},{20,28},{24,16},{28,20},{1,9},{5... | collective-permute-start | bytes 1007624 | tf_op jit(solution)/shard_map/ppermute | solution.py:61
  32.2 15.4 %collective-permute-start.12 = (bf16[784,128]{1,0:T(8,128)(2,1)S(1)}, bf16[784,128]{1,0:T(8,128)(2,1)S(1)}, u32[]{:S(2)}, u32[]{:S(2)}) collective-permute-start(bf16[784,128]{1,0:T(8,128)(2,1)S(1)} %get-tuple-element.76), channel_id=1, source_target_pairs={{0,2},{1,3},{2,0},{3,1},{4,6},{5,7},{6,4},{7,5},{8,10},{9,11},{10,... | collective-permute-start | bytes 602120 | tf_op jit(solution)/shard_map/ppermute | solution.py:61
  44.9 9.2 %collective-permute-start.9 = (bf16[1312,128]{1,0:T(8,128)(2,1)S(1)}, bf16[1312,128]{1,0:T(8,128)(2,1)S(1)}, u32[]{:S(2)}, u32[]{:S(2)}) collective-permute-start(bf16[1312,128]{1,0:T(8,128)(2,1)S(1)} %slice.4.refs_9_), channel_id=1, source_target_pairs={{0,16},{4,20},{8,24},{12,28},{16,0},{20,4},{24,8},{28,12},{1,17},{... | collective-permute-start | bytes 1007624 | tf_op jit(solution)/shard_map/ppermute | solution.py:61
  46.8 7.3 %collective-permute-start.8 = (bf16[1312,128]{1,0:T(8,128)(2,1)S(1)}, bf16[1312,128]{1,0:T(8,128)(2,1)S(1)}, u32[]{:S(2)}, u32[]{:S(2)}) collective-permute-start(bf16[1312,128]{1,0:T(8,128)(2,1)S(1)} %slice.4.refs_9_), channel_id=1, source_target_pairs={{0,8},{4,12},{8,0},{12,4},{16,24},{20,28},{24,16},{28,20},{1,9},{5... | collective-permute-start | bytes 1007624 | tf_op jit(solution)/shard_map/ppermute | solution.py:61
  47.6 6.5 %collective-permute-start.13 = (bf16[784,128]{1,0:T(8,128)(2,1)S(1)}, bf16[784,128]{1,0:T(8,128)(2,1)S(1)}, u32[]{:S(2)}, u32[]{:S(2)}) collective-permute-start(bf16[784,128]{1,0:T(8,128)(2,1)S(1)} %get-tuple-element.77), channel_id=1, source_target_pairs={{0,3},{1,2},{2,1},{3,0},{4,7},{5,6},{6,5},{7,4},{8,11},{9,10},{10,... | collective-permute-start | bytes 602120 | tf_op jit(solution)/shard_map/ppermute | solution.py:61
  54.1 9.7 %collective-permute-start.14 = (bf16[1312,128]{1,0:T(8,128)(2,1)S(1)}, bf16[1312,128]{1,0:T(8,128)(2,1)S(1)}, u32[]{:S(2)}, u32[]{:S(2)}) collective-permute-start(bf16[1312,128]{1,0:T(8,128)(2,1)S(1)} %collective-permute-done.11.refs_8_), channel_id=1, source_target_pairs={{0,8},{4,12},{8,0},{12,4},{16,24},{20,28},{24,16},{28,20},{1,9},{5... | collective-permute-start | bytes 1007624 | tf_op jit(solution)/shard_map/ppermute | solution.py:61
  55.2 8.6 %collective-permute-start.15 = (bf16[1312,128]{1,0:T(8,128)(2,1)S(1)}, bf16[1312,128]{1,0:T(8,128)(2,1)S(1)}, u32[]{:S(2)}, u32[]{:S(2)}) collective-permute-start(bf16[1312,128]{1,0:T(8,128)(2,1)S(1)} %collective-permute-done.8.refs_10_), channel_id=1, source_target_pairs={{0,16},{4,20},{8,24},{12,28},{16,0},{20,4},{24,8},{28,12},{1,17},{... | collective-permute-start | bytes 1007624 | tf_op jit(solution)/shard_map/ppermute | solution.py:61
  64.9 5.2 %collective-permute-start.16 = (f32[256,512]{1,0:T(8,128)S(1)}, f32[256,512]{1,0:T(8,128)S(1)}, u32[]{:S(2)}, u32[]{:S(2)}) collective-permute-start(f32[256,512]{1,0:T(8,128)S(1)} %shard_map.88), channel_id=1, source_target_pairs={{0,4},{4,0},{8,12},{12,8},{16,20},{20,16},{24,28},{28,24},{1,5},{5... | collective-permute-start | bytes 1572872 | tf_op jit(solution)/shard_map/ppermute | solution.py:61
  (3 other events, 12.1 us)

commit v6 on v5

--- a/solution.py
+++ b/solution.py
@@ -149,7 +149,7 @@
 
 def low_rank_kernel(
     tiles, place_ref, share_ref, codes_ref, adapt_refs, tokens_ref,
-    low_ref, b4_ref, tok_t_ref, codes_t_ref, scr, held, table,
+    low_ref, b4_ref, codes_t_ref, scr, held, table,
 ):
     n = len(adapt_refs)
     seqs = b4_ref.shape[0]
@@ -174,10 +174,25 @@
     source = at % per_part // seqs * n + (place_ref[0] ^ (at // per_part))
     order = source * seqs + at % seqs == lax.broadcasted_iota(jnp.int32, (rows, rows), 0)
     codes_t_ref[...] = dot(order.astype(BF16), codes).T.astype(BF16)
-    low_rank_body(held, tokens_ref, low_ref, b4_ref, tok_t_ref, scr)
-
-
-def low_rank_body(adapt_ref, tokens_ref, low_ref, b4_ref, tok_t_ref, scr):
+    low_rank_body(held, tokens_ref, low_ref, b4_ref, scr)
+
+
+def turn_tokens(tokens_ref, tok_t_ref):
+    to = lax.broadcasted_iota(jnp.int32, (BLOCK_D, BLOCK_D), 0)
+    sort = (
+        to % BLOCK_Q * PACK + to // BLOCK_Q
+        == lax.broadcasted_iota(jnp.int32, (BLOCK_D, BLOCK_D), 1)
+    ).astype(BF16)
+    for b in range(D // BLOCK_D):
+        block = tokens_ref[:, b * BLOCK_D : (b + 1) * BLOCK_D]
+        turned = dot_nt(sort, block).astype(BF16)
+        for j in range(PACK):
+            tok_t_ref[
+                b * BLOCK_Q : (b + 1) * BLOCK_Q, j * block.shape[0] : (j + 1) * block.shape[0]
+            ] = turned[j * BLOCK_Q : (j + 1) * BLOCK_Q, :]
+
+
+def low_rank_body(adapt_ref, tokens_ref, low_ref, b4_ref, scr):
     seqs = b4_ref.shape[0]
     lane = lax.broadcasted_iota(jnp.int32, (BLOCK_D, LANES * seqs), 1)
     row = lax.broadcasted_iota(jnp.int32, (BLOCK_D, LANES * seqs), 0)
@@ -185,11 +200,6 @@
     spread = (
         lax.broadcasted_iota(jnp.int32, (BLOCK_D, BLOCK_Q), 0) // PACK
         == lax.broadcasted_iota(jnp.int32, (BLOCK_D, BLOCK_Q), 1)
-    ).astype(BF16)
-    to = lax.broadcasted_iota(jnp.int32, (BLOCK_D, BLOCK_D), 0)
-    sort = (
-        to % BLOCK_Q * PACK + to // BLOCK_Q
-        == lax.broadcasted_iota(jnp.int32, (BLOCK_D, BLOCK_D), 1)
     ).astype(BF16)
     acc = jnp.zeros((tokens_ref.shape[0], LANES * seqs), F32)
     for b in range(D // BLOCK_D):
@@ -200,11 +210,6 @@
         wide = jnp.where(keep, dot(spread, part), 0.0).astype(BF16)
         block = tokens_ref[:, cols]
         acc = acc + dot(block, wide)
-        turned = dot_nt(sort, block).astype(BF16)
-        for j in range(PACK):
-            tok_t_ref[
-                b * BLOCK_Q : (b + 1) * BLOCK_Q, j * block.shape[0] : (j + 1) * block.shape[0]
-            ] = turned[j * BLOCK_Q : (j + 1) * BLOCK_Q, :]
     first = lax.broadcasted_iota(jnp.int32, (SEQ_LEN, LANES), 1) < R
     for s in range(seqs):
         z = acc[s * SEQ_LEN : (s + 1) * SEQ_LEN, s * LANES : (s + 1) * LANES]
@@ -476,10 +481,27 @@
         adapt = lax.all_to_all(sent, ("dp", "mp"), 0, 0, tiled=True)
         adapt = adapt.transpose(1, 0, 2, 3).reshape(seqs, rows, LANES)
 
+    low_outs = [
+        sds((tok_dev, LANES), BF16),
+        sds((seqs, LANES, KV), BF16),
+    ]
+    turned = sds((D // PACK, PACK * tok_dev), BF16)
     far_held = direct(far)
     if fits:
         sets = [(list(near_held.items()), near_rows)]
-        accs = frozen_call(place, depth, half, [tokens, other_tokens], frozen_weight, sets, [])
+        early_layout, flat = frozen_layout(sets)
+
+        def early(place_ref, *refs):
+            *refs, tok_t_ref = refs
+            turn_tokens(refs[0], tok_t_ref)
+            frozen_kernel(2, depth, True, early_layout, False, 0, place_ref, *refs)
+
+        *accs, tok_t = call(
+            early,
+            [sds((tok_dev, half), F32)] * 2 + [turned],
+            n_smem=1,
+            n_in=3 + len(flat),
+        )(place, tokens, other_tokens, frozen_weight, *flat)
         last = chips - 1
         third, accs, near_last = tied(third, accs, near_pieces[last])
         third_held = direct(third)
@@ -487,11 +509,6 @@
         third_pieces = forwarded(third_held, True)
     far_pieces = forwarded(far_held, False)
 
-    low_outs = [
-        sds((tok_dev, LANES), BF16),
-        sds((seqs, LANES, KV), BF16),
-        sds((D // PACK, PACK * tok_dev), BF16),
-    ]
     low_cost = dict(
         flops=4 * tokens.size * LANES * seqs, nbytes=4 * tokens.size + 4 * seqs * rows * LANES
     )
@@ -525,7 +542,7 @@
                 *out_refs,
             )
 
-        *accs, late_tokens, low, b4, tok_t, codes_t = call(
+        *accs, late_tokens, low, b4, codes_t = call(
             middle,
             [sds((tok_dev, half), F32)] * 2
             + [sds((tok_dev, (members - 2) * depth), BF16)]
@@ -543,9 +560,10 @@
         theirs = frozen_call(place, depth, half, [late_tokens], None, sets, accs[1:], 2)[0]
         mine = frozen_call(place, depth, half, [tokens], None, sets, accs[:1])[0]
     else:
-        low, b4, tok_t = call(
-            low_rank_body, low_outs, scratch=low_scratch, n_in=2, **low_cost
-        )(adapt, tokens)
+        low, b4 = call(low_rank_body, low_outs, scratch=low_scratch, n_in=2, **low_cost)(
+            adapt, tokens
+        )
+        tok_t = call(turn_tokens, [turned], n_in=1)(tokens)[0]
         own_half = lax.dynamic_slice_in_dim(frozen_weight, core * half, half, 1)
         order = jnp.arange(chips) ^ chip
         found = {0: own_half}

time: 99.4 us -> 98.8 us (level)
  waiting for transfers between devices: 17.1 us -> 15.2 us
  starting transfers between devices: 30.4 us -> 31.6 us
    pallas_call x0 -> x1, Pallas kernels: none -> 4.99 us  [shards(): call(early, [sds((tok_dev, half), F32)] * 2 + [turned], n_smem=1, n_in=3...]
    pallas_call x3 -> x2, Pallas kernels: 5.69 us -> 2.1 us  [frozen_call(): call(functools.partial(frozen_kernel, len(tokens), depth, weight is not N...]
    ppermute x17, waiting for transfers between devices: 17.1 us -> 15.2 us  [xor_permute(): lax.ppermute(array, axis, [(i, i ^ mask) for i in range(lax.axis_size(axi...]
    pallas_call x1, Pallas kernels: 7.46 us -> 5.69 us  [shards(): call(middle, [sds((tok_dev, half), F32)] * 2 + [sds((tok_dev, (members -...]
    ppermute x17, starting transfers between devices: 26 us -> 27.2 us  [xor_permute(): lax.ppermute(array, axis, [(i, i ^ mask) for i in range(lax.axis_size(axi...]
where the time goes in v6:
time: 98.8 us; the launch traced here: 98.4 us
  starting transfers between devices  31.6 us (32%)
  blocking collectives  25.1 us (25%)
  Pallas kernels  23 us (23%)
  waiting for transfers between devices  15.2 us (15%)
  local copies, waits for them, and re-layouts  2.75 us (3%)
    ppermute x17, starting transfers between devices, xor_permute(): lax.ppermute(array, axis, [(i, i ^ mask) for i in range(lax.axis_size(axi...  27.2 us
    all_to_all x1, blocking collectives, shards(): routed = lax.all_to_all(grads, ('dp', 'mp'), 0, 0, tiled=True)  25.1 us
    ppermute x17, waiting for transfers between devices, xor_permute(): lax.ppermute(array, axis, [(i, i ^ mask) for i in range(lax.axis_size(axi...  15.2 us
    pallas_call x1, Pallas kernels, shards(): call(middle, [sds((tok_dev, half), F32)] * 2 + [sds((tok_dev, (members -...  5.69 us
    pallas_call x1, Pallas kernels, shards(): call(early, [sds((tok_dev, half), F32)] * 2 + [turned], n_smem=1, n_in=3...  4.99 us
    all_to_all x1, starting transfers between devices, shards(): got = lax.all_to_all(sent, 'dp', 0, 0, tiled=True)  4.32 us
    unnamed x19, local copies, waits for them, and re-layouts  2.71 us
    pallas_call x1, Pallas kernels, shards(): pl.pallas_call(chunk_kernel, in_specs=[pl.BlockSpec(memory_space=pltpu.SM...  2.66 us
  transfers between devices with their start and end apart: 18, of which 6 were waited for; matrix products, arithmetic and copies ran while one was open for 2% of the time, Pallas kernels for 18%

profile of v6, /device:TPU:1, one launch (start us, length us, event | category | flops | bytes accessed | tf_op | source)
XLA Modules:
  0.0 98.4 jit_solution(3805115292787818064)
XLA Ops:
  0.7 2.7 %shard_map.82 = (bf16[1296,128]{1,0:T(8,128)(2,1)}, bf16[656,128]{1,0:T(8,128)(2,1)}, bf16[656,128]{1,0:T(8,128)(2,1)}) custom-call(s32[4]{0:T(128)} %pad_add_fusion.place_ref.refs_0_, s32[2]{0:T(128)} %slot_ref.5, bf16[1280,1024]{1,0:T(8,128)(2,1)} %refs_2_.1), custom_call_target="tpu_custom_call" | custom-call | tf_op jit(solution)/shard_map/pallas_call | solution.py:415
  3.4 2.8 %collective-permute-start.1 = (bf16[1296,128]{1,0:T(8,128)(2,1)}, bf16[1296,128]{1,0:T(8,128)(2,1)}, u32[]{:S(2)}, u32[]{:S(2)}) collective-permute-start(bf16[1296,128]{1,0:T(8,128)(2,1)} %get-tuple-element.57), channel_id=1, source_target_pairs={{0,1},{1,0},{2,3},{3,2},{4,5},{5,4},{6,7},{7,6},{8,9},{9,8},{10,11... | collective-permute-start | bytes 995336 | tf_op jit(solution)/shard_map/ppermute | solution.py:61
  6.2 2.3 %collective-permute-start.4 = (bf16[656,128]{1,0:T(8,128)(2,1)}, bf16[656,128]{1,0:T(8,128)(2,1)}, u32[]{:S(2)}, u32[]{:S(2)}) collective-permute-start(bf16[656,128]{1,0:T(8,128)(2,1)} %get-tuple-element.58), channel_id=1, source_target_pairs={{0,2},{1,3},{2,0},{3,1},{4,6},{5,7},{6,4},{7,5},{8,10},{9,11},{10,... | collective-permute-start | bytes 503816 | tf_op jit(solution)/shard_map/ppermute | solution.py:61
  8.5 2.0 %shard_map.83 = bf16[8,208,128]{2,1,0:T(8,128)(2,1)} custom-call(s32[8]{0:T(128)S(1)} %copy-done.7, s32[2]{0:T(128)S(1)} %copy-done.6, bf16[16,128]{1,0:T(8,128)(2,1)S(1)} %copy-done.5, bf16[128,6144]{1,0:T(8,128)(2,1)S(1)} %copy-done.2), custom_call_target="tpu_custom_call" | custom-call | flops 50331648 | bytes 3145728 | tf_op jit(solution)/shard_map/pallas_call | solution.py:447
  10.5 4.3 %all-to-all-start = ((bf16[8,208,128]{2,1,0:T(8,128)(2,1)}), bf16[8,208,128]{2,1,0:T(8,128)(2,1)S(1)}, u32[]{:S(2)}, u32[]{:S(2)}) async-start(bf16[8,208,128]{2,1,0:T(8,128)(2,1)} %shard_map.83), calls=%async_computation | async-start | bytes 851968 | tf_op jit(solution)/shard_map/all_to_all | solution.py:456
  14.8 3.4 %collective-permute-done.1.near_ref.refs_3_ = bf16[1296,128]{1,0:T(8,128)(2,1)} collective-permute-done((bf16[1296,128]{1,0:T(8,128)(2,1)}, bf16[1296,128]{1,0:T(8,128)(2,1)}, u32[]{:S(2)}, u32[]{:S(2)}) %collective-permute-start.1) | collective-permute-done | bytes 331808 | tf_op jit(solution)/shard_map/ppermute | solution.py:61
  18.2 1.2 %collective-permute-start.3 = (bf16[1296,128]{1,0:T(8,128)(2,1)}, bf16[1296,128]{1,0:T(8,128)(2,1)}, u32[]{:S(2)}, u32[]{:S(2)}) collective-permute-start(bf16[1296,128]{1,0:T(8,128)(2,1)} %collective-permute-done.1.near_ref.refs_3_), channel_id=1, source_target_pairs={{0,16},{4,20},{8,24},{12,28},{16,0},{20,4},{24,8},{28,12},{1,17},{... | collective-permute-start | bytes 995336 | tf_op jit(solution)/shard_map/ppermute | solution.py:61
  19.4 1.2 %collective-permute-start.2 = (bf16[1296,128]{1,0:T(8,128)(2,1)}, bf16[1296,128]{1,0:T(8,128)(2,1)}, u32[]{:S(2)}, u32[]{:S(2)}) collective-permute-start(bf16[1296,128]{1,0:T(8,128)(2,1)} %collective-permute-done.1.near_ref.refs_3_), channel_id=1, source_target_pairs={{0,8},{4,12},{8,0},{12,4},{16,24},{20,28},{24,16},{28,20},{1,9},{5... | collective-permute-start | bytes 995336 | tf_op jit(solution)/shard_map/ppermute | solution.py:61
  20.6 3.3 %collective-permute-start.5 = (bf16[656,128]{1,0:T(8,128)(2,1)}, bf16[656,128]{1,0:T(8,128)(2,1)S(1)}, u32[]{:S(2)}, u32[]{:S(2)}) collective-permute-start(bf16[656,128]{1,0:T(8,128)(2,1)} %get-tuple-element.59), channel_id=1, source_target_pairs={{0,3},{1,2},{2,1},{3,0},{4,7},{5,6},{6,5},{7,4},{8,11},{9,10},{10,... | collective-permute-start | bytes 503816 | tf_op jit(solution)/shard_map/ppermute | solution.py:61
  24.9 2.1 %collective-permute-done.5 = bf16[656,128]{1,0:T(8,128)(2,1)S(1)} collective-permute-done((bf16[656,128]{1,0:T(8,128)(2,1)}, bf16[656,128]{1,0:T(8,128)(2,1)S(1)}, u32[]{:S(2)}, u32[]{:S(2)}) %collective-permute-start.5) | collective-permute-done | bytes 167968 | tf_op jit(solution)/shard_map/ppermute | solution.py:61
  27.1 1.2 %shard_map.84 = (bf16[784,128]{1,0:T(8,128)(2,1)S(1)}, bf16[2096,128]{1,0:T(8,128)(2,1)S(1)}, bf16[784,128]{1,0:T(8,128)(2,1)S(1)}, bf16[784,128]{1,0:T(8,128)(2,1)S(1)}) custom-call(s32[2]{0:T(128)S(1)} %copy-done.6, bf16[1296,128]{1,0:T(8,128)(2,1)} %collective-permute-done.1.near_ref.refs_3_, ...), custom_call_target="tpu_custom_call" | custom-call | bytes 6291456 | tf_op jit(solution)/shard_map/pallas_call | solution.py:457
  30.3 1.9 %collective-permute-start.12 = (bf16[784,128]{1,0:T(8,128)(2,1)S(1)}, bf16[784,128]{1,0:T(8,128)(2,1)S(1)}, u32[]{:S(2)}, u32[]{:S(2)}) collective-permute-start(bf16[784,128]{1,0:T(8,128)(2,1)S(1)} %get-tuple-element.76), channel_id=1, source_target_pairs={{0,2},{1,3},{2,0},{3,1},{4,6},{5,7},{6,4},{7,5},{8,10},{9,11},{10,... | collective-permute-start | bytes 602120 | tf_op jit(solution)/shard_map/ppermute | solution.py:61
  32.3 1.1 %collective-permute-start.11 = (bf16[1312,128]{1,0:T(8,128)(2,1)S(1)}, bf16[1312,128]{1,0:T(8,128)(2,1)S(1)}, u32[]{:S(2)}, u32[]{:S(2)}) collective-permute-start(bf16[1312,128]{1,0:T(8,128)(2,1)S(1)} %constant_dynamic-update-slice_fusion.far_ref.refs_6_), channel_id=1, source_target_pairs={{0,16},{4,20},{8,24},{12,28},{16,0},{20,4},{24,8},{28,12},{1,17},{... | collective-permute-start | bytes 1007624 | tf_op jit(solution)/shard_map/ppermute | solution.py:61
  34.2 1.7 %copy-done.1 = bf16[1280,1024]{1,0:T(8,128)(2,1)S(1)} copy-done((bf16[1280,1024]{1,0:T(8,128)(2,1)S(1)}, bf16[1280,1024]{1,0:T(8,128)(2,1)}, u32[]{:S(2)}) %copy-start.1) | copy-done | bytes 2621464
  36.0 5.0 %shard_map.85 = (f32[256,512]{1,0:T(8,128)S(1)}, f32[256,512]{1,0:T(8,128)S(1)}, bf16[1280,1024]{1,0:T(8,128)(2,1)S(1)}) custom-call(s32[4]{0:T(128)S(1)} %copy-done.4, bf16[256,5120]{1,0:T(8,128)(2,1)S(1)} %copy-done, bf16[256,5120]{1,0:T(8,128)(2,1)} %collective-permute-done.refs_1_.refs_4_, bf16[1280,1024]{1,0:T(8,128)(2,1)S(1)} %copy-done.1, ...), custom_call_target="tpu_custom_call" | custom-call | tf_op jit(solution)/shard_map/pallas_call | solution.py:499
  41.0 4.1 %collective-permute-done.6.refs_15_ = bf16[2096,128]{1,0:T(8,128)(2,1)S(1)} collective-permute-done((bf16[2096,128]{1,0:T(8,128)(2,1)S(1)}, bf16[2096,128]{1,0:T(8,128)(2,1)S(1)}, u32[]{:S(2)}, u32[]{:S(2)}) %collective-permute-start.6) | collective-permute-done | bytes 536608 | tf_op jit(solution)/shard_map/ppermute | solution.py:61
  45.0 1.7 %collective-permute-start.9 = (bf16[1312,128]{1,0:T(8,128)(2,1)S(1)}, bf16[1312,128]{1,0:T(8,128)(2,1)S(1)}, u32[]{:S(2)}, u32[]{:S(2)}) collective-permute-start(bf16[1312,128]{1,0:T(8,128)(2,1)S(1)} %slice.4.refs_9_), channel_id=1, source_target_pairs={{0,16},{4,20},{8,24},{12,28},{16,0},{20,4},{24,8},{28,12},{1,17},{... | collective-permute-start | bytes 1007624 | tf_op jit(solution)/shard_map/ppermute | solution.py:61
  47.6 2.0 %collective-permute-start.13 = (bf16[784,128]{1,0:T(8,128)(2,1)S(1)}, bf16[784,128]{1,0:T(8,128)(2,1)S(1)}, u32[]{:S(2)}, u32[]{:S(2)}) collective-permute-start(bf16[784,128]{1,0:T(8,128)(2,1)S(1)} %get-tuple-element.77), channel_id=1, source_target_pairs={{0,3},{1,2},{2,1},{3,0},{4,7},{5,6},{6,5},{7,4},{8,11},{9,10},{10,... | collective-permute-start | bytes 602120 | tf_op jit(solution)/shard_map/ppermute | solution.py:61
  49.7 4.4 %collective-permute-done.13.refs_17_ = bf16[784,128]{1,0:T(8,128)(2,1)S(1)} collective-permute-done((bf16[784,128]{1,0:T(8,128)(2,1)S(1)}, bf16[784,128]{1,0:T(8,128)(2,1)S(1)}, u32[]{:S(2)}, u32[]{:S(2)}) %collective-permute-start.13) | collective-permute-done | bytes 200736 | tf_op jit(solution)/shard_map/ppermute | solution.py:61
  56.3 5.7 %shard_map.86 = (f32[256,512]{1,0:T(8,128)S(1)}, f32[256,512]{1,0:T(8,128)S(1)}, bf16[256,2560]{1,0:T(8,128)(2,1)S(1)}, bf16[256,128]{1,0:T(8,128)(2,1)S(1)}, bf...) custom-call(s32[4]{0:T(128)S(1)} %copy-done.4, s32[8]{0:T(128)S(1)} %copy-done.7, ...), custom_call_target="tpu_custom_call" | custom-call | tf_op jit(solution)/shard_map/pallas_call | solution.py:545
  63.1 4.2 %collective-permute-start.16 = (f32[256,512]{1,0:T(8,128)S(1)}, f32[256,512]{1,0:T(8,128)S(1)}, u32[]{:S(2)}, u32[]{:S(2)}) collective-permute-start(f32[256,512]{1,0:T(8,128)S(1)} %shard_map.88), channel_id=1, source_target_pairs={{0,4},{4,0},{8,12},{12,8},{16,20},{20,16},{24,28},{28,24},{1,5},{5... | collective-permute-start | bytes 1572872 | tf_op jit(solution)/shard_map/ppermute | solution.py:61
  68.9 2.3 %shard_map.89 = bf16[32,2,48,128]{3,2,1,0:T(8,128)(2,1)S(1)} custom-call(s32[4]{0:T(128)S(1)} %copy-done.4, s32[8]{0:T(128)S(1)} %copy-done.7, s32[2]{0:T(128)S(1)} %copy-done.6, s32[16]{0:T(128)S(1)} %copy-done.8, f32[256,512]{1,0:T(8,128)S(1)} %shard_map.87.mine_ref, f32[256,512]{1,0:T(8,128)S(1)} %collective-permute-done.16.theirs_ref, ...), custom_call_target="tpu_custom_call" | custom-call | flops 1342177280 | bytes 5242880 | tf_op jit(solution)/shard_map/pallas_call | solution.py:582
  71.2 25.1 %all_to_all.10.grads_ref = bf16[32,2,48,128]{3,2,1,0:T(8,128)(2,1)S(1)} all-to-all(bf16[32,2,48,128]{3,2,1,0:T(8,128)(2,1)S(1)} %shard_map.89), channel_id=1, replica_groups=mesh['dp'=8,'mp'=4] {'dp','mp'}, dimensions={0} | all-to-all | bytes 1572864 | tf_op jit(solution)/shard_map/all_to_all | solution.py:597
  96.3 2.0 %shard_map.90 = f32[128,6144]{1,0:T(8,128)} custom-call(bf16[128,64]{1,0:T(8,128)(2,1)S(1)} %get-tuple-element.90.codes_t_ref, bf16[32,2,48,128]{3,2,1,0:T(8,128)(2,1)S(1)} %all_to_all.10.grads_ref), custom_call_target="tpu_custom_call" | custom-call | tf_op jit(solution)/shard_map/pallas_call | solution.py:599
  (44 shorter events, 10.1 us)
Async XLA Ops:
  0.0 8.5 %copy-start.6 = (s32[2]{0:T(128)S(1)}, s32[2]{0:T(128)}, u32[]{:S(2)}) copy-start(s32[2]{0:T(128)} %slot_ref.5) | copy-start | bytes 28
  0.0 8.5 %copy-start.5 = (bf16[16,128]{1,0:T(8,128)(2,1)S(1)}, bf16[16,128]{1,0:T(8,128)(2,1)}, u32[]{:S(2)}) copy-start(bf16[16,128]{1,0:T(8,128)(2,1)} %refs_2_.2) | copy-start | bytes 12292
  0.0 8.5 %copy-start.7 = (s32[8]{0:T(128)S(1)}, s32[8]{0:T(128)}, u32[]{:S(2)}) copy-start(s32[8]{0:T(128)} %share_ref.3) | copy-start | bytes 100
  0.0 8.5 %collective-permute-start = (bf16[256,5120]{1,0:T(8,128)(2,1)}, bf16[256,5120]{1,0:T(8,128)(2,1)}, u32[]{:S(2)}, u32[]{:S(2)}) collective-permute-start(bf16[256,5120]{1,0:T(8,128)(2,1)} %refs_0_.3), channel_id=1, source_target_pairs={{0,4},{4,0},{8,12},{12,8},{16,20},{20,16},{24,28},{28,24},{1,5},{5... | collective-permute-start | bytes 7864328 | tf_op jit(solution)/shard_map/ppermute | solution.py:61
  0.1 8.4 %copy-start.2 = (bf16[128,6144]{1,0:T(8,128)(2,1)S(1)}, bf16[128,6144]{1,0:T(8,128)(2,1)}, u32[]{:S(2)}) copy-start(bf16[128,6144]{1,0:T(8,128)(2,1)} %weight_ref.3) | copy-start | bytes 4718596
  3.3 30.9 %copy-start = (bf16[256,5120]{1,0:T(8,128)(2,1)S(1)}, bf16[256,5120]{1,0:T(8,128)(2,1)}, u32[]{:S(2)}) copy-start(bf16[256,5120]{1,0:T(8,128)(2,1)} %refs_0_.3) | copy-start | bytes 7864324
  3.4 30.9 %copy-start.4 = (s32[4]{0:T(128)S(1)}, s32[4]{0:T(128)}, u32[]{:S(2)}) copy-start(s32[4]{0:T(128)} %pad_add_fusion.place_ref.refs_0_) | copy-start | bytes 52
  3.4 14.9 %collective-permute-start.1 = (bf16[1296,128]{1,0:T(8,128)(2,1)}, bf16[1296,128]{1,0:T(8,128)(2,1)}, u32[]{:S(2)}, u32[]{:S(2)}) collective-permute-start(bf16[1296,128]{1,0:T(8,128)(2,1)} %get-tuple-element.57), channel_id=1, source_target_pairs={{0,1},{1,0},{2,3},{3,2},{4,5},{5,4},{6,7},{7,6},{8,9},{9,8},{10,11... | collective-permute-start | bytes 995336 | tf_op jit(solution)/shard_map/ppermute | solution.py:61
  6.2 17.8 %collective-permute-start.4 = (bf16[656,128]{1,0:T(8,128)(2,1)}, bf16[656,128]{1,0:T(8,128)(2,1)}, u32[]{:S(2)}, u32[]{:S(2)}) collective-permute-start(bf16[656,128]{1,0:T(8,128)(2,1)} %get-tuple-element.58), channel_id=1, source_target_pairs={{0,2},{1,3},{2,0},{3,1},{4,6},{5,7},{6,4},{7,5},{8,10},{9,11},{10,... | collective-permute-start | bytes 503816 | tf_op jit(solution)/shard_map/ppermute | solution.py:61
  10.5 16.5 %all-to-all-start = ((bf16[8,208,128]{2,1,0:T(8,128)(2,1)}), bf16[8,208,128]{2,1,0:T(8,128)(2,1)S(1)}, u32[]{:S(2)}, u32[]{:S(2)}) async-start(bf16[8,208,128]{2,1,0:T(8,128)(2,1)} %shard_map.83), calls=%async_computation | async-start | bytes 851968 | tf_op jit(solution)/shard_map/all_to_all | solution.py:456
  18.2 10.7 %collective-permute-start.3 = (bf16[1296,128]{1,0:T(8,128)(2,1)}, bf16[1296,128]{1,0:T(8,128)(2,1)}, u32[]{:S(2)}, u32[]{:S(2)}) collective-permute-start(bf16[1296,128]{1,0:T(8,128)(2,1)} %collective-permute-done.1.near_ref.refs_3_), channel_id=1, source_target_pairs={{0,16},{4,20},{8,24},{12,28},{16,0},{20,4},{24,8},{28,12},{1,17},{... | collective-permute-start | bytes 995336 | tf_op jit(solution)/shard_map/ppermute | solution.py:61
  19.4 9.5 %collective-permute-start.2 = (bf16[1296,128]{1,0:T(8,128)(2,1)}, bf16[1296,128]{1,0:T(8,128)(2,1)}, u32[]{:S(2)}, u32[]{:S(2)}) collective-permute-start(bf16[1296,128]{1,0:T(8,128)(2,1)} %collective-permute-done.1.near_ref.refs_3_), channel_id=1, source_target_pairs={{0,8},{4,12},{8,0},{12,4},{16,24},{20,28},{24,16},{28,20},{1,9},{5... | collective-permute-start | bytes 995336 | tf_op jit(solution)/shard_map/ppermute | solution.py:61
  20.6 6.4 %collective-permute-start.5 = (bf16[656,128]{1,0:T(8,128)(2,1)}, bf16[656,128]{1,0:T(8,128)(2,1)S(1)}, u32[]{:S(2)}, u32[]{:S(2)}) collective-permute-start(bf16[656,128]{1,0:T(8,128)(2,1)} %get-tuple-element.59), channel_id=1, source_target_pairs={{0,3},{1,2},{2,1},{3,0},{4,7},{5,6},{6,5},{7,4},{8,11},{9,10},{10,... | collective-permute-start | bytes 503816 | tf_op jit(solution)/shard_map/ppermute | solution.py:61
  29.0 16.1 %collective-permute-start.6 = (bf16[2096,128]{1,0:T(8,128)(2,1)S(1)}, bf16[2096,128]{1,0:T(8,128)(2,1)S(1)}, u32[]{:S(2)}, u32[]{:S(2)}) collective-permute-start(bf16[2096,128]{1,0:T(8,128)(2,1)S(1)} %get-tuple-element.64), channel_id=1, source_target_pairs={{0,1},{1,0},{2,3},{3,2},{4,5},{5,4},{6,7},{7,6},{8,9},{9,8},{10,11... | collective-permute-start | bytes 1609736 | tf_op jit(solution)/shard_map/ppermute | solution.py:61
  29.4 15.6 %collective-permute-start.7 = (bf16[1296,128]{1,0:T(8,128)(2,1)}, bf16[1296,128]{1,0:T(8,128)(2,1)S(1)}, u32[]{:S(2)}, u32[]{:S(2)}) collective-permute-start(bf16[1296,128]{1,0:T(8,128)(2,1)} %collective-permute-done.2.refs_4_), channel_id=1, source_target_pairs={{0,16},{4,20},{8,24},{12,28},{16,0},{20,4},{24,8},{28,12},{1,17},{... | collective-permute-start | bytes 995336 | tf_op jit(solution)/shard_map/ppermute | solution.py:61
  30.3 17.3 %collective-permute-start.12 = (bf16[784,128]{1,0:T(8,128)(2,1)S(1)}, bf16[784,128]{1,0:T(8,128)(2,1)S(1)}, u32[]{:S(2)}, u32[]{:S(2)}) collective-permute-start(bf16[784,128]{1,0:T(8,128)(2,1)S(1)} %get-tuple-element.76), channel_id=1, source_target_pairs={{0,2},{1,3},{2,0},{3,1},{4,6},{5,7},{6,4},{7,5},{8,10},{9,11},{10,... | collective-permute-start | bytes 602120 | tf_op jit(solution)/shard_map/ppermute | solution.py:61
  32.3 21.8 %collective-permute-start.11 = (bf16[1312,128]{1,0:T(8,128)(2,1)S(1)}, bf16[1312,128]{1,0:T(8,128)(2,1)S(1)}, u32[]{:S(2)}, u32[]{:S(2)}) collective-permute-start(bf16[1312,128]{1,0:T(8,128)(2,1)S(1)} %constant_dynamic-update-slice_fusion.far_ref.refs_6_), channel_id=1, source_target_pairs={{0,16},{4,20},{8,24},{12,28},{16,0},{20,4},{24,8},{28,12},{1,17},{... | collective-permute-start | bytes 1007624 | tf_op jit(solution)/shard_map/ppermute | solution.py:61
  33.4 20.7 %collective-permute-start.10 = (bf16[1312,128]{1,0:T(8,128)(2,1)S(1)}, bf16[1312,128]{1,0:T(8,128)(2,1)S(1)}, u32[]{:S(2)}, u32[]{:S(2)}) collective-permute-start(bf16[1312,128]{1,0:T(8,128)(2,1)S(1)} %constant_dynamic-update-slice_fusion.far_ref.refs_6_), channel_id=1, source_target_pairs={{0,8},{4,12},{8,0},{12,4},{16,24},{20,28},{24,16},{28,20},{1,9},{5... | collective-permute-start | bytes 1007624 | tf_op jit(solution)/shard_map/ppermute | solution.py:61
  45.0 9.1 %collective-permute-start.9 = (bf16[1312,128]{1,0:T(8,128)(2,1)S(1)}, bf16[1312,128]{1,0:T(8,128)(2,1)S(1)}, u32[]{:S(2)}, u32[]{:S(2)}) collective-permute-start(bf16[1312,128]{1,0:T(8,128)(2,1)S(1)} %slice.4.refs_9_), channel_id=1, source_target_pairs={{0,16},{4,20},{8,24},{12,28},{16,0},{20,4},{24,8},{28,12},{1,17},{... | collective-permute-start | bytes 1007624 | tf_op jit(solution)/shard_map/ppermute | solution.py:61
  46.8 7.3 %collective-permute-start.8 = (bf16[1312,128]{1,0:T(8,128)(2,1)S(1)}, bf16[1312,128]{1,0:T(8,128)(2,1)S(1)}, u32[]{:S(2)}, u32[]{:S(2)}) collective-permute-start(bf16[1312,128]{1,0:T(8,128)(2,1)S(1)} %slice.4.refs_9_), channel_id=1, source_target_pairs={{0,8},{4,12},{8,0},{12,4},{16,24},{20,28},{24,16},{28,20},{1,9},{5... | collective-permute-start | bytes 1007624 | tf_op jit(solution)/shard_map/ppermute | solution.py:61
  47.6 6.5 %collective-permute-start.13 = (bf16[784,128]{1,0:T(8,128)(2,1)S(1)}, bf16[784,128]{1,0:T(8,128)(2,1)S(1)}, u32[]{:S(2)}, u32[]{:S(2)}) collective-permute-start(bf16[784,128]{1,0:T(8,128)(2,1)S(1)} %get-tuple-element.77), channel_id=1, source_target_pairs={{0,3},{1,2},{2,1},{3,0},{4,7},{5,6},{6,5},{7,4},{8,11},{9,10},{10,... | collective-permute-start | bytes 602120 | tf_op jit(solution)/shard_map/ppermute | solution.py:61
  54.1 7.9 %collective-permute-start.14 = (bf16[1312,128]{1,0:T(8,128)(2,1)S(1)}, bf16[1312,128]{1,0:T(8,128)(2,1)S(1)}, u32[]{:S(2)}, u32[]{:S(2)}) collective-permute-start(bf16[1312,128]{1,0:T(8,128)(2,1)S(1)} %collective-permute-done.11.refs_8_), channel_id=1, source_target_pairs={{0,8},{4,12},{8,0},{12,4},{16,24},{20,28},{24,16},{28,20},{1,9},{5... | collective-permute-start | bytes 1007624 | tf_op jit(solution)/shard_map/ppermute | solution.py:61
  55.2 6.8 %collective-permute-start.15 = (bf16[1312,128]{1,0:T(8,128)(2,1)S(1)}, bf16[1312,128]{1,0:T(8,128)(2,1)S(1)}, u32[]{:S(2)}, u32[]{:S(2)}) collective-permute-start(bf16[1312,128]{1,0:T(8,128)(2,1)S(1)} %collective-permute-done.8.refs_10_), channel_id=1, source_target_pairs={{0,16},{4,20},{8,24},{12,28},{16,0},{20,4},{24,8},{28,12},{1,17},{... | collective-permute-start | bytes 1007624 | tf_op jit(solution)/shard_map/ppermute | solution.py:61
  63.1 5.8 %collective-permute-start.16 = (f32[256,512]{1,0:T(8,128)S(1)}, f32[256,512]{1,0:T(8,128)S(1)}, u32[]{:S(2)}, u32[]{:S(2)}) collective-permute-start(f32[256,512]{1,0:T(8,128)S(1)} %shard_map.88), channel_id=1, source_target_pairs={{0,4},{4,0},{8,12},{12,8},{16,20},{20,16},{24,28},{28,24},{1,5},{5... | collective-permute-start | bytes 1572872 | tf_op jit(solution)/shard_map/ppermute | solution.py:61
  (3 other events, 13.3 us)

commit v7 on v6

--- a/solution.py
+++ b/solution.py
@@ -595,7 +595,7 @@
     if not whole_tiles:
         grads = grads.reshape(seqs, devices, tiles, LANES).transpose(1, 0, 2, 3)
     routed = lax.all_to_all(grads, ("dp", "mp"), 0, 0, tiled=True)
-    step = 8 if whole_tiles else tiles
+    step = 4 if whole_tiles else tiles
     return pl.pallas_call(
         functools.partial(hyper_kernel, step),
         out_shape=sds((width_h, tiles * LANES), F32),

time: 98.8 us -> 98.8 us (level)
  no operation moved by 1% of the time
where the time goes in v7:
time: 98.8 us; the launch traced here: 98.4 us
  starting transfers between devices  31.6 us (32%)
  blocking collectives  25.1 us (25%)
  Pallas kernels  23 us (23%)
  waiting for transfers between devices  15.2 us (15%)
  local copies, waits for them, and re-layouts  2.75 us (3%)
    ppermute x17, starting transfers between devices, xor_permute(): lax.ppermute(array, axis, [(i, i ^ mask) for i in range(lax.axis_size(axi...  27.2 us
    all_to_all x1, blocking collectives, shards(): routed = lax.all_to_all(grads, ('dp', 'mp'), 0, 0, tiled=True)  25.1 us
    ppermute x17, waiting for transfers between devices, xor_permute(): lax.ppermute(array, axis, [(i, i ^ mask) for i in range(lax.axis_size(axi...  15.2 us
    pallas_call x1, Pallas kernels, shards(): call(middle, [sds((tok_dev, half), F32)] * 2 + [sds((tok_dev, (members -...  5.69 us
    pallas_call x1, Pallas kernels, shards(): call(early, [sds((tok_dev, half), F32)] * 2 + [turned], n_smem=1, n_in=3...  4.99 us
    all_to_all x1, starting transfers between devices, shards(): got = lax.all_to_all(sent, 'dp', 0, 0, tiled=True)  4.32 us
    unnamed x19, local copies, waits for them, and re-layouts  2.71 us
    pallas_call x1, Pallas kernels, shards(): pl.pallas_call(chunk_kernel, in_specs=[pl.BlockSpec(memory_space=pltpu.SM...  2.66 us
  transfers between devices with their start and end apart: 18, of which 6 were waited for; matrix products, arithmetic and copies ran while one was open for 2% of the time, Pallas kernels for 18%

profile of v7, /device:TPU:1, one launch (start us, length us, event | category | flops | bytes accessed | tf_op | source)
XLA Modules:
  0.0 98.4 jit_solution(2928094165808754742)
XLA Ops:
  0.7 2.7 %shard_map.82 = (bf16[1296,128]{1,0:T(8,128)(2,1)}, bf16[656,128]{1,0:T(8,128)(2,1)}, bf16[656,128]{1,0:T(8,128)(2,1)}) custom-call(s32[4]{0:T(128)} %pad_add_fusion.place_ref.refs_0_, s32[2]{0:T(128)} %slot_ref.5, bf16[1280,1024]{1,0:T(8,128)(2,1)} %refs_2_.1), custom_call_target="tpu_custom_call" | custom-call | tf_op jit(solution)/shard_map/pallas_call | solution.py:415
  3.4 2.8 %collective-permute-start.1 = (bf16[1296,128]{1,0:T(8,128)(2,1)}, bf16[1296,128]{1,0:T(8,128)(2,1)}, u32[]{:S(2)}, u32[]{:S(2)}) collective-permute-start(bf16[1296,128]{1,0:T(8,128)(2,1)} %get-tuple-element.57), channel_id=1, source_target_pairs={{0,1},{1,0},{2,3},{3,2},{4,5},{5,4},{6,7},{7,6},{8,9},{9,8},{10,11... | collective-permute-start | bytes 995336 | tf_op jit(solution)/shard_map/ppermute | solution.py:61
  6.2 2.3 %collective-permute-start.4 = (bf16[656,128]{1,0:T(8,128)(2,1)}, bf16[656,128]{1,0:T(8,128)(2,1)}, u32[]{:S(2)}, u32[]{:S(2)}) collective-permute-start(bf16[656,128]{1,0:T(8,128)(2,1)} %get-tuple-element.58), channel_id=1, source_target_pairs={{0,2},{1,3},{2,0},{3,1},{4,6},{5,7},{6,4},{7,5},{8,10},{9,11},{10,... | collective-permute-start | bytes 503816 | tf_op jit(solution)/shard_map/ppermute | solution.py:61
  8.5 2.0 %shard_map.83 = bf16[8,208,128]{2,1,0:T(8,128)(2,1)} custom-call(s32[8]{0:T(128)S(1)} %copy-done.7, s32[2]{0:T(128)S(1)} %copy-done.6, bf16[16,128]{1,0:T(8,128)(2,1)S(1)} %copy-done.5, bf16[128,6144]{1,0:T(8,128)(2,1)S(1)} %copy-done.2), custom_call_target="tpu_custom_call" | custom-call | flops 50331648 | bytes 3145728 | tf_op jit(solution)/shard_map/pallas_call | solution.py:447
  10.5 4.3 %all-to-all-start = ((bf16[8,208,128]{2,1,0:T(8,128)(2,1)}), bf16[8,208,128]{2,1,0:T(8,128)(2,1)S(1)}, u32[]{:S(2)}, u32[]{:S(2)}) async-start(bf16[8,208,128]{2,1,0:T(8,128)(2,1)} %shard_map.83), calls=%async_computation | async-start | bytes 851968 | tf_op jit(solution)/shard_map/all_to_all | solution.py:456
  14.8 3.4 %collective-permute-done.1.near_ref.refs_3_ = bf16[1296,128]{1,0:T(8,128)(2,1)} collective-permute-done((bf16[1296,128]{1,0:T(8,128)(2,1)}, bf16[1296,128]{1,0:T(8,128)(2,1)}, u32[]{:S(2)}, u32[]{:S(2)}) %collective-permute-start.1) | collective-permute-done | bytes 331808 | tf_op jit(solution)/shard_map/ppermute | solution.py:61
  18.2 1.2 %collective-permute-start.3 = (bf16[1296,128]{1,0:T(8,128)(2,1)}, bf16[1296,128]{1,0:T(8,128)(2,1)}, u32[]{:S(2)}, u32[]{:S(2)}) collective-permute-start(bf16[1296,128]{1,0:T(8,128)(2,1)} %collective-permute-done.1.near_ref.refs_3_), channel_id=1, source_target_pairs={{0,16},{4,20},{8,24},{12,28},{16,0},{20,4},{24,8},{28,12},{1,17},{... | collective-permute-start | bytes 995336 | tf_op jit(solution)/shard_map/ppermute | solution.py:61
  19.4 1.2 %collective-permute-start.2 = (bf16[1296,128]{1,0:T(8,128)(2,1)}, bf16[1296,128]{1,0:T(8,128)(2,1)}, u32[]{:S(2)}, u32[]{:S(2)}) collective-permute-start(bf16[1296,128]{1,0:T(8,128)(2,1)} %collective-permute-done.1.near_ref.refs_3_), channel_id=1, source_target_pairs={{0,8},{4,12},{8,0},{12,4},{16,24},{20,28},{24,16},{28,20},{1,9},{5... | collective-permute-start | bytes 995336 | tf_op jit(solution)/shard_map/ppermute | solution.py:61
  20.6 3.3 %collective-permute-start.5 = (bf16[656,128]{1,0:T(8,128)(2,1)}, bf16[656,128]{1,0:T(8,128)(2,1)S(1)}, u32[]{:S(2)}, u32[]{:S(2)}) collective-permute-start(bf16[656,128]{1,0:T(8,128)(2,1)} %get-tuple-element.59), channel_id=1, source_target_pairs={{0,3},{1,2},{2,1},{3,0},{4,7},{5,6},{6,5},{7,4},{8,11},{9,10},{10,... | collective-permute-start | bytes 503816 | tf_op jit(solution)/shard_map/ppermute | solution.py:61
  24.9 2.1 %collective-permute-done.5 = bf16[656,128]{1,0:T(8,128)(2,1)S(1)} collective-permute-done((bf16[656,128]{1,0:T(8,128)(2,1)}, bf16[656,128]{1,0:T(8,128)(2,1)S(1)}, u32[]{:S(2)}, u32[]{:S(2)}) %collective-permute-start.5) | collective-permute-done | bytes 167968 | tf_op jit(solution)/shard_map/ppermute | solution.py:61
  27.1 1.2 %shard_map.84 = (bf16[784,128]{1,0:T(8,128)(2,1)S(1)}, bf16[2096,128]{1,0:T(8,128)(2,1)S(1)}, bf16[784,128]{1,0:T(8,128)(2,1)S(1)}, bf16[784,128]{1,0:T(8,128)(2,1)S(1)}) custom-call(s32[2]{0:T(128)S(1)} %copy-done.6, bf16[1296,128]{1,0:T(8,128)(2,1)} %collective-permute-done.1.near_ref.refs_3_, ...), custom_call_target="tpu_custom_call" | custom-call | bytes 6291456 | tf_op jit(solution)/shard_map/pallas_call | solution.py:457
  30.3 1.9 %collective-permute-start.12 = (bf16[784,128]{1,0:T(8,128)(2,1)S(1)}, bf16[784,128]{1,0:T(8,128)(2,1)S(1)}, u32[]{:S(2)}, u32[]{:S(2)}) collective-permute-start(bf16[784,128]{1,0:T(8,128)(2,1)S(1)} %get-tuple-element.76), channel_id=1, source_target_pairs={{0,2},{1,3},{2,0},{3,1},{4,6},{5,7},{6,4},{7,5},{8,10},{9,11},{10,... | collective-permute-start | bytes 602120 | tf_op jit(solution)/shard_map/ppermute | solution.py:61
  32.3 1.1 %collective-permute-start.11 = (bf16[1312,128]{1,0:T(8,128)(2,1)S(1)}, bf16[1312,128]{1,0:T(8,128)(2,1)S(1)}, u32[]{:S(2)}, u32[]{:S(2)}) collective-permute-start(bf16[1312,128]{1,0:T(8,128)(2,1)S(1)} %constant_dynamic-update-slice_fusion.far_ref.refs_6_), channel_id=1, source_target_pairs={{0,16},{4,20},{8,24},{12,28},{16,0},{20,4},{24,8},{28,12},{1,17},{... | collective-permute-start | bytes 1007624 | tf_op jit(solution)/shard_map/ppermute | solution.py:61
  34.2 1.7 %copy-done.1 = bf16[1280,1024]{1,0:T(8,128)(2,1)S(1)} copy-done((bf16[1280,1024]{1,0:T(8,128)(2,1)S(1)}, bf16[1280,1024]{1,0:T(8,128)(2,1)}, u32[]{:S(2)}) %copy-start.1) | copy-done | bytes 2621464
  36.0 5.0 %shard_map.85 = (f32[256,512]{1,0:T(8,128)S(1)}, f32[256,512]{1,0:T(8,128)S(1)}, bf16[1280,1024]{1,0:T(8,128)(2,1)S(1)}) custom-call(s32[4]{0:T(128)S(1)} %copy-done.4, bf16[256,5120]{1,0:T(8,128)(2,1)S(1)} %copy-done, bf16[256,5120]{1,0:T(8,128)(2,1)} %collective-permute-done.refs_1_.refs_4_, bf16[1280,1024]{1,0:T(8,128)(2,1)S(1)} %copy-done.1, ...), custom_call_target="tpu_custom_call" | custom-call | tf_op jit(solution)/shard_map/pallas_call | solution.py:499
  41.0 4.1 %collective-permute-done.6.refs_15_ = bf16[2096,128]{1,0:T(8,128)(2,1)S(1)} collective-permute-done((bf16[2096,128]{1,0:T(8,128)(2,1)S(1)}, bf16[2096,128]{1,0:T(8,128)(2,1)S(1)}, u32[]{:S(2)}, u32[]{:S(2)}) %collective-permute-start.6) | collective-permute-done | bytes 536608 | tf_op jit(solution)/shard_map/ppermute | solution.py:61
  45.0 1.7 %collective-permute-start.9 = (bf16[1312,128]{1,0:T(8,128)(2,1)S(1)}, bf16[1312,128]{1,0:T(8,128)(2,1)S(1)}, u32[]{:S(2)}, u32[]{:S(2)}) collective-permute-start(bf16[1312,128]{1,0:T(8,128)(2,1)S(1)} %slice.4.refs_9_), channel_id=1, source_target_pairs={{0,16},{4,20},{8,24},{12,28},{16,0},{20,4},{24,8},{28,12},{1,17},{... | collective-permute-start | bytes 1007624 | tf_op jit(solution)/shard_map/ppermute | solution.py:61
  47.6 2.0 %collective-permute-start.13 = (bf16[784,128]{1,0:T(8,128)(2,1)S(1)}, bf16[784,128]{1,0:T(8,128)(2,1)S(1)}, u32[]{:S(2)}, u32[]{:S(2)}) collective-permute-start(bf16[784,128]{1,0:T(8,128)(2,1)S(1)} %get-tuple-element.77), channel_id=1, source_target_pairs={{0,3},{1,2},{2,1},{3,0},{4,7},{5,6},{6,5},{7,4},{8,11},{9,10},{10,... | collective-permute-start | bytes 602120 | tf_op jit(solution)/shard_map/ppermute | solution.py:61
  49.7 4.4 %collective-permute-done.13.refs_17_ = bf16[784,128]{1,0:T(8,128)(2,1)S(1)} collective-permute-done((bf16[784,128]{1,0:T(8,128)(2,1)S(1)}, bf16[784,128]{1,0:T(8,128)(2,1)S(1)}, u32[]{:S(2)}, u32[]{:S(2)}) %collective-permute-start.13) | collective-permute-done | bytes 200736 | tf_op jit(solution)/shard_map/ppermute | solution.py:61
  56.3 5.7 %shard_map.86 = (f32[256,512]{1,0:T(8,128)S(1)}, f32[256,512]{1,0:T(8,128)S(1)}, bf16[256,2560]{1,0:T(8,128)(2,1)S(1)}, bf16[256,128]{1,0:T(8,128)(2,1)S(1)}, bf...) custom-call(s32[4]{0:T(128)S(1)} %copy-done.4, s32[8]{0:T(128)S(1)} %copy-done.7, ...), custom_call_target="tpu_custom_call" | custom-call | tf_op jit(solution)/shard_map/pallas_call | solution.py:545
  63.1 4.2 %collective-permute-start.16 = (f32[256,512]{1,0:T(8,128)S(1)}, f32[256,512]{1,0:T(8,128)S(1)}, u32[]{:S(2)}, u32[]{:S(2)}) collective-permute-start(f32[256,512]{1,0:T(8,128)S(1)} %shard_map.88), channel_id=1, source_target_pairs={{0,4},{4,0},{8,12},{12,8},{16,20},{20,16},{24,28},{28,24},{1,5},{5... | collective-permute-start | bytes 1572872 | tf_op jit(solution)/shard_map/ppermute | solution.py:61
  68.9 2.3 %shard_map.89 = bf16[32,2,48,128]{3,2,1,0:T(8,128)(2,1)S(1)} custom-call(s32[4]{0:T(128)S(1)} %copy-done.4, s32[8]{0:T(128)S(1)} %copy-done.7, s32[2]{0:T(128)S(1)} %copy-done.6, s32[16]{0:T(128)S(1)} %copy-done.8, f32[256,512]{1,0:T(8,128)S(1)} %shard_map.87.mine_ref, f32[256,512]{1,0:T(8,128)S(1)} %collective-permute-done.16.theirs_ref, ...), custom_call_target="tpu_custom_call" | custom-call | flops 1342177280 | bytes 5242880 | tf_op jit(solution)/shard_map/pallas_call | solution.py:582
  71.2 25.1 %all_to_all.10.grads_ref = bf16[32,2,48,128]{3,2,1,0:T(8,128)(2,1)S(1)} all-to-all(bf16[32,2,48,128]{3,2,1,0:T(8,128)(2,1)S(1)} %shard_map.89), channel_id=1, replica_groups=mesh['dp'=8,'mp'=4] {'dp','mp'}, dimensions={0} | all-to-all | bytes 1572864 | tf_op jit(solution)/shard_map/all_to_all | solution.py:597
  96.3 2.0 %shard_map.90 = f32[128,6144]{1,0:T(8,128)} custom-call(bf16[128,64]{1,0:T(8,128)(2,1)S(1)} %get-tuple-element.90.codes_t_ref, bf16[32,2,48,128]{3,2,1,0:T(8,128)(2,1)S(1)} %all_to_all.10.grads_ref), custom_call_target="tpu_custom_call" | custom-call | tf_op jit(solution)/shard_map/pallas_call | solution.py:599
  (44 shorter events, 10.1 us)
Async XLA Ops:
  0.0 8.5 %copy-start.6 = (s32[2]{0:T(128)S(1)}, s32[2]{0:T(128)}, u32[]{:S(2)}) copy-start(s32[2]{0:T(128)} %slot_ref.5) | copy-start | bytes 28
  0.0 8.5 %copy-start.5 = (bf16[16,128]{1,0:T(8,128)(2,1)S(1)}, bf16[16,128]{1,0:T(8,128)(2,1)}, u32[]{:S(2)}) copy-start(bf16[16,128]{1,0:T(8,128)(2,1)} %refs_2_.2) | copy-start | bytes 12292
  0.0 8.5 %copy-start.7 = (s32[8]{0:T(128)S(1)}, s32[8]{0:T(128)}, u32[]{:S(2)}) copy-start(s32[8]{0:T(128)} %share_ref.3) | copy-start | bytes 100
  0.0 8.5 %collective-permute-start = (bf16[256,5120]{1,0:T(8,128)(2,1)}, bf16[256,5120]{1,0:T(8,128)(2,1)}, u32[]{:S(2)}, u32[]{:S(2)}) collective-permute-start(bf16[256,5120]{1,0:T(8,128)(2,1)} %refs_0_.3), channel_id=1, source_target_pairs={{0,4},{4,0},{8,12},{12,8},{16,20},{20,16},{24,28},{28,24},{1,5},{5... | collective-permute-start | bytes 7864328 | tf_op jit(solution)/shard_map/ppermute | solution.py:61
  0.1 8.4 %copy-start.2 = (bf16[128,6144]{1,0:T(8,128)(2,1)S(1)}, bf16[128,6144]{1,0:T(8,128)(2,1)}, u32[]{:S(2)}) copy-start(bf16[128,6144]{1,0:T(8,128)(2,1)} %weight_ref.3) | copy-start | bytes 4718596
  3.3 30.9 %copy-start = (bf16[256,5120]{1,0:T(8,128)(2,1)S(1)}, bf16[256,5120]{1,0:T(8,128)(2,1)}, u32[]{:S(2)}) copy-start(bf16[256,5120]{1,0:T(8,128)(2,1)} %refs_0_.3) | copy-start | bytes 7864324
  3.4 30.9 %copy-start.4 = (s32[4]{0:T(128)S(1)}, s32[4]{0:T(128)}, u32[]{:S(2)}) copy-start(s32[4]{0:T(128)} %pad_add_fusion.place_ref.refs_0_) | copy-start | bytes 52
  3.4 14.9 %collective-permute-start.1 = (bf16[1296,128]{1,0:T(8,128)(2,1)}, bf16[1296,128]{1,0:T(8,128)(2,1)}, u32[]{:S(2)}, u32[]{:S(2)}) collective-permute-start(bf16[1296,128]{1,0:T(8,128)(2,1)} %get-tuple-element.57), channel_id=1, source_target_pairs={{0,1},{1,0},{2,3},{3,2},{4,5},{5,4},{6,7},{7,6},{8,9},{9,8},{10,11... | collective-permute-start | bytes 995336 | tf_op jit(solution)/shard_map/ppermute | solution.py:61
  6.2 17.8 %collective-permute-start.4 = (bf16[656,128]{1,0:T(8,128)(2,1)}, bf16[656,128]{1,0:T(8,128)(2,1)}, u32[]{:S(2)}, u32[]{:S(2)}) collective-permute-start(bf16[656,128]{1,0:T(8,128)(2,1)} %get-tuple-element.58), channel_id=1, source_target_pairs={{0,2},{1,3},{2,0},{3,1},{4,6},{5,7},{6,4},{7,5},{8,10},{9,11},{10,... | collective-permute-start | bytes 503816 | tf_op jit(solution)/shard_map/ppermute | solution.py:61
  10.5 16.5 %all-to-all-start = ((bf16[8,208,128]{2,1,0:T(8,128)(2,1)}), bf16[8,208,128]{2,1,0:T(8,128)(2,1)S(1)}, u32[]{:S(2)}, u32[]{:S(2)}) async-start(bf16[8,208,128]{2,1,0:T(8,128)(2,1)} %shard_map.83), calls=%async_computation | async-start | bytes 851968 | tf_op jit(solution)/shard_map/all_to_all | solution.py:456
  18.2 10.7 %collective-permute-start.3 = (bf16[1296,128]{1,0:T(8,128)(2,1)}, bf16[1296,128]{1,0:T(8,128)(2,1)}, u32[]{:S(2)}, u32[]{:S(2)}) collective-permute-start(bf16[1296,128]{1,0:T(8,128)(2,1)} %collective-permute-done.1.near_ref.refs_3_), channel_id=1, source_target_pairs={{0,16},{4,20},{8,24},{12,28},{16,0},{20,4},{24,8},{28,12},{1,17},{... | collective-permute-start | bytes 995336 | tf_op jit(solution)/shard_map/ppermute | solution.py:61
  19.4 9.5 %collective-permute-start.2 = (bf16[1296,128]{1,0:T(8,128)(2,1)}, bf16[1296,128]{1,0:T(8,128)(2,1)}, u32[]{:S(2)}, u32[]{:S(2)}) collective-permute-start(bf16[1296,128]{1,0:T(8,128)(2,1)} %collective-permute-done.1.near_ref.refs_3_), channel_id=1, source_target_pairs={{0,8},{4,12},{8,0},{12,4},{16,24},{20,28},{24,16},{28,20},{1,9},{5... | collective-permute-start | bytes 995336 | tf_op jit(solution)/shard_map/ppermute | solution.py:61
  20.6 6.4 %collective-permute-start.5 = (bf16[656,128]{1,0:T(8,128)(2,1)}, bf16[656,128]{1,0:T(8,128)(2,1)S(1)}, u32[]{:S(2)}, u32[]{:S(2)}) collective-permute-start(bf16[656,128]{1,0:T(8,128)(2,1)} %get-tuple-element.59), channel_id=1, source_target_pairs={{0,3},{1,2},{2,1},{3,0},{4,7},{5,6},{6,5},{7,4},{8,11},{9,10},{10,... | collective-permute-start | bytes 503816 | tf_op jit(solution)/shard_map/ppermute | solution.py:61
  29.0 16.1 %collective-permute-start.6 = (bf16[2096,128]{1,0:T(8,128)(2,1)S(1)}, bf16[2096,128]{1,0:T(8,128)(2,1)S(1)}, u32[]{:S(2)}, u32[]{:S(2)}) collective-permute-start(bf16[2096,128]{1,0:T(8,128)(2,1)S(1)} %get-tuple-element.64), channel_id=1, source_target_pairs={{0,1},{1,0},{2,3},{3,2},{4,5},{5,4},{6,7},{7,6},{8,9},{9,8},{10,11... | collective-permute-start | bytes 1609736 | tf_op jit(solution)/shard_map/ppermute | solution.py:61
  29.4 15.6 %collective-permute-start.7 = (bf16[1296,128]{1,0:T(8,128)(2,1)}, bf16[1296,128]{1,0:T(8,128)(2,1)S(1)}, u32[]{:S(2)}, u32[]{:S(2)}) collective-permute-start(bf16[1296,128]{1,0:T(8,128)(2,1)} %collective-permute-done.2.refs_4_), channel_id=1, source_target_pairs={{0,16},{4,20},{8,24},{12,28},{16,0},{20,4},{24,8},{28,12},{1,17},{... | collective-permute-start | bytes 995336 | tf_op jit(solution)/shard_map/ppermute | solution.py:61
  30.3 17.3 %collective-permute-start.12 = (bf16[784,128]{1,0:T(8,128)(2,1)S(1)}, bf16[784,128]{1,0:T(8,128)(2,1)S(1)}, u32[]{:S(2)}, u32[]{:S(2)}) collective-permute-start(bf16[784,128]{1,0:T(8,128)(2,1)S(1)} %get-tuple-element.76), channel_id=1, source_target_pairs={{0,2},{1,3},{2,0},{3,1},{4,6},{5,7},{6,4},{7,5},{8,10},{9,11},{10,... | collective-permute-start | bytes 602120 | tf_op jit(solution)/shard_map/ppermute | solution.py:61
  32.3 21.8 %collective-permute-start.11 = (bf16[1312,128]{1,0:T(8,128)(2,1)S(1)}, bf16[1312,128]{1,0:T(8,128)(2,1)S(1)}, u32[]{:S(2)}, u32[]{:S(2)}) collective-permute-start(bf16[1312,128]{1,0:T(8,128)(2,1)S(1)} %constant_dynamic-update-slice_fusion.far_ref.refs_6_), channel_id=1, source_target_pairs={{0,16},{4,20},{8,24},{12,28},{16,0},{20,4},{24,8},{28,12},{1,17},{... | collective-permute-start | bytes 1007624 | tf_op jit(solution)/shard_map/ppermute | solution.py:61
  33.4 20.7 %collective-permute-start.10 = (bf16[1312,128]{1,0:T(8,128)(2,1)S(1)}, bf16[1312,128]{1,0:T(8,128)(2,1)S(1)}, u32[]{:S(2)}, u32[]{:S(2)}) collective-permute-start(bf16[1312,128]{1,0:T(8,128)(2,1)S(1)} %constant_dynamic-update-slice_fusion.far_ref.refs_6_), channel_id=1, source_target_pairs={{0,8},{4,12},{8,0},{12,4},{16,24},{20,28},{24,16},{28,20},{1,9},{5... | collective-permute-start | bytes 1007624 | tf_op jit(solution)/shard_map/ppermute | solution.py:61
  45.0 9.1 %collective-permute-start.9 = (bf16[1312,128]{1,0:T(8,128)(2,1)S(1)}, bf16[1312,128]{1,0:T(8,128)(2,1)S(1)}, u32[]{:S(2)}, u32[]{:S(2)}) collective-permute-start(bf16[1312,128]{1,0:T(8,128)(2,1)S(1)} %slice.4.refs_9_), channel_id=1, source_target_pairs={{0,16},{4,20},{8,24},{12,28},{16,0},{20,4},{24,8},{28,12},{1,17},{... | collective-permute-start | bytes 1007624 | tf_op jit(solution)/shard_map/ppermute | solution.py:61
  46.8 7.3 %collective-permute-start.8 = (bf16[1312,128]{1,0:T(8,128)(2,1)S(1)}, bf16[1312,128]{1,0:T(8,128)(2,1)S(1)}, u32[]{:S(2)}, u32[]{:S(2)}) collective-permute-start(bf16[1312,128]{1,0:T(8,128)(2,1)S(1)} %slice.4.refs_9_), channel_id=1, source_target_pairs={{0,8},{4,12},{8,0},{12,4},{16,24},{20,28},{24,16},{28,20},{1,9},{5... | collective-permute-start | bytes 1007624 | tf_op jit(solution)/shard_map/ppermute | solution.py:61
  47.6 6.5 %collective-permute-start.13 = (bf16[784,128]{1,0:T(8,128)(2,1)S(1)}, bf16[784,128]{1,0:T(8,128)(2,1)S(1)}, u32[]{:S(2)}, u32[]{:S(2)}) collective-permute-start(bf16[784,128]{1,0:T(8,128)(2,1)S(1)} %get-tuple-element.77), channel_id=1, source_target_pairs={{0,3},{1,2},{2,1},{3,0},{4,7},{5,6},{6,5},{7,4},{8,11},{9,10},{10,... | collective-permute-start | bytes 602120 | tf_op jit(solution)/shard_map/ppermute | solution.py:61
  54.1 7.9 %collective-permute-start.14 = (bf16[1312,128]{1,0:T(8,128)(2,1)S(1)}, bf16[1312,128]{1,0:T(8,128)(2,1)S(1)}, u32[]{:S(2)}, u32[]{:S(2)}) collective-permute-start(bf16[1312,128]{1,0:T(8,128)(2,1)S(1)} %collective-permute-done.11.refs_8_), channel_id=1, source_target_pairs={{0,8},{4,12},{8,0},{12,4},{16,24},{20,28},{24,16},{28,20},{1,9},{5... | collective-permute-start | bytes 1007624 | tf_op jit(solution)/shard_map/ppermute | solution.py:61
  55.2 6.8 %collective-permute-start.15 = (bf16[1312,128]{1,0:T(8,128)(2,1)S(1)}, bf16[1312,128]{1,0:T(8,128)(2,1)S(1)}, u32[]{:S(2)}, u32[]{:S(2)}) collective-permute-start(bf16[1312,128]{1,0:T(8,128)(2,1)S(1)} %collective-permute-done.8.refs_10_), channel_id=1, source_target_pairs={{0,16},{4,20},{8,24},{12,28},{16,0},{20,4},{24,8},{28,12},{1,17},{... | collective-permute-start | bytes 1007624 | tf_op jit(solution)/shard_map/ppermute | solution.py:61
  63.1 5.8 %collective-permute-start.16 = (f32[256,512]{1,0:T(8,128)S(1)}, f32[256,512]{1,0:T(8,128)S(1)}, u32[]{:S(2)}, u32[]{:S(2)}) collective-permute-start(f32[256,512]{1,0:T(8,128)S(1)} %shard_map.88), channel_id=1, source_target_pairs={{0,4},{4,0},{8,12},{12,8},{16,20},{20,16},{24,28},{28,24},{1,5},{5... | collective-permute-start | bytes 1572872 | tf_op jit(solution)/shard_map/ppermute | solution.py:61
  (3 other events, 13.3 us)
